TPU v7x, 32 devices: a whole 2x2x4 slice. The times are simulated.
32 devices in a mesh: dp: 8 (over z, x), tensor: 4 (over y, core).
Axes of the slice: x: 2, y: 2, z: 4, core: 2. Of those that a mesh axis runs over, the one named last changes fastest.
Arguments:
- tokens: bfloat16 [4096, 768], P(('dp', 'tensor')), may hold values from -6 to 6
- lengths: int32 [8, 3], P('dp'), may hold values from 1 to 480, 512 in all within a row
- routes: int32 [4096, 1], P('dp'), may hold values from 0 to 7; in each aligned block of 128 rows (0 to 127, 128 to 255, ...) at most 24 rows name the same one
- norm_attn: bfloat16 [768], P('dp'), may hold values from 0.099609375 to 1.8984375
- w_query: bfloat16 [768, 768], P('dp', 'tensor'), may hold values from -0.21875 to 0.21875
- w_key: bfloat16 [768, 768], P('dp', 'tensor'), may hold values from -0.21875 to 0.21875
- w_value: bfloat16 [768, 768], P('dp', 'tensor'), may hold values from -0.21875 to 0.21875
- w_attn_out: bfloat16 [768, 768], P('tensor', 'dp'), may hold values from -1.25 to 1.25
- norm_moe: bfloat16 [768], P('dp'), may hold values from 0.099609375 to 1.8984375
- w_router: bfloat16 [768, 8], P('dp'), may hold values from -0.15625 to 0.15625
- w_expert_in: bfloat16 [8, 768, 3072], P('dp', None, 'tensor'), may hold values from -0.21875 to 0.21875
- w_expert_out: bfloat16 [8, 3072, 768], P('dp', 'tensor'), may hold values from -0.875 to 0.875
- cotangent: bfloat16 [4096, 768], P(('dp', 'tensor')), may hold values from -6 to 6
Outputs:
- result: bfloat16 [4096, 768], P(('dp', 'tensor'))
- grad_tokens: float32 [4096, 768], P(('dp', 'tensor'))
- grad_norm_attn: float32 [768], P('dp')
- grad_query: float32 [768, 768], P('dp', 'tensor')
- grad_key: float32 [768, 768], P('dp', 'tensor')
- grad_value: float32 [768, 768], P('dp', 'tensor')
- grad_attn_out: float32 [768, 768], P('tensor', 'dp')
- grad_norm_moe: float32 [768], P('dp')
- grad_router: float32 [768, 8], P('dp')
- grad_expert_in: float32 [8, 768, 3072], P('dp', None, 'tensor')
- grad_expert_out: float32 [8, 3072, 768], P('dp', 'tensor')
Inputs may be any that keep to these rules, and one draw needn't show every extreme that they name: `routes`: in each aligned block of 128 tokens no expert is named by more than 24 tokens. `lengths`: each row sums to 512.
All inputs are finite; a program needn't handle non-finite values.
Results may differ from a plain program's by a relative error of at most 0.012.
The roundings to bfloat16 on the way count: a program that leaves them out, or rounds other values in their place, can miss the bound.
Values may be sent and summed in bfloat16 or wider, within the bound.
No kernel may reach another device: no remote copies, remote signals or barrier semaphores. Data moves between devices by JAX's collectives and lax.ppermute only.
A program may use at most 128 MiB of HBM per device.

v0:
```python
import math

import jax
import jax.numpy as jnp
from jax import lax
from jax.sharding import PartitionSpec as P

HEAD_DIM = 64


EPSILON = 1e-06
NEGATIVE = -1e30
BLOCK_ROWS = 512


def split_up(shard, dim, count):
    before, after = (shard.shape[:dim], shard.shape[dim + 1 :])
    return jnp.moveaxis(shard.reshape(*before, count, -1, *after), dim, 0)


def summed_on_arrival(shard, axis, dim):
    count = lax.axis_size(axis)
    blocks = lax.all_to_all(split_up(shard, dim, count), axis, 0, 0, tiled=True)
    return jnp.sum(blocks.astype(jnp.float32), axis=0)


def in_one_piece(arrays, axis, dim, along):
    ends, at = ([], 0)
    for a in arrays[:-1]:
        at += a.shape[along]
        ends.append(at)
    both = jnp.concatenate(arrays, axis=along)
    return tuple(jnp.split(summed_on_arrival(both, axis, dim), ends, axis=along))


def side_by_side(arrays, axis, dim, along):
    widths = [math.prod(a.shape[along:]) for a in arrays]
    both = jnp.concatenate(
        [a.reshape(*a.shape[:along], w) for a, w in zip(arrays, widths)], axis=along
    )
    whole = summed_on_arrival(both, axis, dim)
    blocks = jnp.split(whole, [sum(widths[:k]) for k in range(1, len(widths))], axis=along)
    return tuple(
        (b.reshape(*whole.shape[:along], *a.shape[along:]) for a, b in zip(arrays, blocks))
    )


def gather_rows(values):
    return lax.all_gather(values, "tensor", axis=0, tiled=True)


def scatter_rows(values):
    return lax.psum_scatter(values, "tensor", scatter_dimension=0, tiled=True)


def send_out(buffer):
    return lax.all_to_all(buffer, "dp", split_axis=0, concat_axis=0, tiled=True)


def send_back(buffer):
    return lax.all_to_all(buffer, "dp", split_axis=0, concat_axis=0, tiled=True)


def norm_forward(values, gain_vec):
    inv_root = lax.rsqrt(jnp.mean(values * values, axis=1, keepdims=True) + EPSILON)
    return (values * inv_root * gain_vec, inv_root)


def norm_backward(values, inv_root, gain_vec, upstream):
    normed = values * inv_root
    scaled = upstream * gain_vec
    grad_gain = jnp.sum(upstream * normed, axis=0)
    grad_values = inv_root * (scaled - normed * jnp.mean(scaled * normed, axis=1, keepdims=True))
    return (grad_values, grad_gain)


def segment_ids(lengths_row, row_count):
    seq_ends = jnp.cumsum(lengths_row)
    positions = jnp.arange(row_count, dtype=jnp.int32)
    return jnp.sum((positions[:, None] >= seq_ends[None, :]).astype(jnp.int32), axis=1)


def block_scores(queries, key_rows, segment, first_row, low_key, high_key):
    head_size = queries.shape[2]
    scaled = jnp.einsum(
        "qhd,khd->hqk", queries, key_rows, preferred_element_type=jnp.float32
    ) * head_size ** (-0.5)
    query_pos = jnp.arange(first_row, first_row + BLOCK_ROWS)
    key_pos = jnp.arange(low_key, high_key)
    same_seq = segment[:, None] == segment[None, :]
    allowed = same_seq & (key_pos[None, :] <= query_pos[:, None])
    return jnp.where(allowed[None], scaled, NEGATIVE)


def attention_forward(queries, key_rows, value_rows, segment):
    low_key = max(0, 0 - BLOCK_ROWS)
    high_key = BLOCK_ROWS
    scores = block_scores(queries, key_rows, segment, 0, low_key, high_key)
    largest = jnp.max(scores, axis=2, keepdims=True)
    shifted = jnp.exp(scores - largest)
    row_total = jnp.sum(shifted, axis=2, keepdims=True)
    weights = (shifted / row_total).astype(jnp.bfloat16)
    outputs = jnp.einsum("hqk,khd->qhd", weights, value_rows, preferred_element_type=jnp.float32)
    log_totals = (largest + jnp.log(row_total))[:, :, 0]
    return (outputs, log_totals)


def attention_backward(queries, key_rows, value_rows, segment, log_total, grad_attended):
    head_size = queries.shape[2]
    grad_query = jnp.zeros(queries.shape, jnp.float32)
    grad_key = jnp.zeros(queries.shape, jnp.float32)
    grad_value = jnp.zeros(queries.shape, jnp.float32)
    low_key = max(0, 0 - BLOCK_ROWS)
    high_key = BLOCK_ROWS
    scores = block_scores(queries, key_rows, segment, 0, low_key, high_key)
    probs_block = jnp.exp(scores - log_total[:, 0:BLOCK_ROWS, None])
    grad_probs = jnp.einsum(
        "qhd,khd->hqk", grad_attended, value_rows, preferred_element_type=jnp.float32
    )
    inner_sum = jnp.sum(probs_block * grad_probs, axis=2, keepdims=True)
    grad_scores = (probs_block * (grad_probs - inner_sum)).astype(jnp.bfloat16)
    grad_query = grad_query.at[0:BLOCK_ROWS].add(
        jnp.einsum("hqk,khd->qhd", grad_scores, key_rows, preferred_element_type=jnp.float32)
        * head_size ** (-0.5)
    )
    grad_key = grad_key.at[low_key:high_key].add(
        jnp.einsum("hqk,qhd->khd", grad_scores, queries, preferred_element_type=jnp.float32)
        * head_size ** (-0.5)
    )
    grad_value = grad_value.at[low_key:high_key].add(
        jnp.einsum(
            "hqk,qhd->khd",
            probs_block.astype(jnp.bfloat16),
            grad_attended,
            preferred_element_type=jnp.float32,
        )
    )
    return (grad_query, grad_key, grad_value)


def through_experts(piece_values, group_dest, expert_count, capacity, work):
    feature_count = piece_values.shape[1]
    pieces = lax.axis_size("tensor")
    group_rows = gather_rows(piece_values)
    buffer = (
        jnp.zeros((expert_count * pieces * capacity, feature_count), piece_values.dtype)
        .at[group_dest]
        .set(group_rows)
    )
    arrived = send_out(buffer.reshape(expert_count, pieces * capacity, feature_count))
    produced, extra_out = work(arrived.reshape(-1, feature_count))
    returned = send_back(produced.reshape(arrived.shape))
    return (scatter_rows(returned.reshape(-1, feature_count)[group_dest]), extra_out)


def on_device(
    tokens,
    lengths,
    routes,
    norm_attn,
    w_query,
    w_key,
    w_value,
    w_attn_out,
    norm_moe,
    w_router,
    w_expert_in,
    w_expert_out,
    cotangent,
):
    query_full, key_full, value_full, out_full, router_full, gain_attn, gain_moe = (
        lax.all_gather(w_query, "dp", axis=0, tiled=True),
        lax.all_gather(w_key, "dp", axis=0, tiled=True),
        lax.all_gather(w_value, "dp", axis=0, tiled=True),
        lax.all_gather(w_attn_out, "dp", axis=1, tiled=True),
        lax.all_gather(w_router, "dp", axis=0, tiled=True),
        lax.all_gather(norm_attn, "dp", axis=0, tiled=True),
        lax.all_gather(norm_moe, "dp", axis=0, tiled=True),
    )
    pieces = lax.axis_size("tensor")
    piece_index = lax.axis_index("tensor")
    gain_one = gain_attn.astype(jnp.float32)
    gain_two = gain_moe.astype(jnp.float32)
    inputs = tokens.astype(jnp.float32)
    piece_rows = inputs.shape[0]
    normed_one, root_one = norm_forward(inputs, gain_one)
    group_one = gather_rows(normed_one.astype(jnp.bfloat16))
    row_count = group_one.shape[0]
    local_width = query_full.shape[1]
    head_count = local_width // HEAD_DIM

    def project(weight):
        return (
            jnp.dot(group_one, weight, preferred_element_type=jnp.float32)
            .astype(jnp.bfloat16)
            .reshape(row_count, head_count, HEAD_DIM)
        )

    queries = project(query_full)
    key_rows = project(key_full)
    value_rows = project(value_full)
    segment = segment_ids(lengths[0], row_count)
    attended, log_total = attention_forward(queries, key_rows, value_rows, segment)
    attended_low = attended.reshape(row_count, local_width).astype(jnp.bfloat16)
    attn_sum = scatter_rows(jnp.dot(attended_low, out_full, preferred_element_type=jnp.float32))
    middle = inputs + attn_sum
    normed_two, root_two = norm_forward(middle, gain_two)
    moe_input = normed_two.astype(jnp.bfloat16)
    logits = jnp.dot(moe_input, router_full, preferred_element_type=jnp.float32)
    probabilities = jax.nn.softmax(logits, axis=1)
    expert_count = router_full.shape[1]
    capacity = 3 * piece_rows // (2 * expert_count)
    route_all = routes[:, 0]
    expert_ids = jnp.arange(expert_count, dtype=jnp.int32)
    chosen = (
        (route_all[:, None] == expert_ids[None, :])
        .astype(jnp.int32)
        .reshape(pieces, piece_rows, expert_count)
    )
    earlier = jnp.cumsum(chosen, axis=1) - chosen
    slot_all = jnp.sum(earlier * chosen, axis=2).reshape(row_count)
    group_dest = (
        route_all * (pieces * capacity)
        + jnp.arange(row_count, dtype=jnp.int32) // piece_rows * capacity
        + slot_all
    )
    route_piece = lax.dynamic_slice_in_dim(route_all, piece_index * piece_rows, piece_rows)
    picked = (route_piece[:, None] == expert_ids[None, :]).astype(jnp.float32)
    gate_value = jnp.sum(probabilities * picked, axis=1)
    weight_in = w_expert_in[0]
    weight_out = w_expert_out[0]

    def expert_forward(arrived):
        hidden = jnp.dot(arrived, weight_in, preferred_element_type=jnp.float32)
        active = jax.nn.gelu(hidden).astype(jnp.bfloat16)
        return (
            jnp.dot(active, weight_out, preferred_element_type=jnp.float32),
            (arrived, hidden, active),
        )

    expert_sum, kept_rows = through_experts(
        moe_input, group_dest, expert_count, capacity, expert_forward
    )
    result = (middle + gate_value[:, None] * expert_sum).astype(jnp.bfloat16)
    upstream = cotangent.astype(jnp.float32)
    grad_gate = jnp.sum(upstream * expert_sum, axis=1)
    grad_expert_rows = (gate_value[:, None] * upstream).astype(jnp.bfloat16)

    def expert_backward(arrived_grad):
        arrived, hidden, active = kept_rows
        grad_active = jnp.dot(arrived_grad, weight_out.T, preferred_element_type=jnp.float32)
        unused_value, gelu_pull = jax.vjp(jax.nn.gelu, hidden)
        grad_hidden = gelu_pull(grad_active)[0].astype(jnp.bfloat16)
        grad_w_out = jnp.dot(active.T, arrived_grad, preferred_element_type=jnp.float32)
        grad_w_in = jnp.dot(arrived.T, grad_hidden, preferred_element_type=jnp.float32)
        return (
            jnp.dot(grad_hidden, weight_in.T, preferred_element_type=jnp.float32),
            (grad_w_in, grad_w_out),
        )

    grad_from_experts, expert_grads = through_experts(
        grad_expert_rows, group_dest, expert_count, capacity, expert_backward
    )
    grad_logits = ((gate_value * grad_gate)[:, None] * (picked - probabilities)).astype(
        jnp.bfloat16
    )
    grad_router_part = jnp.dot(moe_input.T, grad_logits, preferred_element_type=jnp.float32)
    grad_two = grad_from_experts + jnp.dot(
        grad_logits, router_full.T, preferred_element_type=jnp.float32
    )
    grad_middle_norm, grad_gain_two = norm_backward(middle, root_two, gain_two, grad_two)
    grad_middle = upstream + grad_middle_norm
    grad_attn_rows = gather_rows(grad_middle.astype(jnp.bfloat16))
    grad_out_w = jnp.dot(attended_low.T, grad_attn_rows, preferred_element_type=jnp.float32)
    grad_attended = jnp.dot(grad_attn_rows, out_full.T, preferred_element_type=jnp.float32).astype(
        jnp.bfloat16
    )
    grad_attended = grad_attended.reshape(row_count, head_count, HEAD_DIM)
    grad_query, grad_key, grad_value = attention_backward(
        queries, key_rows, value_rows, segment, log_total, grad_attended
    )
    grad_query = grad_query.reshape(row_count, local_width).astype(jnp.bfloat16)
    grad_key = grad_key.reshape(row_count, local_width).astype(jnp.bfloat16)
    grad_value = grad_value.reshape(row_count, local_width).astype(jnp.bfloat16)
    grad_wq = jnp.dot(group_one.T, grad_query, preferred_element_type=jnp.float32)
    grad_wk = jnp.dot(group_one.T, grad_key, preferred_element_type=jnp.float32)
    grad_wv = jnp.dot(group_one.T, grad_value, preferred_element_type=jnp.float32)
    grad_group = jnp.dot(grad_query, query_full.T, preferred_element_type=jnp.float32)
    grad_group = grad_group + jnp.dot(grad_key, key_full.T, preferred_element_type=jnp.float32)
    grad_group = grad_group + jnp.dot(grad_value, value_full.T, preferred_element_type=jnp.float32)
    grad_normed_one = scatter_rows(grad_group)
    grad_in_norm, grad_gain_one = norm_backward(inputs, root_one, gain_one, grad_normed_one)
    grad_tokens = grad_middle + grad_in_norm
    shards = (
        *in_one_piece(
            (
                grad_wq.astype(jnp.bfloat16),
                grad_wk.astype(jnp.bfloat16),
                grad_wv.astype(jnp.bfloat16),
            ),
            "dp",
            0,
            1,
        ),
        summed_on_arrival(grad_out_w.astype(jnp.bfloat16), "dp", 1),
        *side_by_side(
            (
                grad_router_part.astype(jnp.bfloat16),
                grad_gain_one.astype(jnp.bfloat16),
                grad_gain_two.astype(jnp.bfloat16),
            ),
            "dp",
            0,
            1,
        ),
    )
    router_shard, gain_one_shard, gain_two_shard = lax.psum(
        (shards[4], shards[5], shards[6]), "tensor"
    )
    return (
        result,
        grad_tokens,
        gain_one_shard,
        shards[0],
        shards[1],
        shards[2],
        shards[3],
        gain_two_shard,
        router_shard,
        expert_grads[0][None],
        expert_grads[1][None],
    )


def solution(mesh):
    return jax.shard_map(
        on_device,
        mesh=mesh,
        in_specs=(
            P(("dp", "tensor"), None),
            P("dp", None),
            P("dp", None),
            P("dp"),
            P("dp", "tensor"),
            P("dp", "tensor"),
            P("dp", "tensor"),
            P("tensor", "dp"),
            P("dp"),
            P("dp", None),
            P("dp", None, "tensor"),
            P("dp", "tensor", None),
            P(("dp", "tensor"), None),
        ),
        out_specs=(
            P(("dp", "tensor"), None),
            P(("dp", "tensor"), None),
            P("dp"),
            P("dp", "tensor"),
            P("dp", "tensor"),
            P("dp", "tensor"),
            P("tensor", "dp"),
            P("dp"),
            P("dp", None),
            P("dp", None, "tensor"),
            P("dp", "tensor", None),
        ),
        check_vma=False,
    )
```

profile of v0, /device:TPU:0, one launch (start us, length us, event | category | flops | bytes accessed | tf_op | source)
XLA Modules:
  0.0 576.1 jit_solution(13836325086908859616)
XLA Ops:
  12.9 23.1 %all-reduce.3 = (bf16[768]{0:T(1024)(128)(2,1)S(1)}, bf16[768]{0:T(1024)(128)(2,1)S(1)}) all-reduce(bf16[768]{0:T(1024)(128)(2,1)S(1)} %dynamic-update-slice.6, bf16[768]{0:T(1024)(128)(2,1)S(1)} %dynamic-update-slice.7), channel_id=1, replica_groups=mesh['dp'=8,'tensor'=4] {'dp'}, use_global_device_ids=true, to_apply=%add | all-reduce | flops 1536 | bytes 6144
  37.1 31.0 %all_gather.38 = bf16[192,768]{0,1:T(8,128)(2,1)S(1)} all-gather(bf16[192,96]{0,1:T(8,128)(2,1)S(1)} %copy.55), channel_id=1, replica_groups=mesh['dp'=8,'tensor'=4] {'dp'}, dimensions={1}, use_global_device_ids=true | all-gather | bytes 331776 | tf_op jit(solution)/shard_map/all_gather | solution.py:175
  68.2 31.2 %all_gather.36 = bf16[768,192]{1,0:T(8,128)(2,1)S(1)} all-gather(bf16[96,192]{1,0:T(8,128)(2,1)} %param.29), channel_id=1, replica_groups=mesh['dp'=8,'tensor'=4] {'dp'}, dimensions={0}, use_global_device_ids=true | all-gather | bytes 331776 | tf_op jit(solution)/shard_map/all_gather | solution.py:172
  99.4 31.2 %all_gather.37 = bf16[768,192]{1,0:T(8,128)(2,1)S(1)} all-gather(bf16[96,192]{1,0:T(8,128)(2,1)} %param.30), channel_id=1, replica_groups=mesh['dp'=8,'tensor'=4] {'dp'}, dimensions={0}, use_global_device_ids=true | all-gather | bytes 331776 | tf_op jit(solution)/shard_map/all_gather | solution.py:173
  130.5 31.0 %all_gather.35 = bf16[768,192]{1,0:T(8,128)(2,1)S(1)} all-gather(bf16[96,192]{1,0:T(8,128)(2,1)S(1)} %copy-done.42), channel_id=1, replica_groups=mesh['dp'=8,'tensor'=4] {'dp'}, dimensions={0}, use_global_device_ids=true | all-gather | bytes 331776 | tf_op jit(solution)/shard_map/all_gather | solution.py:174
  161.6 8.6 %all_gather.34 = bf16[512,768]{1,0:T(8,128)(2,1)S(1)} all-gather(bf16[128,768]{1,0:T(8,128)(2,1)S(1)} %fusion.38), channel_id=1, replica_groups=mesh['dp'=8,'tensor'=4] {'tensor'}, dimensions={0}, use_global_device_ids=true | all-gather | bytes 983040 | tf_op jit(solution)/shard_map/all_gather | solution.py:49
  177.0 24.0 %reduce-scatter.5.cloned.1.call-done = f32[128,768]{1,0:T(8,128)} async-done(((f32[512,768]{1,0:T(8,128)}), f32[128,768]{1,0:T(8,128)}) %reduce-scatter.5.cloned.1.call-update) | async-done | bytes 393232 | tf_op jit(solution)/shard_map/reduce_scatter | solution.py:53
  203.0 8.2 %all_gather.41 = bf16[512,768]{1,0:T(8,128)(2,1)S(1)} all-gather(bf16[128,768]{1,0:T(8,128)(2,1)S(1)} %multiply_convert_fusion.2), channel_id=1, replica_groups=mesh['dp'=8,'tensor'=4] {'tensor'}, dimensions={0}, use_global_device_ids=true | all-gather | bytes 983040 | tf_op jit(solution)/shard_map/all_gather | solution.py:49
  214.0 34.7 %all_to_all.35 = bf16[8,96,768]{2,1,0:T(8,128)(2,1)S(1)} all-to-all(bf16[8,96,768]{2,1,0:T(8,128)(2,1)S(1)} %bitcast.120), channel_id=1, replica_groups=mesh['dp'=8,'tensor'=4] {'dp'}, dimensions={0} | all-to-all | bytes 2359296 | tf_op jit(solution)/shard_map/all_to_all | solution.py:57
  258.8 53.2 %all-to-all-done.1 = f32[8,96,768]{2,1,0:T(8,128)S(1)} async-done(((f32[8,96,768]{2,1,0:T(8,128)}), f32[8,96,768]{2,1,0:T(8,128)S(1)}, u32[]{:S(2)}, u32[]{:S(2)}) %all-to-all-start.1) | async-done | bytes 2359328 | tf_op jit(solution)/shard_map/all_to_all | solution.py:61
  314.7 26.2 %all-gather = bf16[8,96,8]{1,2,0:T(8,128)(2,1)S(1)} all-gather(bf16[1,96,8]{1,2,0:T(8,128)(2,1)S(1)} %bitcast.147), channel_id=1, replica_groups=mesh['dp'=8,'tensor'=4] {'dp'}, dimensions={0}, use_global_device_ids=true | all-gather | bytes 13824 | tf_op jit(solution)/shard_map/all_gather | solution.py:176
  345.0 8.0 %all_gather.42 = bf16[512,768]{1,0:T(8,128)(2,1)S(1)} all-gather(bf16[128,768]{1,0:T(8,128)(2,1)S(1)} %get-tuple-element.88), channel_id=1, replica_groups=mesh['dp'=8,'tensor'=4] {'tensor'}, dimensions={0}, use_global_device_ids=true | all-gather | bytes 983040 | tf_op jit(solution)/shard_map/all_gather | solution.py:49
  356.0 33.1 %all_to_all.36 = bf16[8,96,768]{2,1,0:T(8,128)(2,1)S(1)} all-to-all(bf16[8,96,768]{2,1,0:T(8,128)(2,1)S(1)} %bitcast.119), channel_id=1, replica_groups=mesh['dp'=8,'tensor'=4] {'dp'}, dimensions={0} | all-to-all | bytes 2359296 | tf_op jit(solution)/shard_map/all_to_all | solution.py:57
  389.1 4.3 fusion.8
  394.6 56.8 %all_to_all.37 = f32[8,96,768]{2,1,0:T(8,128)S(1)} all-to-all(f32[8,96,768]{2,1,0:T(8,128)S(1)} %fusion.13), channel_id=1, replica_groups=mesh['dp'=8,'tensor'=4] {'dp'}, dimensions={0} | all-to-all | bytes 4718592 | tf_op jit(solution)/shard_map/all_to_all | solution.py:61
  455.7 25.2 %reduce-scatter.9.cloned.1.call-done = f32[128,768]{1,0:T(8,128)} async-done(((f32[512,768]{1,0:T(8,128)}), f32[128,768]{1,0:T(8,128)}) %reduce-scatter.9.cloned.1.call-update) | async-done | bytes 393232 | tf_op jit(solution)/shard_map/reduce_scatter | solution.py:53
  483.9 8.6 %all_gather.43 = bf16[512,768]{1,0:T(8,128)(2,1)S(1)} all-gather(bf16[128,768]{1,0:T(8,128)(2,1)S(1)} %fusion.53), channel_id=1, replica_groups=mesh['dp'=8,'tensor'=4] {'tensor'}, dimensions={0}, use_global_device_ids=true | all-gather | bytes 983040 | tf_op jit(solution)/shard_map/all_gather | solution.py:49
  503.9 5.5 all-to-all-start.6
  511.9 9.8 %all-to-all-done.6 = bf16[8,192,96]{2,1,0:T(8,128)(2,1)} async-done(((bf16[8,192,96]{2,1,0:T(8,128)(2,1)}), bf16[8,192,96]{2,1,0:T(8,128)(2,1)}, u32[]{:S(2)}, u32[]{:S(2)}) %all-to-all-start.6) | async-done | bytes 294944 | tf_op jit(solution)/shard_map/all_to_all | solution.py:23
  525.7 4.3 convolution_bitcast_fusion
  534.5 15.4 %all-to-all-done.5 = bf16[8,96,576]{2,1,0:T(8,128)(2,1)S(1)} async-done(((bf16[8,96,576]{2,1,0:T(8,128)(2,1)}), bf16[8,96,576]{2,1,0:T(8,128)(2,1)S(1)}, u32[]{:S(2)}, u32[]{:S(2)}) %all-to-all-start.5) | async-done | bytes 884768 | tf_op jit(solution)/shard_map/all_to_all | solution.py:23
  552.9 3.6 all-to-all-start.4
  558.7 4.4 all-to-all-done.4
  563.2 6.3 %all-reduce.2 = (f32[96]{0:T(128)}, f32[96]{0:T(128)}, f32[96,8]{0,1:T(8,128)}) all-reduce(f32[96]{0:T(128)S(1)} %get-tuple-element.90, f32[96]{0:T(128)S(1)} %get-tuple-element.89, f32[96,8]{0,1:T(8,128)S(1)} %split.29), channel_id=1, replica_groups=mesh['dp'=8,'tensor'=4] {'tensor'}, use_global_device_ids=true, to_apply=%region_24.25 | all-reduce | flops 960 | bytes 7680 | tf_op jit(solution)/shard_map/psum | solution.py:317
  (233 shorter events, 73.0 us)
Async XLA Ops:
  7.2 241.6 %copy-start = (bf16[1,768,768]{2,1,0:T(8,128)(2,1)S(1)}, bf16[1,768,768]{2,1,0:T(8,128)(2,1)}, u32[]{:S(2)}) copy-start(bf16[1,768,768]{2,1,0:T(8,128)(2,1)} %param.35) | copy-start | bytes 3538948
  7.2 154.3 %copy-start.7 = (bf16[128,768]{1,0:T(8,128)(2,1)S(1)}, bf16[128,768]{1,0:T(8,128)(2,1)}, u32[]{:S(2)}) copy-start(bf16[128,768]{1,0:T(8,128)(2,1)} %param.25) | copy-start | bytes 589828
  7.2 123.3 %copy-start.42 = (bf16[96,192]{1,0:T(8,128)(2,1)S(1)}, bf16[96,192]{1,0:T(8,128)(2,1)}, u32[]{:S(2)}) copy-start(bf16[96,192]{1,0:T(8,128)(2,1)} %param.31) | copy-start | bytes 110596
  7.2 193.8 %reduce-scatter.5.cloned.1.call-start = ((), (), s32[]{:S(2)}) async-start(), calls=%async_computation.11 | async-start | bytes 1966080 | tf_op jit(solution)/shard_map/reduce_scatter | solution.py:53
  8.4 162.3 %copy-start.55 = (f32[128]{0:T(128)}, f32[128]{0:T(128)S(1)}, u32[]{:S(2)}) copy-start(f32[128]{0:T(128)S(1)} %add_rsqrt_fusion.1) | copy-start | bytes 1540
  36.0 134.7 %copy-start.40 = (f32[768]{0:T(1024)}, f32[768]{0:T(1024)S(1)}, u32[]{:S(2)}) copy-start(f32[768]{0:T(1024)S(1)} %convert_element_type.156) | copy-start | bytes 9220
  68.2 105.9 %copy-start.15 = (bf16[192,768]{0,1:T(8,128)(2,1)}, bf16[192,768]{0,1:T(8,128)(2,1)S(1)}, u32[]{:S(2)}) copy-start(bf16[192,768]{0,1:T(8,128)(2,1)S(1)} %all_gather.38) | copy-start | bytes 884740
  99.4 71.8 %copy-start.13 = (bf16[768,192]{1,0:T(8,128)(2,1)}, bf16[768,192]{1,0:T(8,128)(2,1)S(1)}, u32[]{:S(2)}) copy-start(bf16[768,192]{1,0:T(8,128)(2,1)S(1)} %all_gather.36) | copy-start | bytes 884740
  130.5 40.6 %copy-start.11 = (bf16[768,192]{1,0:T(8,128)(2,1)}, bf16[768,192]{1,0:T(8,128)(2,1)S(1)}, u32[]{:S(2)}) copy-start(bf16[768,192]{1,0:T(8,128)(2,1)S(1)} %all_gather.37) | copy-start | bytes 884740
  177.0 81.7 %copy-start.51 = (s32[512,1]{0,1:T(1,128)}, s32[512,1]{0,1:T(1,128)S(1)}, u32[]{:S(2)}) copy-start(s32[512,1]{0,1:T(1,128)S(1)} %compare_select_fusion) | copy-start | bytes 6148
  202.1 46.6 %copy-start.52 = (f32[128]{0:T(128)}, f32[128]{0:T(128)S(1)}, u32[]{:S(2)}) copy-start(f32[128]{0:T(128)S(1)} %add_rsqrt_fusion) | copy-start | bytes 1540
  255.1 57.0 %all-to-all-start.1 = ((f32[8,96,768]{2,1,0:T(8,128)}), f32[8,96,768]{2,1,0:T(8,128)S(1)}, u32[]{:S(2)}, u32[]{:S(2)}) async-start(f32[8,96,768]{2,1,0:T(8,128)} %fusion.15), calls=%async_computation.2 | async-start | bytes 4718592 | tf_op jit(solution)/shard_map/all_to_all | solution.py:61
  258.7 84.7 %reduce-scatter.7.cloned.1.call-start = ((), (), s32[]{:S(2)}) async-start(), calls=%async_computation.12 | async-start | bytes 1966080 | tf_op jit(solution)/shard_map/reduce_scatter | solution.py:53
  258.8 55.8 %copy-start.45 = (s32[1024]{0:T(1024)}, s32[1024]{0:T(1024)S(1)}, u32[]{:S(2)}) copy-start(s32[1024]{0:T(1024)S(1)} %pad_clamp_fusion) | copy-start | bytes 12292
  314.6 166.2 %reduce-scatter.9.cloned.1.call-start = ((), (), s32[]{:S(2)}) async-start(), calls=%async_computation.13 | async-start | bytes 1966080 | tf_op jit(solution)/shard_map/reduce_scatter | solution.py:53
  356.0 33.1 %copy-start.65 = (bf16[1,768,768]{2,1,0:T(8,128)(2,1)S(1)}, bf16[1,768,768]{2,1,0:T(8,128)(2,1)}, u32[]{:S(2)}) copy-start(bf16[1,768,768]{2,1,0:T(8,128)(2,1)} %param.36) | copy-start | bytes 3538948
  454.1 29.6 %copy-start.22 = (bf16[128,768]{1,0:T(8,128)(2,1)S(1)}, bf16[128,768]{1,0:T(8,128)(2,1)}, u32[]{:S(2)}) copy-start(bf16[128,768]{1,0:T(8,128)(2,1)} %param.37) | copy-start | bytes 589828
  454.1 29.6 %copy-start.53 = (f32[128]{0:T(128)S(1)}, f32[128]{0:T(128)}, u32[]{:S(2)}) copy-start(f32[128]{0:T(128)} %copy-done.52) | copy-start | bytes 1540
  454.1 38.3 %copy-start.16 = (bf16[192,768]{0,1:T(8,128)(2,1)S(1)}, bf16[192,768]{0,1:T(8,128)(2,1)}, u32[]{:S(2)}) copy-start(bf16[192,768]{0,1:T(8,128)(2,1)} %copy-done.15) | copy-start | bytes 884740
  454.1 96.6 %reduce-scatter.11.cloned.1.call-start = ((), (), s32[]{:S(2)}) async-start(), calls=%async_computation.14 | async-start | bytes 1966080 | tf_op jit(solution)/shard_map/reduce_scatter | solution.py:53
  455.7 37.2 %copy-start.61 = (f32[128]{0:T(128)}, f32[128]{0:T(128)S(1)}, u32[]{:S(2)}) copy-start(f32[128]{0:T(128)S(1)} %mul.261) | copy-start | bytes 1540
  503.9 17.8 %all-to-all-start.6 = ((bf16[8,192,96]{2,1,0:T(8,128)(2,1)}), bf16[8,192,96]{2,1,0:T(8,128)(2,1)}, u32[]{:S(2)}, u32[]{:S(2)}) async-start(bf16[8,192,96]{2,1,0:T(8,128)(2,1)} %bitcast.114), calls=%async_computation.10 | async-start | bytes 786432 | tf_op jit(solution)/shard_map/all_to_all | solution.py:23
  521.7 28.2 %all-to-all-start.5 = ((bf16[8,96,576]{2,1,0:T(8,128)(2,1)}), bf16[8,96,576]{2,1,0:T(8,128)(2,1)S(1)}, u32[]{:S(2)}, u32[]{:S(2)}) async-start(bf16[8,96,576]{2,1,0:T(8,128)(2,1)} %bitcast.36), calls=%async_computation.9 | async-start | bytes 1966080 | tf_op jit(solution)/shard_map/all_to_all | solution.py:23
  552.9 10.2 %all-to-all-start.4 = ((bf16[8,2,480]{2,1,0:T(2,128)(2,1)}), bf16[8,2,480]{2,1,0:T(2,128)(2,1)S(1)}, u32[]{:S(2)}, u32[]{:S(2)}) async-start(bf16[8,2,480]{2,1,0:T(2,128)(2,1)} %reshape.433), calls=%async_computation.8 | async-start | bytes 32768 | tf_op jit(solution)/shard_map/all_to_all | solution.py:23
  (53 other events, 381.5 us)
Sparse Core Ops, SparseCore 0:
  176.4 24.5 reduce-scatter.4
  314.8 26.6 reduce-scatter.6
  454.3 26.5 reduce-scatter.8
  499.7 28.5 reduce-scatter.10
where the time goes:
time: 577 us; the launch traced here: 576 us
  blocking collectives  338 us (59%)
  waiting for transfers between devices  132 us (23%)
  matrix products  33.2 us (6%)
  local copies, waits for them, and re-layouts  26.6 us (5%)
  starting transfers between devices  16.6 us (3%)
  between operations  15.3 us (3%)
  other arithmetic  14.4 us (2%)
    all_to_all x2, blocking collectives, send_out(): return lax.all_to_all(buffer, 'dp', split_axis=0, concat_axis=0, tiled=True)  67.8 us
    all_to_all x1, blocking collectives, send_back(): return lax.all_to_all(buffer, 'dp', split_axis=0, concat_axis=0, tiled=True)  56.8 us
    all_to_all x1, waiting for transfers between devices, send_back(): return lax.all_to_all(buffer, 'dp', split_axis=0, concat_axis=0, tiled=True)  53.2 us
    reduce_scatter x4, waiting for transfers between devices, scatter_rows(): return lax.psum_scatter(values, 'tensor', scatter_dimension=0, tiled=True)  49.1 us
    all_gather x4, blocking collectives, gather_rows(): return lax.all_gather(values, 'tensor', axis=0, tiled=True)  33.4 us
    all_gather x1, blocking collectives, on_device(): lax.all_gather(w_query, 'dp', axis=0, tiled=True)  31.2 us
    all_gather x1, blocking collectives, on_device(): lax.all_gather(w_key, 'dp', axis=0, tiled=True)  31.2 us
    all_gather x1, blocking collectives, on_device(): lax.all_gather(w_attn_out, 'dp', axis=1, tiled=True)  31 us
  transfers between devices with their start and end apart: 8, of which 6 were waited for; matrix products, arithmetic and copies ran while one was open for 4% of the time, Pallas kernels for 0%

commit v1 on v0

v1 whole, which is shorter than its diff:
```python
import jax
import jax.numpy as jnp
from jax import lax
from jax.sharding import PartitionSpec as P

HEAD_DIM = 64
EPSILON = 1e-06
NEGATIVE = -1e30
LOW = jnp.bfloat16
FULL = jnp.float32


def dot(a, b):
    return jnp.dot(a, b, preferred_element_type=FULL)


def dot_nt(a, b):
    return lax.dot_general(a, b, (((1,), (1,)), ((), ())), preferred_element_type=FULL)


def dot_tn(a, b):
    return lax.dot_general(a, b, (((0,), (0,)), ((), ())), preferred_element_type=FULL)


def after(value, *others):
    return lax.optimization_barrier((value, *others))[0]


def swap(values, axis, bit):
    count = lax.axis_size(axis)
    return lax.ppermute(values, axis, [(i, i ^ bit) for i in range(count)])


def tensor_bits():
    count = lax.axis_size("tensor")
    bits = []
    bit = count // 2
    while bit:
        bits.append(bit)
        bit //= 2
    return bits


def block_offsets():
    offsets = [0]
    for bit in tensor_bits():
        offsets = offsets + [o ^ bit for o in offsets]
    return offsets


def gather_rows(rows):
    for bit in tensor_bits():
        rows = jnp.concatenate([rows, swap(rows, "tensor", bit)], axis=0)
    return rows


def scatter_rows(partial):
    for bit in reversed(tensor_bits()):
        half = partial.shape[0] // 2
        came = swap(partial[half:].astype(LOW), "tensor", bit)
        partial = partial[:half].astype(FULL) + came.astype(FULL)
    return partial


def ring_order(count):
    return list(range(0, count, 2)) + list(range(1, count, 2))[::-1]


def ring_gather(block, split):
    count = lax.axis_size("dp")
    order = ring_order(count)
    place = [order.index(d) for d in range(count)]
    me = lax.axis_index("dp")
    my_place = jnp.array(place, jnp.int32)[me]
    order_of = jnp.array(order, jnp.int32)
    right = [(order[k], order[(k + 1) % count]) for k in range(count)]
    left = [(b, a) for a, b in right]
    first = jnp.zeros((count, split, block.shape[1]), block.dtype)
    second = jnp.zeros((count, block.shape[0] - split, block.shape[1]), block.dtype)

    def put(arrays, rows, source):
        one, two = arrays
        return (
            lax.dynamic_update_index_in_dim(one, rows[:split], source, 0),
            lax.dynamic_update_index_in_dim(two, rows[split:], source, 0),
        )

    arrays = put((first, second), block, me)
    ahead, behind = block, block
    middle = split // 32 * 16
    for step in range(1, count // 2 + 1):
        source_right = order_of[(my_place - step) % count]
        source_left = order_of[(my_place + step) % count]
        if step < count // 2:
            ahead = lax.ppermute(ahead, "dp", right)
            behind = lax.ppermute(behind, "dp", left)
            arrays = put(arrays, ahead, source_right)
            arrays = put(arrays, behind, source_left)
        else:
            top = lax.ppermute(ahead[:middle], "dp", right)
            bottom = lax.ppermute(behind[middle:], "dp", left)
            arrays = put(arrays, jnp.concatenate([top, bottom], axis=0), source_right)
    return arrays


def exchange(buffer):
    return lax.all_to_all(buffer, "dp", split_axis=0, concat_axis=0, tiled=True)


def on_device(
    tokens,
    lengths,
    routes,
    norm_attn,
    w_query,
    w_key,
    w_value,
    w_attn_out,
    norm_moe,
    w_router,
    w_expert_in,
    w_expert_out,
    cotangent,
):
    owners = lax.axis_size("dp")
    pieces = lax.axis_size("tensor")
    expert_index = lax.axis_index("dp")
    piece_index = lax.axis_index("tensor")
    piece_rows, width = tokens.shape
    shard = w_query.shape[0]
    local_width = w_query.shape[1]
    experts = w_router.shape[1]
    capacity = 3 * piece_rows // (2 * experts)
    heads = local_width // HEAD_DIM

    gains = jnp.concatenate([norm_attn, norm_moe]).reshape(1, 2 * shard)
    small = jnp.concatenate(
        [w_router.reshape(1, -1), jnp.pad(gains, ((0, 0), (0, width - 2 * shard)))], axis=0
    )
    small = jnp.pad(small, ((0, 14), (0, 0)))
    large = jnp.concatenate([w_query, w_key, w_value, w_attn_out.T], axis=1)
    weights, smalls = ring_gather(jnp.concatenate([large, small], axis=0), shard)
    weights = weights.reshape(owners * shard, 4 * local_width)
    w_qkv = weights[:, : 3 * local_width]
    w_out_t = weights[:, 3 * local_width :]
    router = smalls[:, 0, :].reshape(owners * shard, experts)
    gain_one = smalls[:, 1, :shard].reshape(width).astype(FULL)
    gain_two = smalls[:, 1, shard : 2 * shard].reshape(width).astype(FULL)

    route = lax.dynamic_slice_in_dim(routes[:, 0], piece_index * piece_rows, piece_rows)
    expert_ids = jnp.arange(experts, dtype=jnp.int32)
    chosen = (route[:, None] == expert_ids[None, :]).astype(LOW)
    ids = jnp.arange(piece_rows, dtype=jnp.int32)
    before = (ids[None, :] < ids[:, None]).astype(LOW)
    earlier = dot(before, chosen)
    slot = jnp.sum(earlier * chosen.astype(FULL), axis=1).astype(jnp.int32)
    place = route * capacity + slot
    slots = experts * capacity
    spread = (jnp.arange(slots, dtype=jnp.int32)[:, None] == place[None, :]).astype(LOW)

    def dispatch(rows):
        return exchange(dot(spread, rows).astype(LOW).reshape(experts, capacity, width)).reshape(
            slots, width
        )

    def collect(rows):
        back = exchange(rows.reshape(experts, capacity, width)).reshape(slots, width)
        return dot_tn(spread, back)

    group = gather_rows(tokens).astype(FULL)
    group_rows = group.shape[0]
    group_root = lax.rsqrt(jnp.mean(group * group, axis=1, keepdims=True) + EPSILON)
    group_one = (group * group_root * gain_one).astype(LOW)
    qkv = dot(group_one, w_qkv).astype(LOW)

    def by_head(values):
        return values.reshape(group_rows, heads, HEAD_DIM)

    queries = by_head(qkv[:, :local_width])
    key_rows = by_head(qkv[:, local_width : 2 * local_width])
    value_rows = by_head(qkv[:, 2 * local_width :])
    block_piece = piece_index ^ jnp.array(block_offsets(), jnp.int32)
    positions = (block_piece[:, None] * piece_rows + ids[None, :]).reshape(group_rows)
    ends = jnp.cumsum(lengths[0])
    segment = jnp.sum((positions[:, None] >= ends[None, :]).astype(jnp.int32), axis=1)
    allowed = (segment[:, None] == segment[None, :]) & (positions[None, :] <= positions[:, None])
    scale = HEAD_DIM ** (-0.5)
    scores = jnp.einsum("qhd,khd->hqk", queries, key_rows, preferred_element_type=FULL) * scale
    scores = jnp.where(allowed[None], scores, NEGATIVE)
    largest = jnp.max(scores, axis=2, keepdims=True)
    shifted = jnp.exp(scores - largest)
    probs = shifted / jnp.sum(shifted, axis=2, keepdims=True)
    probs_low = probs.astype(LOW)
    attended = jnp.einsum("hqk,khd->qhd", probs_low, value_rows, preferred_element_type=FULL)
    attended = attended.reshape(group_rows, local_width).astype(LOW)
    attn = scatter_rows(dot_nt(attended, w_out_t))
    inputs = tokens.astype(FULL)
    middle = inputs + attn
    root_two = lax.rsqrt(jnp.mean(middle * middle, axis=1, keepdims=True) + EPSILON)
    normed_two = middle * root_two
    moe_input = (normed_two * gain_two).astype(LOW)

    weight_in = w_expert_in[0]
    weight_out = w_expert_out[0]
    cot_rows = dispatch(after(cotangent, qkv))
    own_rows = dispatch(moe_input)
    cot_all = gather_rows(after(cot_rows, moe_input))
    arrived = gather_rows(own_rows)
    pulled = dot_nt(cot_all, weight_out)
    hidden = dot(arrived, weight_in)
    active_full, gelu_pull = jax.vjp(jax.nn.gelu, hidden)
    active = active_full.astype(LOW)
    router_p = jax.nn.softmax(dot(arrived, router), axis=1)
    is_mine = (expert_ids == expert_index)[None, :]
    gate = jnp.sum(jnp.where(is_mine, router_p, 0.0), axis=1, keepdims=True)
    grad_hidden = gelu_pull(gate * pulled)[0].astype(LOW)
    grad_gate = jnp.sum(active.astype(FULL) * pulled, axis=1, keepdims=True)
    grad_logits = (gate * grad_gate * (is_mine.astype(FULL) - router_p)).astype(LOW)
    grad_two_part = dot_nt(grad_hidden, weight_in) + dot_nt(grad_logits, router)
    grad_two = collect(scatter_rows(grad_two_part).astype(LOW))

    expert_part = gate * dot(active, weight_out)
    expert_rows = scatter_rows(after(expert_part, grad_two_part)).astype(LOW)
    result = (middle + collect(expert_rows)).astype(LOW)
    grad_buffer = (gate * cot_all.astype(FULL)).astype(LOW)
    grad_expert_out = dot_tn(active, grad_buffer)
    grad_expert_in = dot_tn(arrived, grad_hidden)
    grad_router_part = dot_tn(grad_logits, arrived)

    upstream = cotangent.astype(FULL)
    scaled_two = grad_two * gain_two
    grad_gain_two = jnp.sum(grad_two * normed_two, axis=0, keepdims=True)
    grad_middle = upstream + root_two * (
        scaled_two - normed_two * jnp.mean(scaled_two * normed_two, axis=1, keepdims=True)
    )

    grad_attn = gather_rows(grad_middle.astype(LOW))
    grad_out_t = dot_tn(grad_attn, attended)
    grad_attended = by_head(dot(grad_attn, w_out_t).astype(LOW))
    grad_probs = jnp.einsum(
        "qhd,khd->hqk", grad_attended, value_rows, preferred_element_type=FULL
    )
    inner = jnp.sum(probs * grad_probs, axis=2, keepdims=True)
    grad_scores = (probs * (grad_probs - inner)).astype(LOW)
    grad_query = jnp.einsum("hqk,khd->qhd", grad_scores, key_rows, preferred_element_type=FULL)
    grad_key = jnp.einsum("hqk,qhd->khd", grad_scores, queries, preferred_element_type=FULL)
    grad_value = jnp.einsum("hqk,qhd->khd", probs_low, grad_attended, preferred_element_type=FULL)
    grad_qkv = jnp.concatenate(
        [
            (grad_query * scale).reshape(group_rows, local_width).astype(LOW),
            (grad_key * scale).reshape(group_rows, local_width).astype(LOW),
            grad_value.reshape(group_rows, local_width).astype(LOW),
        ],
        axis=1,
    )
    grad_w = jnp.concatenate([dot_tn(group_one, grad_qkv), grad_out_t], axis=1).astype(LOW)
    grad_one = scatter_rows(dot_nt(grad_qkv, w_qkv))

    root_one = group_root[:piece_rows]
    normed_one = inputs * root_one
    scaled_one = grad_one * gain_one
    grad_gain_one = jnp.sum(grad_one * normed_one, axis=0, keepdims=True)
    grad_tokens = grad_middle + root_one * (
        scaled_one - normed_one * jnp.mean(scaled_one * normed_one, axis=1, keepdims=True)
    )

    blocks = exchange(grad_w.reshape(owners, shard, 4 * local_width))
    grad_w_sum = jnp.sum(blocks.astype(FULL), axis=0)

    def sum_small(values):
        count = values.shape[0]
        parts = values.reshape(count, owners, shard).transpose(1, 0, 2)
        total = jnp.sum(exchange(parts), axis=0)
        for bit in reversed(tensor_bits()):
            total = total + swap(total, "tensor", bit)
        return total

    early = sum_small(jnp.concatenate([grad_router_part, grad_gain_two], axis=0))
    late = sum_small(grad_gain_one)
    return (
        result,
        grad_tokens,
        late[0],
        grad_w_sum[:, :local_width],
        grad_w_sum[:, local_width : 2 * local_width],
        grad_w_sum[:, 2 * local_width : 3 * local_width],
        grad_w_sum[:, 3 * local_width :].T,
        early[experts],
        early[:experts].T,
        grad_expert_in[None],
        grad_expert_out[None],
    )


def solution(mesh):
    return jax.shard_map(
        on_device,
        mesh=mesh,
        in_specs=(
            P(("dp", "tensor"), None),
            P("dp", None),
            P("dp", None),
            P("dp"),
            P("dp", "tensor"),
            P("dp", "tensor"),
            P("dp", "tensor"),
            P("tensor", "dp"),
            P("dp"),
            P("dp", None),
            P("dp", None, "tensor"),
            P("dp", "tensor", None),
            P(("dp", "tensor"), None),
        ),
        out_specs=(
            P(("dp", "tensor"), None),
            P(("dp", "tensor"), None),
            P("dp"),
            P("dp", "tensor"),
            P("dp", "tensor"),
            P("dp", "tensor"),
            P("tensor", "dp"),
            P("dp"),
            P("dp", None),
            P("dp", None, "tensor"),
            P("dp", "tensor", None),
        ),
        check_vma=False,
    )
```

time: 577 us -> 267 us (0.46)
  blocking collectives: 338 us -> 0 us
  waiting for transfers between devices: 132 us -> 69.5 us
  starting transfers between devices: 16.6 us -> 53 us
  local copies, waits for them, and re-layouts: 26.6 us -> 46 us
  other arithmetic: 14.4 us -> 29.3 us
  matrix products: 33.2 us -> 46.9 us
    all_gather x9 -> x0, blocking collectives: 184 us -> none  [the longest x4 33.4 us: gather_rows(): return lax.all_gather(values, 'tensor', axis=0, tiled=True)]
    all_to_all x3 -> x0, blocking collectives: 125 us -> none  [the longest x2 67.8 us: send_out(): return lax.all_to_all(buffer, 'dp', split_axis=0, concat_axis=0, tiled=True)]
    all_to_all x4 -> x7, waiting for transfers between devices: 82.8 us -> 32.6 us  [exchange(): return lax.all_to_all(buffer, 'dp', split_axis=0, concat_axis=0, tiled=True)]
    reduce_scatter x4 -> x0, waiting for transfers between devices: 49.1 us -> none  [scatter_rows(): return lax.psum_scatter(values, 'tensor', scatter_dimension=0, tiled=True)]
    ppermute x0 -> x28, waiting for transfers between devices: none -> 36.9 us  [the longest x20 33.8 us: swap(): return lax.ppermute(values, axis, [(i, i ^ bit) for i in range(count)])]
    unnamed x1 -> x0, blocking collectives: 23.1 us -> none
    ppermute x0 -> x28, starting transfers between devices: none -> 20.6 us  [the longest x20 11.4 us: swap(): return lax.ppermute(values, axis, [(i, i ^ bit) for i in range(count)])]
    all_to_all x4 -> x7, starting transfers between devices: 16.4 us -> 32.4 us  [exchange(): return lax.all_to_all(buffer, 'dp', split_axis=0, concat_axis=0, tiled=True)]
  transfers between devices with their start and end apart: 8 -> 35, of which waited for: 6 -> 18; matrix products, arithmetic and copies ran while one was open for 4% -> 34% of each run, Pallas kernels for 0% -> 0%
where the time goes in v1:
time: 267 us; the launch traced here: 265 us
  waiting for transfers between devices  69.5 us (26%)
  starting transfers between devices  53 us (20%)
  matrix products  46.9 us (18%)
  local copies, waits for them, and re-layouts  46 us (17%)
  other arithmetic  29.3 us (11%)
  between operations  20.1 us (8%)
    ppermute x20, waiting for transfers between devices, swap(): return lax.ppermute(values, axis, [(i, i ^ bit) for i in range(count)])  33.8 us
    all_to_all x7, waiting for transfers between devices, exchange(): return lax.all_to_all(buffer, 'dp', split_axis=0, concat_axis=0, tiled=True)  32.6 us
    all_to_all x7, starting transfers between devices, exchange(): return lax.all_to_all(buffer, 'dp', split_axis=0, concat_axis=0, tiled=True)  32.4 us
    dot_general x7, matrix products, dot_tn(): lax.dot_general(a, b, (((0,), (0,)), ((), ())), preferred_element_type=FULL)  16.7 us
    dot_general x8, matrix products, dot(): return jnp.dot(a, b, preferred_element_type=FULL)  11.6 us
    dynamic_update_slice x8, local copies, waits for them, and re-layouts, put(): lax.dynamic_update_index_in_dim(two, rows[split:], source, 0)  11.5 us
    ppermute x20, starting transfers between devices, swap(): return lax.ppermute(values, axis, [(i, i ^ bit) for i in range(count)])  11.4 us
    unnamed x121, local copies, waits for them, and re-layouts  9.76 us
  transfers between devices with their start and end apart: 35, of which 18 were waited for; matrix products, arithmetic and copies ran while one was open for 34% of the time, Pallas kernels for 0%

profile of v1, /device:TPU:0, one launch (start us, length us, event | category | flops | bytes accessed | tf_op | source)
XLA Modules:
  0.0 264.8 jit_solution(14906903065664520313)
XLA Ops:
  4.3 3.0 %collective-permute-start.3 = (bf16[112,768]{1,0:T(8,128)(2,1)S(1)}, bf16[112,768]{1,0:T(8,128)(2,1)}, u32[]{:S(2)}, u32[]{:S(2)}) collective-permute-start(bf16[112,768]{1,0:T(8,128)(2,1)S(1)} %pad_maximum_fusion.15), channel_id=1, source_target_pairs={{8,0},{16,8},{24,16},{28,24},{20,28},{12,20},{4,12},{0,4},{9,1},{1... | collective-permute-start | bytes 516104 | tf_op jit(solution)/shard_map/ppermute | solution.py:96
  51.7 3.1 %collective-permute-done.7 = bf16[112,768]{1,0:T(8,128)(2,1)S(1)} collective-permute-done((bf16[112,768]{1,0:T(8,128)(2,1)}, bf16[112,768]{1,0:T(8,128)(2,1)S(1)}, u32[]{:S(2)}, u32[]{:S(2)}) %collective-permute-start.7) | collective-permute-done | bytes 172064 | tf_op jit(solution)/shard_map/ppermute | solution.py:96
  68.7 4.1 %fusion.83 = (f32[3,512]{1,0:T(4,128)S(1)}, f32[3,512,512]{1,2,0:T(8,128)}) fusion(pred[512,512]{0,1:T(8,128)(4,1)} %compare_and_fusion, bf16[512,3,64]{0,2,1:T(8,128)(2,1)S(1)} %bitcast.178, bf16[512,3,64]{0,2,1:T(8,128)(2,1)S(1)} %bitcast.176), kind=kOutput, calls=%fused_computation.186 | convolution fusion | flops 103809536 | bytes 3807232 | tf_op jit(solution)/shard_map/sub | solution.py:191
  81.7 6.5 %collective-permute-done.11 = bf16[128,768]{1,0:T(8,128)(2,1)S(1)} collective-permute-done((bf16[128,768]{1,0:T(8,128)(2,1)S(1)}, bf16[128,768]{1,0:T(8,128)(2,1)S(1)}, u32[]{:S(2)}, u32[]{:S(2)}) %collective-permute-start.11) | collective-permute-done | bytes 196640 | tf_op jit(solution)/shard_map/ppermute | solution.py:31
  90.5 5.8 %all-to-all-start = ((bf16[8,24,768]{2,1,0:T(8,128)(2,1)}), bf16[8,24,768]{2,1,0:T(8,128)(2,1)S(1)}, u32[]{:S(2)}, u32[]{:S(2)}) async-start(bf16[8,24,768]{2,1,0:T(8,128)(2,1)} %bitcast.41), calls=%async_computation | async-start | bytes 589824 | tf_op jit(solution)/shard_map/all_to_all | solution.py:107
  96.3 9.0 %all-to-all-done = bf16[8,24,768]{2,1,0:T(8,128)(2,1)S(1)} async-done(((bf16[8,24,768]{2,1,0:T(8,128)(2,1)}), bf16[8,24,768]{2,1,0:T(8,128)(2,1)S(1)}, u32[]{:S(2)}, u32[]{:S(2)}) %all-to-all-start) | async-done | bytes 294944 | tf_op jit(solution)/shard_map/all_to_all | solution.py:107
  106.8 3.6 %all-to-all-start.1 = ((bf16[8,24,768]{2,1,0:T(8,128)(2,1)}), bf16[8,24,768]{2,1,0:T(8,128)(2,1)S(1)}, u32[]{:S(2)}, u32[]{:S(2)}) async-start(bf16[8,24,768]{2,1,0:T(8,128)(2,1)} %bitcast.45), calls=%async_computation.1 | async-start | bytes 589824 | tf_op jit(solution)/shard_map/all_to_all | solution.py:107
  112.9 6.3 %all-to-all-done.1 = bf16[8,24,768]{2,1,0:T(8,128)(2,1)S(1)} async-done(((bf16[8,24,768]{2,1,0:T(8,128)(2,1)}), bf16[8,24,768]{2,1,0:T(8,128)(2,1)S(1)}, u32[]{:S(2)}, u32[]{:S(2)}) %all-to-all-start.1) | async-done | bytes 294944 | tf_op jit(solution)/shard_map/all_to_all | solution.py:107
  122.0 5.9 %collective-permute-done.14 = bf16[192,768]{0,1:T(8,128)(2,1)} collective-permute-done((bf16[192,768]{0,1:T(8,128)(2,1)S(1)}, bf16[192,768]{0,1:T(8,128)(2,1)}, u32[]{:S(2)}, u32[]{:S(2)}) %collective-permute-start.14) | collective-permute-done | bytes 294944 | tf_op jit(solution)/shard_map/ppermute | solution.py:31
  133.4 4.0 %multiply_reduce_fusion.1 = (f32[768]{0:T(1024)S(1)}, bf16[768,768]{0,1:T(8,128)(2,1)S(1)}) fusion(f32[768,768]{0,1:T(8,128)S(1)} %fusion.20, f32[768]{0:T(1024)S(1)} %select_reduce_fusion, bf16[384,768]{0,1:T(8,128)(2,1)S(1)} %collective-permute-done.15, bf16[192,768]{0,1:T(8,128)(2,1)} %collective-permute-done.14, bf16[192,768]{0,1:T(8,128)(2,1)S(1)} %copy.125, ...), kind=kOutput, calls=%fused_computation.17 | convolution fusion | flops 924843264 | bytes 5904384 | tf_op jit(solution)/shard_map/dot_general | solution.py:18
  143.0 7.8 %collective-permute-done.19 = bf16[192,768]{1,0:T(8,128)(2,1)S(1)} collective-permute-done((bf16[192,768]{1,0:T(8,128)(2,1)S(1)}, bf16[192,768]{1,0:T(8,128)(2,1)S(1)}, u32[]{:S(2)}, u32[]{:S(2)}) %collective-permute-start.19) | collective-permute-done | bytes 294944 | tf_op jit(solution)/shard_map/ppermute | solution.py:31
  151.6 5.5 %all-to-all-start.3 = ((bf16[8,24,768]{2,1,0:T(8,128)(2,1)}), bf16[8,24,768]{2,1,0:T(8,128)(2,1)S(1)}, u32[]{:S(2)}, u32[]{:S(2)}) async-start(bf16[8,24,768]{2,1,0:T(8,128)(2,1)} %bitcast.49), calls=%async_computation.3 | async-start | bytes 589824 | tf_op jit(solution)/shard_map/all_to_all | solution.py:107
  157.6 3.1 %convolution_multiply_fusion = f32[768,768]{0,1:T(8,128)S(1)} fusion(bf16[1,768,768]{2,1,0:T(8,128)(2,1)S(1)} %copy-done, f32[768]{0:T(1024)S(1)} %select_reduce_fusion, f32[768,768]{0,1:T(8,128)} %copy-done.56), kind=kOutput, calls=%fused_computation.24 | convolution fusion | flops 911867904 | bytes 5901312 | tf_op jit(solution)/shard_map/dot_general | solution.py:14
  162.2 4.1 %all-to-all-done.3 = bf16[8,24,768]{2,1,0:T(8,128)(2,1)S(1)} async-done(((bf16[8,24,768]{2,1,0:T(8,128)(2,1)}), bf16[8,24,768]{2,1,0:T(8,128)(2,1)S(1)}, u32[]{:S(2)}, u32[]{:S(2)}) %all-to-all-start.3) | async-done | bytes 294944 | tf_op jit(solution)/shard_map/all_to_all | solution.py:107
  178.0 3.3 %collective-permute-done.17 = bf16[192,768]{0,1:T(8,128)(2,1)} collective-permute-done((bf16[192,768]{0,1:T(8,128)(2,1)}, bf16[192,768]{0,1:T(8,128)(2,1)}, u32[]{:S(2)}, u32[]{:S(2)}) %collective-permute-start.17) | collective-permute-done | bytes 294944 | tf_op jit(solution)/shard_map/ppermute | solution.py:31
  183.2 4.4 %all-to-all-start.2 = ((bf16[8,24,768]{2,1,0:T(8,128)(2,1)}), bf16[8,24,768]{2,1,0:T(8,128)(2,1)}, u32[]{:S(2)}, u32[]{:S(2)}) async-start(bf16[8,24,768]{2,1,0:T(8,128)(2,1)} %bitcast.47), calls=%async_computation.2 | async-start | bytes 589824 | tf_op jit(solution)/shard_map/all_to_all | solution.py:107
  210.1 6.0 %all-to-all-start.6 = ((f32[8,1,864]{2,1,0:T(1,128)}), f32[8,1,864]{2,1,0:T(1,128)}, u32[]{:S(2)}, u32[]{:S(2)}) async-start(f32[8,1,864]{2,1,0:T(1,128)} %reshape.312), calls=%async_computation.6 | async-start | bytes 57344 | tf_op jit(solution)/shard_map/all_to_all | solution.py:107
  218.5 4.4 %all-to-all-done.6 = f32[8,1,864]{2,1,0:T(1,128)} async-done(((f32[8,1,864]{2,1,0:T(1,128)}), f32[8,1,864]{2,1,0:T(1,128)}, u32[]{:S(2)}, u32[]{:S(2)}) %all-to-all-start.6) | async-done | bytes 27680 | tf_op jit(solution)/shard_map/all_to_all | solution.py:107
  222.9 3.3 %all-to-all-start.4 = ((f32[8,1,96]{2,1,0:T(1,128)}), f32[8,1,96]{2,1,0:T(1,128)S(1)}, u32[]{:S(2)}, u32[]{:S(2)}) async-start(f32[8,1,96]{2,1,0:T(1,128)} %transpose_reshape_broadcast_in_dim.3), calls=%async_computation.4 | async-start | bytes 8192 | tf_op jit(solution)/shard_map/all_to_all | solution.py:107
  228.5 4.0 %all-to-all-done.4 = f32[8,1,96]{2,1,0:T(1,128)S(1)} async-done(((f32[8,1,96]{2,1,0:T(1,128)}), f32[8,1,96]{2,1,0:T(1,128)S(1)}, u32[]{:S(2)}, u32[]{:S(2)}) %all-to-all-start.4) | async-done | bytes 3104 | tf_op jit(solution)/shard_map/all_to_all | solution.py:107
  232.5 3.7 %all-to-all-start.5 = ((bf16[8,96,768]{2,1,0:T(8,128)(2,1)}), bf16[8,96,768]{2,1,0:T(8,128)(2,1)S(1)}, u32[]{:S(2)}, u32[]{:S(2)}) async-start(bf16[8,96,768]{2,1,0:T(8,128)(2,1)} %pad_maximum_fusion.2), calls=%async_computation.5 | async-start | bytes 2359296 | tf_op jit(solution)/shard_map/all_to_all | solution.py:107
  236.2 5.0 %convolution_bitcast_fusion = f32[1,768,768]{2,1,0:T(8,128)} fusion(f32[768]{0:T(1024)S(1)} %select_reduce_fusion, bf16[384,768]{0,1:T(8,128)(2,1)} %copy-done.54, bf16[192,768]{0,1:T(8,128)(2,1)} %collective-permute-done.14, bf16[192,768]{0,1:T(8,128)(2,1)S(1)} %copy-done.13, f32[768,768]{0,1:T(8,128)} %copy-done.56), kind=kOutput, calls=%fused_computation.22 | convolution fusion | flops 915996672 | bytes 5901312 | tf_op jit(solution)/shard_map/dot_general | solution.py:22
  243.5 4.2 %convolution_bitcast_fusion.1 = f32[1,768,768]{2,1,0:T(8,128)} fusion(bf16[768,768]{0,1:T(8,128)(2,1)} %copy-done.57, bf16[384,768]{1,0:T(8,128)(2,1)} %collective-permute-done.13, bf16[192,768]{1,0:T(8,128)(2,1)} %copy-done.29, bf16[192,768]{1,0:T(8,128)(2,1)} %bitcast.172), kind=kOutput, calls=%fused_computation.23 | convolution fusion | flops 909508608 | bytes 4718592 | tf_op jit(solution)/shard_map/dot_general | solution.py:22
  258.4 4.7 %all-to-all-done.5 = bf16[8,96,768]{2,1,0:T(8,128)(2,1)S(1)} async-done(((bf16[8,96,768]{2,1,0:T(8,128)(2,1)}), bf16[8,96,768]{2,1,0:T(8,128)(2,1)S(1)}, u32[]{:S(2)}, u32[]{:S(2)}) %all-to-all-start.5) | async-done | bytes 1179680 | tf_op jit(solution)/shard_map/all_to_all | solution.py:107
  (307 shorter events, 129.8 us)
Async XLA Ops:
  4.3 30.2 %collective-permute-start.3 = (bf16[112,768]{1,0:T(8,128)(2,1)S(1)}, bf16[112,768]{1,0:T(8,128)(2,1)}, u32[]{:S(2)}, u32[]{:S(2)}) collective-permute-start(bf16[112,768]{1,0:T(8,128)(2,1)S(1)} %pad_maximum_fusion.15), channel_id=1, source_target_pairs={{8,0},{16,8},{24,16},{28,24},{20,28},{12,20},{4,12},{0,4},{9,1},{1... | collective-permute-start | bytes 516104 | tf_op jit(solution)/shard_map/ppermute | solution.py:96
  7.3 29.6 %collective-permute-start.2 = (bf16[112,768]{1,0:T(8,128)(2,1)S(1)}, bf16[112,768]{1,0:T(8,128)(2,1)}, u32[]{:S(2)}, u32[]{:S(2)}) collective-permute-start(bf16[112,768]{1,0:T(8,128)(2,1)S(1)} %pad_maximum_fusion.15), channel_id=1, source_target_pairs={{0,8},{8,16},{16,24},{24,28},{28,20},{20,12},{12,4},{4,0},{1,9},{9... | collective-permute-start | bytes 516104 | tf_op jit(solution)/shard_map/ppermute | solution.py:95
  7.5 35.0 %collective-permute-start = (bf16[128,768]{1,0:T(8,128)(2,1)}, bf16[128,768]{1,0:T(8,128)(2,1)S(1)}, u32[]{:S(2)}, u32[]{:S(2)}) collective-permute-start(bf16[128,768]{1,0:T(8,128)(2,1)} %param.16), channel_id=1, source_target_pairs={{0,2},{1,3},{2,0},{3,1},{4,6},{5,7},{6,4},{7,5},{8,10},{9,11},{10,... | collective-permute-start | bytes 589832 | tf_op jit(solution)/shard_map/ppermute | solution.py:31
  34.5 8.7 %collective-permute-start.5 = (bf16[112,768]{1,0:T(8,128)(2,1)}, bf16[112,768]{1,0:T(8,128)(2,1)}, u32[]{:S(2)}, u32[]{:S(2)}) collective-permute-start(bf16[112,768]{1,0:T(8,128)(2,1)} %collective-permute-done.3), channel_id=1, source_target_pairs={{8,0},{16,8},{24,16},{28,24},{20,28},{12,20},{4,12},{0,4},{9,1},{1... | collective-permute-start | bytes 516104 | tf_op jit(solution)/shard_map/ppermute | solution.py:96
  36.9 7.2 %collective-permute-start.4 = (bf16[112,768]{1,0:T(8,128)(2,1)}, bf16[112,768]{1,0:T(8,128)(2,1)}, u32[]{:S(2)}, u32[]{:S(2)}) collective-permute-start(bf16[112,768]{1,0:T(8,128)(2,1)} %collective-permute-done.2), channel_id=1, source_target_pairs={{0,8},{8,16},{16,24},{24,28},{28,20},{20,12},{12,4},{4,0},{1,9},{9... | collective-permute-start | bytes 516104 | tf_op jit(solution)/shard_map/ppermute | solution.py:95
  43.3 19.5 %collective-permute-start.1 = (bf16[256,768]{1,0:T(8,128)(2,1)}, bf16[256,768]{1,0:T(8,128)(2,1)S(1)}, u32[]{:S(2)}, u32[]{:S(2)}) collective-permute-start(bf16[256,768]{1,0:T(8,128)(2,1)} %pad_maximum_fusion.8), channel_id=1, source_target_pairs={{0,1},{1,0},{2,3},{3,2},{4,5},{5,4},{6,7},{7,6},{8,9},{9,8},{10,11... | collective-permute-start | bytes 1179656 | tf_op jit(solution)/shard_map/ppermute | solution.py:31
  49.3 7.7 %collective-permute-start.6 = (bf16[112,768]{1,0:T(8,128)(2,1)}, bf16[112,768]{1,0:T(8,128)(2,1)S(1)}, u32[]{:S(2)}, u32[]{:S(2)}) collective-permute-start(bf16[112,768]{1,0:T(8,128)(2,1)} %collective-permute-done.4), channel_id=1, source_target_pairs={{0,8},{8,16},{16,24},{24,28},{28,20},{20,12},{12,4},{4,0},{1,9},{9... | collective-permute-start | bytes 516104 | tf_op jit(solution)/shard_map/ppermute | solution.py:95
  55.5 7.5 %collective-permute-start.8 = (bf16[64,768]{1,0:T(8,128)(2,1)}, bf16[64,768]{1,0:T(8,128)(2,1)}, u32[]{:S(2)}, u32[]{:S(2)}) collective-permute-start(bf16[64,768]{1,0:T(8,128)(2,1)} %slice.203), channel_id=1, source_target_pairs={{8,0},{16,8},{24,16},{28,24},{20,28},{12,20},{4,12},{0,4},{9,1},{1... | collective-permute-start | bytes 294920 | tf_op jit(solution)/shard_map/ppermute | solution.py:101
  58.3 8.3 %collective-permute-start.9 = (bf16[48,768]{1,0:T(8,128)(2,1)}, bf16[48,768]{1,0:T(8,128)(2,1)}, u32[]{:S(2)}, u32[]{:S(2)}) collective-permute-start(bf16[48,768]{1,0:T(8,128)(2,1)} %slice.212), channel_id=1, source_target_pairs={{0,8},{8,16},{16,24},{24,28},{28,20},{20,12},{12,4},{4,0},{1,9},{9... | collective-permute-start | bytes 221192 | tf_op jit(solution)/shard_map/ppermute | solution.py:100
  90.5 14.9 %all-to-all-start = ((bf16[8,24,768]{2,1,0:T(8,128)(2,1)}), bf16[8,24,768]{2,1,0:T(8,128)(2,1)S(1)}, u32[]{:S(2)}, u32[]{:S(2)}) async-start(bf16[8,24,768]{2,1,0:T(8,128)(2,1)} %bitcast.41), calls=%async_computation | async-start | bytes 589824 | tf_op jit(solution)/shard_map/all_to_all | solution.py:107
  106.8 12.5 %all-to-all-start.1 = ((bf16[8,24,768]{2,1,0:T(8,128)(2,1)}), bf16[8,24,768]{2,1,0:T(8,128)(2,1)S(1)}, u32[]{:S(2)}, u32[]{:S(2)}) async-start(bf16[8,24,768]{2,1,0:T(8,128)(2,1)} %bitcast.45), calls=%async_computation.1 | async-start | bytes 589824 | tf_op jit(solution)/shard_map/all_to_all | solution.py:107
  112.9 16.3 %collective-permute-start.13 = (bf16[384,768]{1,0:T(8,128)(2,1)}, bf16[384,768]{1,0:T(8,128)(2,1)}, u32[]{:S(2)}, u32[]{:S(2)}) collective-permute-start(bf16[384,768]{1,0:T(8,128)(2,1)} %pad_maximum_fusion.5), channel_id=1, source_target_pairs={{0,1},{1,0},{2,3},{3,2},{4,5},{5,4},{6,7},{7,6},{8,9},{9,8},{10,11... | collective-permute-start | bytes 1769480 | tf_op jit(solution)/shard_map/ppermute | solution.py:31
  119.5 8.5 %collective-permute-start.14 = (bf16[192,768]{0,1:T(8,128)(2,1)S(1)}, bf16[192,768]{0,1:T(8,128)(2,1)}, u32[]{:S(2)}, u32[]{:S(2)}) collective-permute-start(bf16[192,768]{0,1:T(8,128)(2,1)S(1)} %copy.125), channel_id=1, source_target_pairs={{0,2},{1,3},{2,0},{3,1},{4,6},{5,7},{6,4},{7,5},{8,10},{9,11},{10,... | collective-permute-start | bytes 884744 | tf_op jit(solution)/shard_map/ppermute | solution.py:31
  141.4 9.4 %collective-permute-start.19 = (bf16[192,768]{1,0:T(8,128)(2,1)S(1)}, bf16[192,768]{1,0:T(8,128)(2,1)S(1)}, u32[]{:S(2)}, u32[]{:S(2)}) collective-permute-start(bf16[192,768]{1,0:T(8,128)(2,1)S(1)} %slice.312), channel_id=1, source_target_pairs={{0,2},{1,3},{2,0},{3,1},{4,6},{5,7},{6,4},{7,5},{8,10},{9,11},{10,... | collective-permute-start | bytes 884744 | tf_op jit(solution)/shard_map/ppermute | solution.py:31
  151.6 14.8 %all-to-all-start.3 = ((bf16[8,24,768]{2,1,0:T(8,128)(2,1)}), bf16[8,24,768]{2,1,0:T(8,128)(2,1)S(1)}, u32[]{:S(2)}, u32[]{:S(2)}) async-start(bf16[8,24,768]{2,1,0:T(8,128)(2,1)} %bitcast.49), calls=%async_computation.3 | async-start | bytes 589824 | tf_op jit(solution)/shard_map/all_to_all | solution.py:107
  167.0 7.4 %collective-permute-start.20 = (bf16[128,768]{1,0:T(8,128)(2,1)S(1)}, bf16[128,768]{1,0:T(8,128)(2,1)S(1)}, u32[]{:S(2)}, u32[]{:S(2)}) collective-permute-start(bf16[128,768]{1,0:T(8,128)(2,1)S(1)} %fusion.77), channel_id=1, source_target_pairs={{0,2},{1,3},{2,0},{3,1},{4,6},{5,7},{6,4},{7,5},{8,10},{9,11},{10,... | collective-permute-start | bytes 589832 | tf_op jit(solution)/shard_map/ppermute | solution.py:31
  171.0 10.2 %collective-permute-start.17 = (bf16[192,768]{0,1:T(8,128)(2,1)}, bf16[192,768]{0,1:T(8,128)(2,1)}, u32[]{:S(2)}, u32[]{:S(2)}) collective-permute-start(bf16[192,768]{0,1:T(8,128)(2,1)} %slice.310), channel_id=1, source_target_pairs={{0,2},{1,3},{2,0},{3,1},{4,6},{5,7},{6,4},{7,5},{8,10},{9,11},{10,... | collective-permute-start | bytes 884744 | tf_op jit(solution)/shard_map/ppermute | solution.py:31
  175.8 11.9 %collective-permute-start.21 = (bf16[256,768]{1,0:T(8,128)(2,1)}, bf16[256,768]{1,0:T(8,128)(2,1)}, u32[]{:S(2)}, u32[]{:S(2)}) collective-permute-start(bf16[256,768]{1,0:T(8,128)(2,1)} %pad_maximum_fusion.9), channel_id=1, source_target_pairs={{0,1},{1,0},{2,3},{3,2},{4,5},{5,4},{6,7},{7,6},{8,9},{9,8},{10,11... | collective-permute-start | bytes 1179656 | tf_op jit(solution)/shard_map/ppermute | solution.py:31
  183.2 26.9 %all-to-all-start.2 = ((bf16[8,24,768]{2,1,0:T(8,128)(2,1)}), bf16[8,24,768]{2,1,0:T(8,128)(2,1)}, u32[]{:S(2)}, u32[]{:S(2)}) async-start(bf16[8,24,768]{2,1,0:T(8,128)(2,1)} %bitcast.47), calls=%async_computation.2 | async-start | bytes 589824 | tf_op jit(solution)/shard_map/all_to_all | solution.py:107
  198.1 7.3 %collective-permute-start.22 = (bf16[256,768]{1,0:T(8,128)(2,1)}, bf16[256,768]{1,0:T(8,128)(2,1)}, u32[]{:S(2)}, u32[]{:S(2)}) collective-permute-start(bf16[256,768]{1,0:T(8,128)(2,1)} %slice.309), channel_id=1, source_target_pairs={{0,1},{1,0},{2,3},{3,2},{4,5},{5,4},{6,7},{7,6},{8,9},{9,8},{10,11... | collective-permute-start | bytes 1179656 | tf_op jit(solution)/shard_map/ppermute | solution.py:31
  207.5 8.6 %collective-permute-start.23 = (bf16[128,768]{1,0:T(8,128)(2,1)}, bf16[128,768]{1,0:T(8,128)(2,1)}, u32[]{:S(2)}, u32[]{:S(2)}) collective-permute-start(bf16[128,768]{1,0:T(8,128)(2,1)} %slice.313), channel_id=1, source_target_pairs={{0,2},{1,3},{2,0},{3,1},{4,6},{5,7},{6,4},{7,5},{8,10},{9,11},{10,... | collective-permute-start | bytes 589832 | tf_op jit(solution)/shard_map/ppermute | solution.py:31
  210.1 12.8 %all-to-all-start.6 = ((f32[8,1,864]{2,1,0:T(1,128)}), f32[8,1,864]{2,1,0:T(1,128)}, u32[]{:S(2)}, u32[]{:S(2)}) async-start(f32[8,1,864]{2,1,0:T(1,128)} %reshape.312), calls=%async_computation.6 | async-start | bytes 57344 | tf_op jit(solution)/shard_map/all_to_all | solution.py:107
  222.9 9.6 %all-to-all-start.4 = ((f32[8,1,96]{2,1,0:T(1,128)}), f32[8,1,96]{2,1,0:T(1,128)S(1)}, u32[]{:S(2)}, u32[]{:S(2)}) async-start(f32[8,1,96]{2,1,0:T(1,128)} %transpose_reshape_broadcast_in_dim.3), calls=%async_computation.4 | async-start | bytes 8192 | tf_op jit(solution)/shard_map/all_to_all | solution.py:107
  232.5 30.6 %all-to-all-start.5 = ((bf16[8,96,768]{2,1,0:T(8,128)(2,1)}), bf16[8,96,768]{2,1,0:T(8,128)(2,1)S(1)}, u32[]{:S(2)}, u32[]{:S(2)}) async-start(bf16[8,96,768]{2,1,0:T(8,128)(2,1)} %pad_maximum_fusion.2), calls=%async_computation.5 | async-start | bytes 2359296 | tf_op jit(solution)/shard_map/all_to_all | solution.py:107
  (69 other events, 867.5 us)

commit v2 on v1

v2 whole, which is shorter than its diff:
```python
import functools

import jax
import jax.numpy as jnp
from jax import lax
from jax.experimental import pallas as pl
from jax.experimental.pallas import tpu as pltpu
from jax.sharding import PartitionSpec as P

HEAD_DIM = 64
EPSILON = 1e-06
NEGATIVE = -1e30
LOW = jnp.bfloat16
FULL = jnp.float32
SCALE = HEAD_DIM ** (-0.5)
MIB = 1 << 20


def dot(a, b):
    return jnp.dot(a, b, preferred_element_type=FULL)


def dot_nt(a, b):
    return lax.dot_general(a, b, (((1,), (1,)), ((), ())), preferred_element_type=FULL)


def dot_tn(a, b):
    return lax.dot_general(a, b, (((0,), (0,)), ((), ())), preferred_element_type=FULL)


def after(value, *others):
    return lax.optimization_barrier((value, *others))[0]


class Fetched:
    def __init__(self, ref, held, sem):
        self.held, self.waiting = held, True
        self.copy = pltpu.make_async_copy(ref, held, sem)
        self.copy.start()
        self.shape = held.shape

    def wait(self):
        if self.waiting:
            self.copy.wait()
            self.waiting = False

    def __getitem__(self, index):
        self.wait()
        return self.held[index]


class Stored:
    def __init__(self, ref, held, sem):
        self.ref, self.held, self.sem = ref, held, sem
        self.copy = None
        self.shape, self.dtype = held.shape, held.dtype

    def __getitem__(self, index):
        return self.held[index]

    def __setitem__(self, index, value):
        self.held[index] = value

    def flush(self):
        if self.copy is None:
            self.copy = pltpu.make_async_copy(self.held, self.ref, self.sem)
            self.copy.start()


def kernel_call(body, outs, name, fetch=(), store=(), smem=(), time=1, limit=24, scratch=()):
    def call(*operands):
        n_in, n_out, n_scratch = len(operands), len(outs), len(scratch)
        held = [pltpu.VMEM(operands[i].shape, operands[i].dtype) for i in fetch]
        held += [pltpu.VMEM(*outs[i]) for i in store]
        sems = [pltpu.SemaphoreType.DMA((len(held),))] if held else []

        def kernel(*refs):
            ins, results = list(refs[:n_in]), list(refs[n_in : n_in + n_out])
            rest = refs[n_in + n_out :]
            own, buffers = rest[:n_scratch], rest[n_scratch : n_scratch + len(held)]
            sem = rest[-1] if held else None
            at = 0
            for i in fetch:
                ins[i] = Fetched(ins[i], buffers[at], sem.at[at])
                at += 1
            for i in store:
                results[i] = Stored(results[i], buffers[at], sem.at[at])
                at += 1
            body(*ins, *results, *own)
            for i in fetch:
                ins[i].wait()
            for i in store:
                results[i].flush()
            for i in store:
                results[i].copy.wait()

        def spec(i, hbm):
            return pl.BlockSpec(memory_space=pltpu.HBM if i in hbm else pltpu.VMEM)

        operands = [
            pltpu.with_memory_space_constraint(x, pltpu.HBM) if i in fetch else x
            for i, x in enumerate(operands)
        ]
        return pl.pallas_call(
            kernel,
            out_shape=[
                pltpu.HBM(*outs[i]) if i in store else jax.ShapeDtypeStruct(*outs[i])
                for i in range(n_out)
            ],
            in_specs=[
                pl.BlockSpec(memory_space=pltpu.SMEM) if i in smem else spec(i, fetch)
                for i in range(n_in)
            ],
            out_specs=[spec(i, store) for i in range(n_out)],
            scratch_shapes=[*scratch, *held, *sems],
            compiler_params=pltpu.CompilerParams(vmem_limit_bytes=limit * MIB),
            cost_estimate=pl.CostEstimate(
                flops=int(time * 1.1e9), bytes_accessed=MIB, transcendentals=0
            ),
            name=name,
        )(*operands)

    return call


def move_kernel(*refs):
    count = len(refs) // 2
    sem = refs[-1]
    copies = [
        pltpu.make_async_copy(refs[k], refs[count + k], sem.at[k]) for k in range(count)
    ]
    for copy in copies:
        copy.start()
    for copy in copies:
        copy.wait()


def moved(arrays, source, target, name):
    kinds = [(x.shape, x.dtype) for x in arrays]
    if source is pltpu.HBM:
        arrays = [pltpu.with_memory_space_constraint(x, pltpu.HBM) for x in arrays]
    return pl.pallas_call(
        move_kernel,
        out_shape=[
            pltpu.HBM(*kind) if target is pltpu.HBM else jax.ShapeDtypeStruct(*kind)
            for kind in kinds
        ],
        in_specs=[pl.BlockSpec(memory_space=source) for _ in kinds],
        out_specs=[pl.BlockSpec(memory_space=target) for _ in kinds],
        scratch_shapes=[pltpu.SemaphoreType.DMA((len(kinds),))],
        compiler_params=pltpu.CompilerParams(vmem_limit_bytes=16 * MIB),
        cost_estimate=pl.CostEstimate(flops=2 * 10**9, bytes_accessed=MIB, transcendentals=0),
        name=name,
    )(*arrays)


def save(*arrays):
    return moved(arrays, pltpu.VMEM, pltpu.HBM, "save")


def load(*arrays):
    return moved(arrays, pltpu.HBM, pltpu.VMEM, "load")


def swap(values, axis, bit):
    count = lax.axis_size(axis)
    return lax.ppermute(values, axis, [(i, i ^ bit) for i in range(count)])


def exchange(buffer):
    return lax.all_to_all(buffer, "dp", split_axis=0, concat_axis=0, tiled=True)


OFFSETS = (0, 2, 1, 3)


def swap_far(rows):
    return swap(rows, "tensor", 2)


def swap_near(rows):
    return swap(rows, "tensor", 1)


def ring_source(place, count):
    place = lax.rem(place + 2 * count, count)
    return jnp.where(place < count // 2, 2 * place, 2 * (count - 1 - place) + 1)


def ring_perms(count):
    order = list(range(0, count, 2)) + list(range(1, count, 2))[::-1]
    right = [(order[k], order[(k + 1) % count]) for k in range(count)]
    return right, [(b, a) for a, b in right]


def ring_gather(block):
    count = lax.axis_size("dp")
    right, left = ring_perms(count)
    behind, ahead = [block], [block]
    for _ in range(1, count // 2):
        behind.append(lax.ppermute(behind[-1], "dp", right))
        ahead.append(lax.ppermute(ahead[-1], "dp", left))
    middle = block.shape[0] // 32 * 16
    top = lax.ppermute(behind[-1][:middle], "dp", right)
    bottom = lax.ppermute(ahead[-1][middle:], "dp", left)
    return behind[1:], ahead[1:], top, bottom


def ring_place(me, count):
    return jnp.where(lax.rem(me, 2) == 0, me // 2, count - 1 - me // 2)


def ring_reduce(grad_w, scalars, blocks_shape):
    count = lax.axis_size("dp")
    right, left = ring_perms(count)
    shard, width = blocks_shape
    middle = shard // 32 * 16
    top, bottom = kernel_call(
        functools.partial(ring_first_kernel, count),
        [((middle, width), LOW), ((shard - middle, width), LOW)],
        "ring_first",
        smem=(0,),
    )(scalars, grad_w)
    ahead = lax.ppermute(top, "dp", right)
    behind = lax.ppermute(bottom, "dp", left)
    marks = [top]
    for step in range(count // 2 - 1, 0, -1):
        ahead, behind = kernel_call(
            functools.partial(ring_add_kernel, count, step),
            [((shard, width), LOW), ((shard, width), LOW)],
            "ring_add",
            smem=(0,),
        )(scalars, grad_w, ahead, behind)
        marks.append(ahead)
        ahead = lax.ppermute(ahead, "dp", right)
        behind = lax.ppermute(behind, "dp", left)
    return ahead, behind, marks


def root_of(values):
    return lax.rsqrt(jnp.mean(values * values, axis=1, keepdims=True) + EPSILON)


def pack_kernel(wq, wk, wv, wo, router, gain_one, gain_two, out):
    shard, local = wq.shape
    out[0:shard, 0:local] = wq[...]
    out[0:shard, local : 2 * local] = wk[...]
    out[0:shard, 2 * local : 3 * local] = wv[...]
    out[0:shard, 3 * local :] = wo[...].astype(FULL).T.astype(LOW)
    experts = router.shape[0]
    rows = out.shape[0] - shard
    small = jnp.concatenate(
        [
            router[...].astype(FULL),
            gain_one[...].astype(FULL),
            gain_two[...].astype(FULL),
            jnp.zeros((rows - experts - 2, shard), FULL),
        ],
        axis=0,
    )
    out[shard:, :] = jnp.zeros((rows, out.shape[1]), LOW)
    out[shard:, 0:shard] = small.astype(LOW)


def spread_kernel(capacity, slots, scalars, routes, cot, spread, rows):
    count = cot.shape[0]
    piece = scalars[1]
    route = routes[pl.ds(pl.multiple_of(piece * count, count), count), :]
    experts = slots // capacity
    ids = lax.broadcasted_iota(jnp.int32, (count, experts), 1)
    chosen = jnp.where(route == ids, 1.0, 0.0)
    first = lax.broadcasted_iota(jnp.int32, (count, count), 0)
    second = lax.broadcasted_iota(jnp.int32, (count, count), 1)
    before = jnp.where(second < first, 1.0, 0.0).astype(LOW)
    earlier = dot(before, chosen.astype(LOW))
    slot = jnp.sum(earlier * chosen, axis=1, keepdims=True).astype(jnp.int32)
    place = route * capacity + slot
    lanes = lax.broadcasted_iota(jnp.int32, (count, slots), 1)
    one_hot = jnp.where(place == lanes, 1.0, 0.0).astype(LOW)
    spread[...] = one_hot
    rows[...] = dot_tn(one_hot, cot[...]).astype(LOW)


def assemble_kernel(count, scalars, *refs):
    blocks, (weights, smalls) = refs[:-2], refs[-2:]
    me = scalars[0]
    place = ring_place(me, count)
    shard = weights.shape[0] // count
    half = count // 2
    steps = [0] + [-s for s in range(1, half)] + list(range(1, half))
    for step, block in zip(steps, blocks):
        source = ring_source(place + step, count) if step else me
        weights[pl.ds(pl.multiple_of(source * shard, 16), shard), :] = block[0:shard, :]
        smalls[source] = block[shard:, 0:shard].astype(FULL)


def finish(count, scalars, blocks, weights, smalls, small_out):
    shard = weights.shape[0] // count
    weights[...] = blocks[0][...]
    smalls[...] = blocks[1][...]
    top, bottom = blocks[2:]
    source = ring_source(ring_place(scalars[0], count) + count // 2, count)
    middle = top.shape[0]
    start = pl.multiple_of(source * shard, 16)
    weights[pl.ds(start, middle), :] = top[...]
    rest = shard - middle
    weights[pl.ds(pl.multiple_of(start + middle, 16), rest), :] = bottom[0:rest, :]
    smalls[source] = bottom[rest:, 0:shard].astype(FULL)
    for d in range(count):
        small_out[:, d * shard : (d + 1) * shard] = smalls[d]


def positions_of(piece, rows, shape, dim):
    index = lax.broadcasted_iota(jnp.int32, shape, dim)
    block = index // rows
    flip = jnp.where(block == 1, 2, jnp.where(block == 2, 1, block))
    return (piece ^ flip) * rows + lax.rem(index, rows)


def attend_kernel(count, sequences, has_blocks, *refs):
    scalars, tokens, far, near, near_far = refs[:5]
    given = 4 if has_blocks else 2
    blocks = refs[5 : 5 + given]
    outs = refs[5 + given :]
    keep, keep_far, send, send_far, ones, qkv_out, attended, probs_out, group = outs[:9]
    if has_blocks:
        weights, small_out, smalls = outs[9:]
        finish(count, scalars, blocks, weights, smalls, small_out)
        small = small_out
    else:
        weights, small = blocks
    rows = tokens.shape[0]
    total = 4 * rows
    local = attended.shape[1]
    experts = count
    gain = small[experts : experts + 1, :]
    piece = scalars[1]
    for index, ref in enumerate((tokens, far, near, near_far)):
        group[index * rows : (index + 1) * rows, :] = ref[...]
        values = ref[...].astype(FULL)
        ones[index * rows : (index + 1) * rows, :] = (values * root_of(values) * gain).astype(LOW)
    qkv = dot(ones[...], weights[:, 0 : 3 * local]).astype(LOW)
    qkv_out[...] = qkv
    query_pos = positions_of(piece, rows, (total, 1), 0)
    key_pos = positions_of(piece, rows, (1, total), 1)
    start = jnp.zeros((total, 1), jnp.int32)
    end = jnp.int32(0)
    for s in range(sequences):
        end = end + scalars[2 + s]
        start = jnp.where(query_pos >= end, end, start)
    bias = jnp.where((key_pos <= query_pos) & (key_pos >= start), 0.0, NEGATIVE)
    for h in range(local // HEAD_DIM):
        at = h * HEAD_DIM
        q = qkv[:, at : at + HEAD_DIM]
        k = qkv[:, local + at : local + at + HEAD_DIM]
        v = qkv[:, 2 * local + at : 2 * local + at + HEAD_DIM]
        scores = dot_nt(q, k) * SCALE + bias
        shifted = jnp.exp(scores - jnp.max(scores, axis=1, keepdims=True))
        probs = shifted * (1.0 / jnp.sum(shifted, axis=1, keepdims=True))
        probs_out[h] = probs
        attended[:, at : at + HEAD_DIM] = dot(probs.astype(LOW), v).astype(LOW)
    w_out_t = weights[:, 3 * local :]
    keep[...] = dot_nt(attended[0:rows, :], w_out_t)
    keep_far[...] = dot_nt(attended[rows : 2 * rows, :], w_out_t)
    send[...] = dot_nt(attended[2 * rows : 3 * rows, :], w_out_t).astype(LOW)
    send_far[...] = dot_nt(attended[3 * rows :, :], w_out_t).astype(LOW)


def middle_kernel(gain_row, tokens, keep, near, far, small, spread, middle, rows):
    total = tokens[...].astype(FULL) + (
        keep[...] + near[...].astype(FULL) + far[...].astype(FULL)
    )
    middle[...] = total
    moe = (total * root_of(total) * small[gain_row : gain_row + 1, :]).astype(LOW)
    rows[...] = dot_tn(spread[...], moe).astype(LOW)


def far_kernel(keep_far, near, out):
    out[...] = (keep_far[...] + near[...].astype(FULL)).astype(LOW)


GELU_A = 0.7978845608028654
GELU_B = 0.044715


def expert_kernel(
    experts,
    scalars,
    x_keep,
    x_send,
    cot_keep,
    cot_send,
    w_in,
    w_out,
    small,
    part_keep,
    part_send,
    active_out,
    hidden_out,
    buffer_out,
    gate_out,
    router_out,
    x,
    cot,
):
    rows = x_keep.shape[0]
    x[0:rows, :] = x_keep[...]
    x[rows:, :] = x_send[...]
    cot[0:rows, :] = cot_keep[...]
    cot[rows:, :] = cot_send[...]
    hidden = dot(x[...], w_in[...])
    pulled = dot_nt(cot[...], w_out[...])
    router_t = small[0:experts, :].astype(LOW)
    mine = lax.broadcasted_iota(jnp.int32, (2 * rows, experts), 1) == scalars[0]
    logits = dot_nt(x[...], router_t)
    raised = jnp.exp(logits - jnp.max(logits, axis=1, keepdims=True))
    chances = raised / jnp.sum(raised, axis=1, keepdims=True)
    gate = jnp.sum(jnp.where(mine, chances, 0.0), axis=1, keepdims=True)
    square = hidden * hidden
    wave = jnp.tanh(GELU_A * hidden * (1.0 + GELU_B * square))
    half = 0.5 + 0.5 * wave
    active = (hidden * half).astype(LOW)
    active_out[...] = active
    slope = half + 0.5 * GELU_A * hidden * (1.0 - wave * wave) * (1.0 + 3.0 * GELU_B * square)
    grad_hidden = (gate * pulled * slope).astype(LOW)
    hidden_out[...] = grad_hidden
    grad_gate = jnp.sum(active.astype(FULL) * pulled, axis=1, keepdims=True)
    grad_logits = (gate * grad_gate * (jnp.where(mine, 1.0, 0.0) - chances)).astype(LOW)
    buffer_out[...] = (gate * cot[...].astype(FULL)).astype(LOW)
    gate_out[...] = gate
    router_out[...] = dot_tn(grad_logits, x[...])
    part = dot_nt(grad_hidden, w_in[...]) + dot(grad_logits, router_t)
    part_keep[...] = part[0:rows, :]
    part_send[...] = part[rows:, :].astype(LOW)


def forward_kernel(
    first, first_gate, second, second_gate, w_out, keep, send, keep_far, send_far
):
    rows = keep.shape[0]
    part = second_gate[...] * dot(second[...], w_out[...])
    keep_far[...] = part[0:rows, :]
    send_far[...] = part[rows:, :].astype(LOW)
    part = first_gate[...] * dot(first[...], w_out[...])
    keep[...] = part[0:rows, :]
    send[...] = part[rows:, :].astype(LOW)


def join_kernel(keep, near, far, out):
    out[...] = (keep[...] + near[...].astype(FULL) + far[...].astype(FULL)).astype(LOW)


def grad_w_kernel(*refs):
    *parts, out = refs
    lefts, rights = parts[:-2], parts[-2:]

    def whole(parts):
        return jnp.concatenate([part[...] for part in parts], axis=0)

    out[0] = dot_tn(whole(lefts), whole(rights))


def result_kernel(middle, spread, back, out):
    out[...] = (middle[...] + dot(spread[...], back[...])).astype(LOW)


def back_kernel(gain_row, middle, cot, spread, back, small, grad_middle, grad_low, grad_gain):
    grad_two = dot(spread[...], back[...])
    values = middle[...]
    root = root_of(values)
    normed = values * root
    scaled = grad_two * small[gain_row : gain_row + 1, :]
    grad_gain[...] = jnp.sum(grad_two * normed, axis=0, keepdims=True)
    total = cot[...].astype(FULL) + root * (
        scaled - normed * jnp.mean(scaled * normed, axis=1, keepdims=True)
    )
    grad_middle[...] = total
    grad_low[...] = total.astype(LOW)


def attend_back_kernel(
    experts,
    own,
    far,
    near,
    near_far,
    ones,
    qkv,
    attended,
    probs,
    weights,
    group,
    router_one,
    router_two,
    gain_two,
    keep,
    keep_far,
    send,
    send_far,
    grad_w,
    payload,
    grads,
    joined,
):
    rows = own.shape[0]
    local = attended.shape[1]
    joined[0:rows, :] = own[...]
    joined[rows : 2 * rows, :] = far[...]
    joined[2 * rows : 3 * rows, :] = near[...]
    joined[3 * rows :, :] = near_far[...]
    w_out_t = weights[:, 3 * local :]
    grad_attended = dot(joined[...], w_out_t).astype(LOW)
    for h in range(local // HEAD_DIM):
        at = h * HEAD_DIM
        q = qkv[:, at : at + HEAD_DIM]
        k = qkv[:, local + at : local + at + HEAD_DIM]
        v = qkv[:, 2 * local + at : 2 * local + at + HEAD_DIM]
        upstream = grad_attended[:, at : at + HEAD_DIM]
        grad_p = dot_nt(upstream, v)
        p = probs[h]
        inner = jnp.sum(p * grad_p, axis=1, keepdims=True)
        grad_s = (p * (grad_p - inner)).astype(LOW)
        grads[:, at : at + HEAD_DIM] = (dot(grad_s, k) * SCALE).astype(LOW)
        grads[:, local + at : local + at + HEAD_DIM] = (dot_tn(grad_s, q) * SCALE).astype(LOW)
        grads[:, 2 * local + at : 2 * local + at + HEAD_DIM] = dot_tn(
            p.astype(LOW), upstream
        ).astype(LOW)
    grad_w[:, 3 * local :] = dot_tn(joined[...], attended[...]).astype(LOW)
    grad_w[:, 0 : 3 * local] = dot_tn(ones[...], grads[...]).astype(LOW)
    w_qkv = weights[:, 0 : 3 * local]

    def normed(values):
        values = values.astype(FULL)
        return values * root_of(values)

    gain_one = None
    for index, out in enumerate((keep, keep_far, send, send_far)):
        part = dot_nt(grads[index * rows : (index + 1) * rows, :], w_qkv)
        out[...] = part.astype(out.dtype)
        if index == 0:
            out.flush()
        gain = jnp.sum(
            part * normed(group[index * rows : (index + 1) * rows, :]), axis=0, keepdims=True
        )
        gain_one = gain if gain_one is None else gain_one + gain
    owners, height, shard = payload.shape
    whole = jnp.concatenate(
        [
            router_one[...] + router_two[...],
            gain_one,
            gain_two[...],
            jnp.zeros((height - experts - 2, gain_one.shape[1]), FULL),
        ],
        axis=0,
    )
    for d in range(owners):
        payload[d] = whole[:, d * shard : (d + 1) * shard]


def last_kernel(gain_row, tokens, keep, near, far, grad_middle, small, grad_tokens):
    rows = tokens.shape[0]
    values = tokens[...].astype(FULL)
    root = root_of(values)
    normed = values * root
    grad_one = keep[...] + near[...].astype(FULL) + far[...].astype(FULL)
    scaled = grad_one * small[gain_row : gain_row + 1, :]
    grad_tokens[...] = grad_middle[...] + root * (
        scaled - normed * jnp.mean(scaled * normed, axis=1, keepdims=True)
    )


def ring_rows(count, shard, scalars, offset):
    source = ring_source(ring_place(scalars[0], count) + offset, count)
    return pl.multiple_of(source * shard, 16)


def ring_first_kernel(count, scalars, grad_w, top, bottom):
    middle = top.shape[0]
    rest = bottom.shape[0]
    start = ring_rows(count, middle + rest, scalars, count // 2)
    top[...] = grad_w[pl.ds(start, middle), :]
    bottom[...] = grad_w[pl.ds(pl.multiple_of(start + middle, 16), rest), :]


def ring_add_kernel(count, step, scalars, grad_w, ahead, behind, to_right, to_left):
    shard = to_right.shape[0]
    right = ring_rows(count, shard, scalars, step)
    left = ring_rows(count, shard, scalars, -step)
    if ahead.shape[0] == shard:
        to_right[...] = (
            grad_w[pl.ds(right, shard), :].astype(FULL) + ahead[...].astype(FULL)
        ).astype(LOW)
        to_left[...] = (
            grad_w[pl.ds(left, shard), :].astype(FULL) + behind[...].astype(FULL)
        ).astype(LOW)
        return
    middle = ahead.shape[0]
    rest = shard - middle
    to_right[0:middle, :] = (
        grad_w[pl.ds(right, middle), :].astype(FULL) + ahead[...].astype(FULL)
    ).astype(LOW)
    to_right[middle:, :] = grad_w[pl.ds(pl.multiple_of(right + middle, 16), rest), :]
    to_left[0:middle, :] = grad_w[pl.ds(left, middle), :]
    to_left[middle:, :] = (
        grad_w[pl.ds(pl.multiple_of(left + middle, 16), rest), :].astype(FULL)
        + behind[...].astype(FULL)
    ).astype(LOW)


def write_sums(total, query, key, value, out):
    local = query.shape[1]
    query[...] = total[:, 0:local]
    key[...] = total[:, local : 2 * local]
    value[...] = total[:, 2 * local : 3 * local]
    out[...] = total[:, 3 * local :].T


def ring_last_kernel(count, scalars, grad_w, ahead, behind, query, key, value, out):
    shard = ahead.shape[0]
    start = pl.multiple_of(scalars[0] * shard, 16)
    total = grad_w[pl.ds(start, shard), :].astype(FULL) + (
        ahead[...].astype(FULL) + behind[...].astype(FULL)
    )
    write_sums(total, query, key, value, out)


def sum_kernel(blocks, query, key, value, out):
    total = blocks[0].astype(FULL)
    for d in range(1, blocks.shape[0]):
        total = total + blocks[d].astype(FULL)
    write_sums(total, query, key, value, out)


def on_device(
    tokens,
    lengths,
    routes,
    norm_attn,
    w_query,
    w_key,
    w_value,
    w_attn_out,
    norm_moe,
    w_router,
    w_expert_in,
    w_expert_out,
    cotangent,
):
    owners = lax.axis_size("dp")
    expert_index = lax.axis_index("dp")
    piece_index = lax.axis_index("tensor")
    piece_rows, width = tokens.shape
    shard, local = w_query.shape
    experts = w_router.shape[1]
    capacity = 3 * piece_rows // (2 * experts)
    slots = experts * capacity
    heads = local // HEAD_DIM
    total_rows = 4 * piece_rows
    small_rows = -(-(experts + 2) // 16) * 16
    scalars = jnp.concatenate(
        [jnp.stack([expert_index, piece_index]).astype(jnp.int32), lengths[0]]
    )
    sequences = lengths.shape[1]

    (packed,) = kernel_call(
        pack_kernel, [((shard + small_rows, 4 * local), LOW)], "pack", fetch=range(7)
    )(
        w_query,
        w_key,
        w_value,
        w_attn_out,
        w_router.T,
        norm_attn.reshape(1, shard),
        norm_moe.reshape(1, shard),
    )
    has_blocks = shard % 16 == 0
    scratch = []
    if has_blocks:
        behind, ahead, top, bottom = ring_gather(packed)
        partial = kernel_call(
            functools.partial(assemble_kernel, owners),
            [((width, 4 * local), LOW), ((owners, small_rows, shard), FULL)],
            "assemble",
            smem=(0,),
        )(scalars, packed, *behind, *ahead)
        blocks = [*partial, top, bottom]
        early = behind[0]
        scratch = [pltpu.VMEM((owners, small_rows, shard), FULL)]
    else:
        gathered = lax.all_gather(packed, "dp", axis=0, tiled=False)
        flat = gathered[:, shard:, :shard].transpose(1, 0, 2).reshape(small_rows, width)
        blocks = [gathered[:, :shard].reshape(width, 4 * local), flat.astype(FULL)]
        early = packed
    token_far = swap_far(after(tokens, early))
    token_near = swap_near(after(tokens, early))

    spread, cot_rows = kernel_call(
        functools.partial(spread_kernel, capacity, slots),
        [((piece_rows, slots), LOW), ((slots, width), LOW)],
        "spread",
        smem=(0,),
        fetch=(1, 2),
        store=(0, 1),
        time=2,
    )(scalars, routes, after(cotangent, early))
    token_near_far = swap_near(after(token_far, spread))

    cot_own = exchange(after(cot_rows, blocks[0]).reshape(experts, capacity, width))
    cot_own = cot_own.reshape(slots, width)

    outs = [
        ((piece_rows, width), FULL),
        ((piece_rows, width), FULL),
        ((piece_rows, width), LOW),
        ((piece_rows, width), LOW),
        ((total_rows, width), LOW),
        ((total_rows, 3 * local), LOW),
        ((total_rows, local), LOW),
        ((heads, total_rows, total_rows), FULL),
        ((total_rows, width), LOW),
    ]
    if has_blocks:
        outs += [((width, 4 * local), LOW), ((small_rows, width), FULL)]
    made = kernel_call(
        functools.partial(attend_kernel, owners, sequences, has_blocks),
        outs,
        "attend",
        smem=(0,),
        fetch=(1,),
        scratch=scratch,
        time=4,
    )(scalars, tokens, token_far, token_near, token_near_far, *blocks)
    keep, keep_far, send, send_far = made[:4]
    weights, small = made[9:] if has_blocks else blocks

    def scatter(keep_far, send, send_far, *others):
        near_far = swap_near(send_far)
        near = swap_near(send)
        (out,) = kernel_call(far_kernel, [(keep_far.shape, LOW)], "far")(
            keep_far, after(near_far, *others)
        )
        return near, swap_far(out), out

    near, far, mark = scatter(keep_far, send, send_far, cot_own)
    ones, qkv, attended, probs, group, weights_kept, small_kept = save(
        after(made[4], mark), *made[5:9], weights, small
    )
    tokens_here, spread_here = load(after(tokens, mark), spread)
    middle, own_rows = kernel_call(
        functools.partial(middle_kernel, experts + 1),
        [((piece_rows, width), FULL), ((slots, width), LOW)],
        "middle",
    )(tokens_here, keep, near, after(far, ones, spread_here), small, spread_here)
    (middle_kept,) = save(after(middle, own_rows))

    def over_dp(rows):
        return exchange(rows.reshape(experts, capacity, width)).reshape(slots, width)

    own = over_dp(own_rows)
    cot_far = swap_far(after(cot_own, own_rows))
    cot_near = swap_near(cot_own)
    cot_near_far = swap_near(cot_far)
    own_far = swap_far(after(own, cot_near_far))
    own_near = swap_near(own)
    weight_in = w_expert_in[0]
    weight_out = w_expert_out[0]
    hidden_size = weight_in.shape[1]

    def expert_part(x_keep, x_send, cot_keep, cot_send):
        rows = 2 * slots
        return kernel_call(
            functools.partial(expert_kernel, experts),
            [
                ((slots, width), FULL),
                ((slots, width), LOW),
                ((rows, hidden_size), LOW),
                ((rows, hidden_size), LOW),
                ((rows, width), LOW),
                ((rows, 1), FULL),
                ((experts, width), FULL),
                ((rows, width), LOW),
            ],
            "expert",
            smem=(0,),
            time=4,
            scratch=[pltpu.VMEM((rows, width), LOW)],
        )(scalars, x_keep, x_send, cot_keep, cot_send, weight_in, weight_out, small)

    small = small_kept
    keep, send, active_one, hidden_one, buffer_one, gate_one, router_one, rows_one = expert_part(
        own, own_near, cot_own, cot_near
    )
    keep_far, send_far, active_two, hidden_two, buffer_two, gate_two, router_two, rows_two = (
        expert_part(own_far, swap_near(after(own_far, send)), cot_far, cot_near_far)
    )
    near, far, mark = scatter(keep_far, send, send_far)
    forward_keep, forward_send, forward_keep_far, forward_send_far = kernel_call(
        forward_kernel,
        [((slots, width), kind) for kind in (FULL, LOW, FULL, LOW)],
        "forward",
        time=2,
    )(active_one, gate_one, active_two, gate_two, after(weight_out, mark))
    (grad_expert_out,) = kernel_call(
        grad_w_kernel, [((1, *weight_out.shape), FULL)], "grad_out", store=(0,), time=3
    )(active_one, active_two, after(buffer_one, forward_send), buffer_two)
    (back_rows,) = kernel_call(join_kernel, [((slots, width), LOW)], "join")(
        keep, near, after(far, grad_expert_out)
    )
    back = over_dp(back_rows)
    out_near, out_far, out_mark = scatter(
        forward_keep_far, forward_send, after(forward_send_far, back_rows)
    )
    (grad_expert_in,) = kernel_call(
        grad_w_kernel, [((1, *weight_in.shape), FULL)], "grad_in", store=(0,), time=3
    )(rows_one, rows_two, after(hidden_one, out_mark), hidden_two)
    middle_here, cot_here, spread_here, small_here = load(
        after(middle_kept, out_mark), cotangent, spread, small_kept
    )
    (out_rows,) = kernel_call(join_kernel, [((slots, width), LOW)], "join")(
        forward_keep, out_near, out_far
    )

    grad_middle, grad_low, grad_gain_two = kernel_call(
        functools.partial(back_kernel, experts + 1),
        [((piece_rows, width), FULL), ((piece_rows, width), LOW), ((1, width), FULL)],
        "back",
    )(middle_here, cot_here, spread_here, after(back, grad_expert_in), small_here)
    grad_far = swap_far(grad_low)
    grad_near = swap_near(grad_low)
    out_back = over_dp(after(out_rows, grad_near))
    (grad_middle_kept,) = save(after(grad_middle, grad_low))
    here = load(
        *(after(ones, grad_low), qkv, attended, probs, weights_kept, group)
    )
    grad_near_far = swap_near(grad_far)
    keep, keep_far, send, send_far, grad_w, payload = kernel_call(
        functools.partial(attend_back_kernel, experts),
        [
            ((piece_rows, width), FULL),
            ((piece_rows, width), FULL),
            ((piece_rows, width), LOW),
            ((piece_rows, width), LOW),
            ((width, 4 * local), LOW),
            ((owners, small_rows, shard), FULL),
        ],
        "attend_back",
        store=(0,),
        time=5,
        scratch=[pltpu.VMEM((total_rows, 3 * local), LOW), pltpu.VMEM((total_rows, width), LOW)],
    )(
        grad_low,
        grad_far,
        grad_near,
        grad_near_far,
        *here,
        router_one,
        router_two,
        grad_gain_two,
    )
    last = [((shard, local), FULL)] * 3 + [((local, shard), FULL)]
    near, far, mark = scatter(keep_far, send, send_far)
    marks = [mark] * 4
    if has_blocks:
        ahead, behind, marks = ring_reduce(grad_w, scalars, (shard, 4 * local))
        grad_query, grad_key, grad_value, grad_out = kernel_call(
            functools.partial(ring_last_kernel, owners),
            last,
            "ring_last",
            smem=(0,),
            store=range(4),
        )(scalars, grad_w, ahead, behind)
    else:
        grad_query, grad_key, grad_value, grad_out = kernel_call(
            sum_kernel, last, "sum", store=range(4)
        )(exchange(grad_w.reshape(owners, shard, 4 * local)))
    payload = payload + swap(payload, "tensor", 1)
    payload = payload + swap(payload, "tensor", 2)
    sums = jnp.sum(after(exchange(after(payload, marks[1], out_back)), marks[2]), axis=0)
    (grad_tokens,) = kernel_call(
        functools.partial(last_kernel, experts),
        [((piece_rows, width), FULL)],
        "last",
        fetch=(0, 1, 4, 5),
        store=(0,),
    )(tokens, keep, near, far, after(grad_middle_kept, marks[3]), small_kept)
    (result,) = kernel_call(
        result_kernel, [((piece_rows, width), LOW)], "result", fetch=(0, 1), store=(0,)
    )(after(middle_kept, marks[3]), spread, out_back)
    return (
        result,
        grad_tokens,
        sums[experts],
        grad_query,
        grad_key,
        grad_value,
        grad_out,
        sums[experts + 1],
        sums[:experts].T,
        grad_expert_in,
        grad_expert_out,
    )


def solution(mesh):
    return jax.shard_map(
        on_device,
        mesh=mesh,
        in_specs=(
            P(("dp", "tensor"), None),
            P("dp", None),
            P("dp", None),
            P("dp"),
            P("dp", "tensor"),
            P("dp", "tensor"),
            P("dp", "tensor"),
            P("tensor", "dp"),
            P("dp"),
            P("dp", None),
            P("dp", None, "tensor"),
            P("dp", "tensor", None),
            P(("dp", "tensor"), None),
        ),
        out_specs=(
            P(("dp", "tensor"), None),
            P(("dp", "tensor"), None),
            P("dp"),
            P("dp", "tensor"),
            P("dp", "tensor"),
            P("dp", "tensor"),
            P("tensor", "dp"),
            P("dp"),
            P("dp", None),
            P("dp", None, "tensor"),
            P("dp", "tensor", None),
        ),
        check_vma=False,
    )
```

time: 267 us -> 166 us (0.62)
  Pallas kernels: 0 us -> 49.5 us
  matrix products: 46.9 us -> 0 us
  local copies, waits for them, and re-layouts: 46 us -> 14.2 us
  waiting for transfers between devices: 69.5 us -> 39.9 us
  other arithmetic: 29.3 us -> 0.74 us
  between operations: 20.1 us -> 1.49 us
  starting transfers between devices: 53 us -> 59.4 us
    pallas_call x0 -> x31, Pallas kernels: none -> 49.5 us  [the longest x25 39.7 us: call(): pl.pallas_call(kernel, out_shape=[pltpu.HBM(*outs[i]) if i in store else...]
    dot_general x25 -> x0, matrix products: 42.8 us -> none  [the longest x7 16.7 us: dot_tn(): lax.dot_general(a, b, (((0,), (0,)), ((), ())), preferred_element_type=FULL)]
    all_to_all x7 -> x5, waiting for transfers between devices: 32.6 us -> 7.45 us  [exchange(): return lax.all_to_all(buffer, 'dp', split_axis=0, concat_axis=0, tiled=True)]
    dynamic_update_slice x14 -> x0, local copies, waits for them, and re-layouts: 15.3 us -> none  [the longest x8 11.5 us: put(): lax.dynamic_update_index_in_dim(two, rows[split:], source, 0)]
    ppermute x20 -> x26, waiting for transfers between devices: 33.8 us -> 23.4 us  [swap(): return lax.ppermute(values, axis, [(i, i ^ bit) for i in range(count)])]
    ppermute x8 -> x16, starting transfers between devices: 9.27 us -> 17.7 us  [the longest x3 6.15 us: ring_gather(): ahead.append(lax.ppermute(ahead[-1], 'dp', left))]
    concatenate x8 -> x1, other arithmetic: 7.76 us -> 0.08 us  [on_device(): jnp.concatenate([jnp.stack([expert_index, piece_index]).astype(jnp.int32)...]
    ppermute x8 -> x16, waiting for transfers between devices: 3.1 us -> 9.14 us  [the longest x3 5.71 us: ring_gather(): ahead.append(lax.ppermute(ahead[-1], 'dp', left))]
  transfers between devices with their start and end apart: 35 -> 47, of which waited for: 18 -> 19; matrix products, arithmetic and copies ran while one was open for 34% -> 2% of each run, Pallas kernels for 0% -> 25%
where the time goes in v2:
time: 166 us; the launch traced here: 165 us
  starting transfers between devices  59.4 us (36%)
  Pallas kernels  49.5 us (30%)
  waiting for transfers between devices  39.9 us (24%)
  local copies, waits for them, and re-layouts  14.2 us (9%)
    pallas_call x25, Pallas kernels, call(): pl.pallas_call(kernel, out_shape=[pltpu.HBM(*outs[i]) if i in store else...  39.7 us
    all_to_all x5, starting transfers between devices, exchange(): return lax.all_to_all(buffer, 'dp', split_axis=0, concat_axis=0, tiled=True)  27 us
    ppermute x26, waiting for transfers between devices, swap(): return lax.ppermute(values, axis, [(i, i ^ bit) for i in range(count)])  23.4 us
    ppermute x26, starting transfers between devices, swap(): return lax.ppermute(values, axis, [(i, i ^ bit) for i in range(count)])  14.7 us
    unnamed x73, local copies, waits for them, and re-layouts  13 us
    pallas_call x6, Pallas kernels, moved(): pl.pallas_call(move_kernel, out_shape=[pltpu.HBM(*kind) if target is pltp...  9.79 us
    all_to_all x5, waiting for transfers between devices, exchange(): return lax.all_to_all(buffer, 'dp', split_axis=0, concat_axis=0, tiled=True)  7.45 us
    ppermute x3, starting transfers between devices, ring_gather(): ahead.append(lax.ppermute(ahead[-1], 'dp', left))  6.15 us
  transfers between devices with their start and end apart: 47, of which 19 were waited for; matrix products, arithmetic and copies ran while one was open for 2% of the time, Pallas kernels for 25%

profile of v2, /device:TPU:0, one launch (start us, length us, event | category | flops | bytes accessed | tf_op | source)
XLA Modules:
  0.0 165.1 jit_solution(7103186239881434367)
XLA Ops:
  1.9 3.0 %collective-permute-start.6 = (bf16[112,768]{1,0:T(8,128)(2,1)S(1)}, bf16[112,768]{1,0:T(8,128)(2,1)S(1)}, u32[]{:S(2)}, u32[]{:S(2)}) collective-permute-start(bf16[112,768]{1,0:T(8,128)(2,1)S(1)} %pack.1.refs_1_), channel_id=1, source_target_pairs={{8,0},{16,8},{24,16},{28,24},{20,28},{12,20},{4,12},{0,4},{9,1},{1... | collective-permute-start | bytes 516104 | tf_op jit(solution)/shard_map/ppermute | solution.py:202
  5.0 4.3 %collective-permute-done.6.refs_5_ = bf16[112,768]{1,0:T(8,128)(2,1)S(1)} collective-permute-done((bf16[112,768]{1,0:T(8,128)(2,1)S(1)}, bf16[112,768]{1,0:T(8,128)(2,1)S(1)}, u32[]{:S(2)}, u32[]{:S(2)}) %collective-permute-start.6) | collective-permute-done | bytes 172064 | tf_op jit(solution)/shard_map/ppermute | solution.py:202
  16.9 2.9 %spread.1 = (bf16[128,192]{1,0:T(8,128)(2,1)}, bf16[192,768]{1,0:T(8,128)(2,1)}) custom-call(s32[5]{0:T(128)S(1)} %pad_add_fusion.refs_0_, s32[512,1]{1,0:T(8,128)} %copy.24.refs_1_, bf16[128,768]{1,0:T(8,128)(2,1)} %refs_1_.6), custom_call_target="tpu_custom_call" | custom-call | flops 2200000000 | bytes 1048576 | tf_op jit(solution)/shard_map/spread/pallas_call | solution.py:104
  24.3 5.8 %all-to-all-start = ((bf16[8,24,768]{2,1,0:T(8,128)(2,1)}), bf16[8,24,768]{2,1,0:T(8,128)(2,1)S(1)}, u32[]{:S(2)}, u32[]{:S(2)}) async-start(bf16[8,24,768]{2,1,0:T(8,128)(2,1)} %bitcast.6), calls=%async_computation | async-start | bytes 589824 | tf_op jit(solution)/shard_map/all_to_all | solution.py:171
  31.4 4.6 %attend.1 = (f32[128,768]{1,0:T(8,128)S(1)}, f32[128,768]{1,0:T(8,128)S(1)}, bf16[128,768]{1,0:T(8,128)(2,1)S(1)}, bf16[128,768]{1,0:T(8,128)(2,1)S(1)}, bf16[51...) custom-call(s32[5]{0:T(128)S(1)} %pad_add_fusion.refs_0_, ...), custom_call_target="tpu_custom_call" | custom-call | flops 4400000000 | bytes 1048576 | tf_op jit(solution)/shard_map/attend/pallas_call | solution.py:104
  46.1 2.9 %save.3 = (bf16[512,768]{1,0:T(8,128)(2,1)}, bf16[512,576]{1,0:T(8,128)(2,1)}, bf16[512,192]{1,0:T(8,128)(2,1)}, f32[3,512,512]{2,1,0:T(8,128)}, bf16[512,768]{1...) custom-call(bf16[512,768]{1,0:T(8,128)(2,1)S(1)} %copy-done.5, bf16[512,576]{1,0:T(8,128)(2,1)S(1)} %copy-done.9, ...), custom_call_target="tpu_custom_call" | custom-call | flops 2000000000 | bytes 1048576 | tf_op jit(solution)/shard_map/save/pallas_call | solution.py:142
  52.4 6.0 %all-to-all-start.1 = ((bf16[8,24,768]{2,1,0:T(8,128)(2,1)}), bf16[8,24,768]{2,1,0:T(8,128)(2,1)S(1)}, u32[]{:S(2)}, u32[]{:S(2)}) async-start(bf16[8,24,768]{2,1,0:T(8,128)(2,1)} %bitcast.8), calls=%async_computation.1 | async-start | bytes 589824 | tf_op jit(solution)/shard_map/all_to_all | solution.py:171
  59.7 6.6 %collective-permute-done.16.refs_3_ = bf16[192,768]{1,0:T(8,128)(2,1)S(1)} collective-permute-done((bf16[192,768]{1,0:T(8,128)(2,1)S(1)}, bf16[192,768]{1,0:T(8,128)(2,1)S(1)}, u32[]{:S(2)}, u32[]{:S(2)}) %collective-permute-start.16) | collective-permute-done | bytes 294944 | tf_op jit(solution)/shard_map/ppermute | solution.py:167
  70.5 4.0 %expert.2 = (f32[192,768]{1,0:T(8,128)S(1)}, bf16[192,768]{1,0:T(8,128)(2,1)S(1)}, bf16[384,768]{1,0:T(8,128)(2,1)S(1)}, bf16[384,768]{1,0:T(8,128)(2,1)S(1)}, b...) custom-call(s32[5]{0:T(128)S(1)} %pad_add_fusion.refs_0_, ...), custom_call_target="tpu_custom_call" | custom-call | flops 4400000000 | bytes 1048576 | tf_op jit(solution)/shard_map/expert/pallas_call | solution.py:104
  79.0 3.6 %expert.3 = (f32[192,768]{1,0:T(8,128)S(1)}, bf16[192,768]{1,0:T(8,128)(2,1)S(1)}, bf16[384,768]{1,0:T(8,128)(2,1)S(1)}, bf16[384,768]{1,0:T(8,128)(2,1)S(1)}, b...) custom-call(s32[5]{0:T(128)S(1)} %pad_add_fusion.refs_0_, ...), custom_call_target="tpu_custom_call" | custom-call | flops 4400000000 | bytes 1048576 | tf_op jit(solution)/shard_map/expert/pallas_call | solution.py:104
  86.8 2.5 %grad_out.1 = f32[1,768,768]{2,1,0:T(8,128)} custom-call(bf16[384,768]{1,0:T(8,128)(2,1)S(1)} %get-tuple-element.143.refs_0_, bf16[384,768]{1,0:T(8,128)(2,1)S(1)} %get-tuple-element.149.refs_2_.refs_1_, bf16[384,768]{1,0:T(8,128)(2,1)S(1)} %get-tuple-element.159.refs_2_, bf16[384,768]{1,0:T(8,128)(2,1)S(1)} %get-tuple-element.160.refs_3_), custom_call_target="tpu_custom_call" | custom-call | flops 3300000000 | bytes 1048576 | tf_op jit(solution)/shard_map/grad_out/pallas_call | solution.py:104
  89.4 4.1 %collective-permute-done.22.refs_2_ = bf16[192,768]{1,0:T(8,128)(2,1)S(1)} collective-permute-done((bf16[192,768]{1,0:T(8,128)(2,1)S(1)}, bf16[192,768]{1,0:T(8,128)(2,1)S(1)}, u32[]{:S(2)}, u32[]{:S(2)}) %collective-permute-start.22) | collective-permute-done | bytes 294944 | tf_op jit(solution)/shard_map/ppermute | solution.py:167
  95.2 5.7 %all-to-all-start.2 = ((bf16[8,24,768]{2,1,0:T(8,128)(2,1)}), bf16[8,24,768]{2,1,0:T(8,128)(2,1)S(1)}, u32[]{:S(2)}, u32[]{:S(2)}) async-start(bf16[8,24,768]{2,1,0:T(8,128)(2,1)} %bitcast.12), calls=%async_computation.2 | async-start | bytes 589824 | tf_op jit(solution)/shard_map/all_to_all | solution.py:171
  102.9 2.5 %grad_in.1 = f32[1,768,768]{2,1,0:T(8,128)} custom-call(bf16[384,768]{1,0:T(8,128)(2,1)S(1)} %copy-done.24, bf16[384,768]{1,0:T(8,128)(2,1)S(1)} %copy-done.28, bf16[384,768]{1,0:T(8,128)(2,1)S(1)} %copy-done.22, bf16[384,768]{1,0:T(8,128)(2,1)S(1)} %copy-done.26), custom_call_target="tpu_custom_call" | custom-call | flops 3300000000 | bytes 1048576 | tf_op jit(solution)/shard_map/grad_in/pallas_call | solution.py:104
  105.4 5.6 %all-to-all-done.2 = bf16[8,24,768]{2,1,0:T(8,128)(2,1)S(1)} async-done(((bf16[8,24,768]{2,1,0:T(8,128)(2,1)}), bf16[8,24,768]{2,1,0:T(8,128)(2,1)S(1)}, u32[]{:S(2)}, u32[]{:S(2)}) %all-to-all-start.2) | async-done | bytes 294944 | tf_op jit(solution)/shard_map/all_to_all | solution.py:171
  112.8 4.4 %collective-permute-done.24.refs_1_ = bf16[128,768]{1,0:T(8,128)(2,1)S(1)} collective-permute-done((bf16[128,768]{1,0:T(8,128)(2,1)S(1)}, bf16[128,768]{1,0:T(8,128)(2,1)S(1)}, u32[]{:S(2)}, u32[]{:S(2)}) %collective-permute-start.24) | collective-permute-done | bytes 196640 | tf_op jit(solution)/shard_map/ppermute | solution.py:167
  119.0 3.0 %load.5 = (bf16[512,768]{1,0:T(8,128)(2,1)S(1)}, bf16[512,576]{1,0:T(8,128)(2,1)S(1)}, bf16[512,192]{1,0:T(8,128)(2,1)S(1)}, f32[3,512,512]{2,1,0:T(8,128)S(1)},...) custom-call(bf16[512,768]{1,0:T(8,128)(2,1)} %get-tuple-element.175.refs_0_, ...), custom_call_target="tpu_custom_call" | custom-call | flops 2000000000 | bytes 1048576 | tf_op jit(solution)/shard_map/load/pallas_call | solution.py:142
  122.0 5.4 %attend_back.1 = (f32[128,768]{1,0:T(8,128)}, f32[128,768]{1,0:T(8,128)S(1)}, bf16[128,768]{1,0:T(8,128)(2,1)S(1)}, bf16[128,768]{1,0:T(8,128)(2,1)S(1)}, bf16[7...) custom-call(bf16[128,768]{1,0:T(8,128)(2,1)S(1)} %get-tuple-element.174.refs_0_, ...), custom_call_target="tpu_custom_call" | custom-call | flops 5500000256 | bytes 1048576 | tf_op jit(solution)/shard_map/attend_back/pallas_call | solution.py:104
  130.2 2.3 %collective-permute-done.27.refs_2_ = bf16[48,768]{1,0:T(8,128)(2,1)S(1)} collective-permute-done((bf16[48,768]{1,0:T(8,128)(2,1)S(1)}, bf16[48,768]{1,0:T(8,128)(2,1)S(1)}, u32[]{:S(2)}, u32[]{:S(2)}) %collective-permute-start.27) | collective-permute-done | bytes 73760 | tf_op jit(solution)/shard_map/ppermute | solution.py:224
  137.1 4.3 %all-to-all-start.3 = ((bf16[8,24,768]{2,1,0:T(8,128)(2,1)}), bf16[8,24,768]{2,1,0:T(8,128)(2,1)S(1)}, u32[]{:S(2)}, u32[]{:S(2)}) async-start(bf16[8,24,768]{2,1,0:T(8,128)(2,1)} %bitcast.14), calls=%async_computation.3 | async-start | bytes 589824 | tf_op jit(solution)/shard_map/all_to_all | solution.py:171
  144.1 2.1 %collective-permute-start.32 = (bf16[96,768]{1,0:T(8,128)(2,1)S(1)}, bf16[96,768]{1,0:T(8,128)(2,1)S(1)}, u32[]{:S(2)}, u32[]{:S(2)}) collective-permute-start(bf16[96,768]{1,0:T(8,128)(2,1)S(1)} %get-tuple-element.196), channel_id=1, source_target_pairs={{8,0},{16,8},{24,16},{28,24},{20,28},{12,20},{4,12},{0,4},{9,1},{1... | collective-permute-start | bytes 442376 | tf_op jit(solution)/shard_map/ppermute | solution.py:236
  149.9 5.2 %all-to-all-start.4 = ((f32[8,16,96]{2,1,0:T(8,128)}), f32[8,16,96]{2,1,0:T(8,128)S(1)}, u32[]{:S(2)}, u32[]{:S(2)}) async-start(f32[8,16,96]{2,1,0:T(8,128)} %add.7), calls=%async_computation.4 | async-start | bytes 131072 | tf_op jit(solution)/shard_map/all_to_all | solution.py:171
  155.7 2.1 %collective-permute-start.40 = (bf16[96,768]{1,0:T(8,128)(2,1)S(1)}, bf16[96,768]{1,0:T(8,128)(2,1)S(1)}, u32[]{:S(2)}, u32[]{:S(2)}) collective-permute-start(bf16[96,768]{1,0:T(8,128)(2,1)S(1)} %get-tuple-element.197), channel_id=1, source_target_pairs={{0,8},{8,16},{16,24},{24,28},{28,20},{20,12},{12,4},{4,0},{1,9},{9... | collective-permute-start | bytes 442376 | tf_op jit(solution)/shard_map/ppermute | solution.py:235
  159.8 2.2 %last.1 = f32[128,768]{1,0:T(8,128)} custom-call(bf16[128,768]{1,0:T(8,128)(2,1)} %refs_0_.4, f32[128,768]{1,0:T(8,128)} %get-tuple-element.201.refs_1_, bf16[128,768]{1,0:T(8,128)(2,1)S(1)} %collective-permute-done.35.refs_2_, bf16[128,768]{1,0:T(8,128)(2,1)S(1)} %collective-permute-done.37.refs_3_, f32[128,768]{1,0:T(8,128)} %save.5.refs_4_, ...), custom_call_target="tpu_custom_call" | custom-call | flops 1100000000 | bytes 1048576 | tf_op jit(solution)/shard_map/last/pallas_call | solution.py:104
  (182 shorter events, 68.7 us)
Async XLA Ops:
  12.3 17.8 %collective-permute-start.2 = (bf16[128,768]{1,0:T(8,128)(2,1)S(1)}, bf16[128,768]{1,0:T(8,128)(2,1)S(1)}, u32[]{:S(2)}, u32[]{:S(2)}) collective-permute-start(bf16[128,768]{1,0:T(8,128)(2,1)S(1)} %copy-done.35), channel_id=1, source_target_pairs={{0,1},{1,0},{2,3},{3,2},{4,5},{5,4},{6,7},{7,6},{8,9},{9,8},{10,11... | collective-permute-start | bytes 589832 | tf_op jit(solution)/shard_map/ppermute | solution.py:167
  19.8 10.3 %collective-permute-start.3 = (bf16[128,768]{1,0:T(8,128)(2,1)S(1)}, bf16[128,768]{1,0:T(8,128)(2,1)S(1)}, u32[]{:S(2)}, u32[]{:S(2)}) collective-permute-start(bf16[128,768]{1,0:T(8,128)(2,1)S(1)} %collective-permute-done.1.refs_2_), channel_id=1, source_target_pairs={{0,1},{1,0},{2,3},{3,2},{4,5},{5,4},{6,7},{7,6},{8,9},{9,8},{10,11... | collective-permute-start | bytes 589832 | tf_op jit(solution)/shard_map/ppermute | solution.py:167
  20.5 9.6 %collective-permute-start.10 = (bf16[64,768]{1,0:T(8,128)(2,1)S(1)}, bf16[64,768]{1,0:T(8,128)(2,1)S(1)}, u32[]{:S(2)}, u32[]{:S(2)}) collective-permute-start(bf16[64,768]{1,0:T(8,128)(2,1)S(1)} %slice.21), channel_id=1, source_target_pairs={{8,0},{16,8},{24,16},{28,24},{20,28},{12,20},{4,12},{0,4},{9,1},{1... | collective-permute-start | bytes 294920 | tf_op jit(solution)/shard_map/ppermute | solution.py:205
  22.1 8.1 %collective-permute-start.9 = (bf16[48,768]{1,0:T(8,128)(2,1)S(1)}, bf16[48,768]{1,0:T(8,128)(2,1)S(1)}, u32[]{:S(2)}, u32[]{:S(2)}) collective-permute-start(bf16[48,768]{1,0:T(8,128)(2,1)S(1)} %slice.20), channel_id=1, source_target_pairs={{0,8},{8,16},{16,24},{24,28},{28,20},{20,12},{12,4},{4,0},{1,9},{9... | collective-permute-start | bytes 221192 | tf_op jit(solution)/shard_map/ppermute | solution.py:204
  24.3 18.1 %all-to-all-start = ((bf16[8,24,768]{2,1,0:T(8,128)(2,1)}), bf16[8,24,768]{2,1,0:T(8,128)(2,1)S(1)}, u32[]{:S(2)}, u32[]{:S(2)}) async-start(bf16[8,24,768]{2,1,0:T(8,128)(2,1)} %bitcast.6), calls=%async_computation | async-start | bytes 589824 | tf_op jit(solution)/shard_map/all_to_all | solution.py:171
  41.0 9.5 %collective-permute-start.12 = (bf16[128,768]{1,0:T(8,128)(2,1)S(1)}, bf16[128,768]{1,0:T(8,128)(2,1)S(1)}, u32[]{:S(2)}, u32[]{:S(2)}) collective-permute-start(bf16[128,768]{1,0:T(8,128)(2,1)S(1)} %get-tuple-element.128), channel_id=1, source_target_pairs={{0,1},{1,0},{2,3},{3,2},{4,5},{5,4},{6,7},{7,6},{8,9},{9,8},{10,11... | collective-permute-start | bytes 589832 | tf_op jit(solution)/shard_map/ppermute | solution.py:167
  52.4 15.0 %all-to-all-start.1 = ((bf16[8,24,768]{2,1,0:T(8,128)(2,1)}), bf16[8,24,768]{2,1,0:T(8,128)(2,1)S(1)}, u32[]{:S(2)}, u32[]{:S(2)}) async-start(bf16[8,24,768]{2,1,0:T(8,128)(2,1)} %bitcast.8), calls=%async_computation.1 | async-start | bytes 589824 | tf_op jit(solution)/shard_map/all_to_all | solution.py:171
  58.4 7.9 %collective-permute-start.16 = (bf16[192,768]{1,0:T(8,128)(2,1)S(1)}, bf16[192,768]{1,0:T(8,128)(2,1)S(1)}, u32[]{:S(2)}, u32[]{:S(2)}) collective-permute-start(bf16[192,768]{1,0:T(8,128)(2,1)S(1)} %bitcast.22), channel_id=1, source_target_pairs={{0,2},{1,3},{2,0},{3,1},{4,6},{5,7},{6,4},{7,5},{8,10},{9,11},{10,... | collective-permute-start | bytes 884744 | tf_op jit(solution)/shard_map/ppermute | solution.py:167
  68.3 9.1 %collective-permute-start.18 = (bf16[192,768]{1,0:T(8,128)(2,1)S(1)}, bf16[192,768]{1,0:T(8,128)(2,1)S(1)}, u32[]{:S(2)}, u32[]{:S(2)}) collective-permute-start(bf16[192,768]{1,0:T(8,128)(2,1)S(1)} %bitcast.27), channel_id=1, source_target_pairs={{0,2},{1,3},{2,0},{3,1},{4,6},{5,7},{6,4},{7,5},{8,10},{9,11},{10,... | collective-permute-start | bytes 884744 | tf_op jit(solution)/shard_map/ppermute | solution.py:167
  82.8 10.6 %collective-permute-start.21 = (bf16[192,768]{1,0:T(8,128)(2,1)S(1)}, bf16[192,768]{1,0:T(8,128)(2,1)S(1)}, u32[]{:S(2)}, u32[]{:S(2)}) collective-permute-start(bf16[192,768]{1,0:T(8,128)(2,1)S(1)} %get-tuple-element.147), channel_id=1, source_target_pairs={{0,1},{1,0},{2,3},{3,2},{4,5},{5,4},{6,7},{7,6},{8,9},{9,8},{10,11... | collective-permute-start | bytes 884744 | tf_op jit(solution)/shard_map/ppermute | solution.py:167
  84.3 9.1 %collective-permute-start.22 = (bf16[192,768]{1,0:T(8,128)(2,1)S(1)}, bf16[192,768]{1,0:T(8,128)(2,1)S(1)}, u32[]{:S(2)}, u32[]{:S(2)}) collective-permute-start(bf16[192,768]{1,0:T(8,128)(2,1)S(1)} %far.5), channel_id=1, source_target_pairs={{0,2},{1,3},{2,0},{3,1},{4,6},{5,7},{6,4},{7,5},{8,10},{9,11},{10,... | collective-permute-start | bytes 884744 | tf_op jit(solution)/shard_map/ppermute | solution.py:167
  95.2 15.8 %all-to-all-start.2 = ((bf16[8,24,768]{2,1,0:T(8,128)(2,1)}), bf16[8,24,768]{2,1,0:T(8,128)(2,1)S(1)}, u32[]{:S(2)}, u32[]{:S(2)}) async-start(bf16[8,24,768]{2,1,0:T(8,128)(2,1)} %bitcast.12), calls=%async_computation.2 | async-start | bytes 589824 | tf_op jit(solution)/shard_map/all_to_all | solution.py:171
  112.8 9.2 %collective-permute-start.25 = (bf16[128,768]{1,0:T(8,128)(2,1)S(1)}, bf16[128,768]{1,0:T(8,128)(2,1)S(1)}, u32[]{:S(2)}, u32[]{:S(2)}) collective-permute-start(bf16[128,768]{1,0:T(8,128)(2,1)S(1)} %get-tuple-element.174.refs_0_), channel_id=1, source_target_pairs={{0,1},{1,0},{2,3},{3,2},{4,5},{5,4},{6,7},{7,6},{8,9},{9,8},{10,11... | collective-permute-start | bytes 589832 | tf_op jit(solution)/shard_map/ppermute | solution.py:167
  117.1 19.1 %collective-permute-start.33 = (bf16[192,768]{1,0:T(8,128)(2,1)S(1)}, bf16[192,768]{1,0:T(8,128)(2,1)S(1)}, u32[]{:S(2)}, u32[]{:S(2)}) collective-permute-start(bf16[192,768]{1,0:T(8,128)(2,1)S(1)} %get-tuple-element.158), channel_id=1, source_target_pairs={{0,1},{1,0},{2,3},{3,2},{4,5},{5,4},{6,7},{7,6},{8,9},{9,8},{10,11... | collective-permute-start | bytes 884744 | tf_op jit(solution)/shard_map/ppermute | solution.py:167
  117.7 18.6 %collective-permute-start.34 = (bf16[192,768]{1,0:T(8,128)(2,1)S(1)}, bf16[192,768]{1,0:T(8,128)(2,1)S(1)}, u32[]{:S(2)}, u32[]{:S(2)}) collective-permute-start(bf16[192,768]{1,0:T(8,128)(2,1)S(1)} %far.6), channel_id=1, source_target_pairs={{0,2},{1,3},{2,0},{3,1},{4,6},{5,7},{6,4},{7,5},{8,10},{9,11},{10,... | collective-permute-start | bytes 884744 | tf_op jit(solution)/shard_map/ppermute | solution.py:167
  134.2 9.3 %collective-permute-start.30 = (bf16[96,768]{1,0:T(8,128)(2,1)S(1)}, bf16[96,768]{1,0:T(8,128)(2,1)S(1)}, u32[]{:S(2)}, u32[]{:S(2)}) collective-permute-start(bf16[96,768]{1,0:T(8,128)(2,1)S(1)} %get-tuple-element.194), channel_id=1, source_target_pairs={{8,0},{16,8},{24,16},{28,24},{20,28},{12,20},{4,12},{0,4},{9,1},{1... | collective-permute-start | bytes 442376 | tf_op jit(solution)/shard_map/ppermute | solution.py:236
  135.2 8.2 %collective-permute-start.29 = (bf16[96,768]{1,0:T(8,128)(2,1)S(1)}, bf16[96,768]{1,0:T(8,128)(2,1)S(1)}, u32[]{:S(2)}, u32[]{:S(2)}) collective-permute-start(bf16[96,768]{1,0:T(8,128)(2,1)S(1)} %get-tuple-element.193), channel_id=1, source_target_pairs={{0,8},{8,16},{16,24},{24,28},{28,20},{20,12},{12,4},{4,0},{1,9},{9... | collective-permute-start | bytes 442376 | tf_op jit(solution)/shard_map/ppermute | solution.py:235
  137.1 12.8 %all-to-all-start.3 = ((bf16[8,24,768]{2,1,0:T(8,128)(2,1)}), bf16[8,24,768]{2,1,0:T(8,128)(2,1)S(1)}, u32[]{:S(2)}, u32[]{:S(2)}) async-start(bf16[8,24,768]{2,1,0:T(8,128)(2,1)} %bitcast.14), calls=%async_computation.3 | async-start | bytes 589824 | tf_op jit(solution)/shard_map/all_to_all | solution.py:171
  144.1 11.0 %collective-permute-start.32 = (bf16[96,768]{1,0:T(8,128)(2,1)S(1)}, bf16[96,768]{1,0:T(8,128)(2,1)S(1)}, u32[]{:S(2)}, u32[]{:S(2)}) collective-permute-start(bf16[96,768]{1,0:T(8,128)(2,1)S(1)} %get-tuple-element.196), channel_id=1, source_target_pairs={{8,0},{16,8},{24,16},{28,24},{20,28},{12,20},{4,12},{0,4},{9,1},{1... | collective-permute-start | bytes 442376 | tf_op jit(solution)/shard_map/ppermute | solution.py:236
  146.1 8.9 %collective-permute-start.31 = (bf16[96,768]{1,0:T(8,128)(2,1)S(1)}, bf16[96,768]{1,0:T(8,128)(2,1)S(1)}, u32[]{:S(2)}, u32[]{:S(2)}) collective-permute-start(bf16[96,768]{1,0:T(8,128)(2,1)S(1)} %get-tuple-element.195), channel_id=1, source_target_pairs={{0,8},{8,16},{16,24},{24,28},{28,20},{20,12},{12,4},{4,0},{1,9},{9... | collective-permute-start | bytes 442376 | tf_op jit(solution)/shard_map/ppermute | solution.py:235
  147.0 12.8 %collective-permute-start.35 = (bf16[128,768]{1,0:T(8,128)(2,1)S(1)}, bf16[128,768]{1,0:T(8,128)(2,1)S(1)}, u32[]{:S(2)}, u32[]{:S(2)}) collective-permute-start(bf16[128,768]{1,0:T(8,128)(2,1)S(1)} %get-tuple-element.202), channel_id=1, source_target_pairs={{0,1},{1,0},{2,3},{3,2},{4,5},{5,4},{6,7},{7,6},{8,9},{9,8},{10,11... | collective-permute-start | bytes 589832 | tf_op jit(solution)/shard_map/ppermute | solution.py:167
  147.8 12.0 %collective-permute-start.37 = (bf16[128,768]{1,0:T(8,128)(2,1)S(1)}, bf16[128,768]{1,0:T(8,128)(2,1)S(1)}, u32[]{:S(2)}, u32[]{:S(2)}) collective-permute-start(bf16[128,768]{1,0:T(8,128)(2,1)S(1)} %far.7), channel_id=1, source_target_pairs={{0,2},{1,3},{2,0},{3,1},{4,6},{5,7},{6,4},{7,5},{8,10},{9,11},{10,... | collective-permute-start | bytes 589832 | tf_op jit(solution)/shard_map/ppermute | solution.py:167
  149.9 12.5 %all-to-all-start.4 = ((f32[8,16,96]{2,1,0:T(8,128)}), f32[8,16,96]{2,1,0:T(8,128)S(1)}, u32[]{:S(2)}, u32[]{:S(2)}) async-start(f32[8,16,96]{2,1,0:T(8,128)} %add.7), calls=%async_computation.4 | async-start | bytes 131072 | tf_op jit(solution)/shard_map/all_to_all | solution.py:171
  155.7 7.8 %collective-permute-start.40 = (bf16[96,768]{1,0:T(8,128)(2,1)S(1)}, bf16[96,768]{1,0:T(8,128)(2,1)S(1)}, u32[]{:S(2)}, u32[]{:S(2)}) collective-permute-start(bf16[96,768]{1,0:T(8,128)(2,1)S(1)} %get-tuple-element.197), channel_id=1, source_target_pairs={{0,8},{8,16},{16,24},{24,28},{28,20},{20,12},{12,4},{4,0},{1,9},{9... | collective-permute-start | bytes 442376 | tf_op jit(solution)/shard_map/ppermute | solution.py:235
  (59 other events, 236.9 us)

commit v3 on v2

--- a/solution.py
+++ b/solution.py
@@ -28,10 +28,6 @@
     return lax.dot_general(a, b, (((0,), (0,)), ((), ())), preferred_element_type=FULL)
 
 
-def after(value, *others):
-    return lax.optimization_barrier((value, *others))[0]
-
-
 class Fetched:
     def __init__(self, ref, held, sem):
         self.held, self.waiting = held, True
@@ -67,7 +63,7 @@
             self.copy.start()
 
 
-def kernel_call(body, outs, name, fetch=(), store=(), smem=(), time=1, limit=24, scratch=()):
+def kernel_call(body, outs, name, fetch=(), store=(), smem=(), time=1, limit=24, scratch=(), raw=(), alias=(), wait=(), wait_hbm=()):
     def call(*operands):
         n_in, n_out, n_scratch = len(operands), len(outs), len(scratch)
         held = [pltpu.VMEM(operands[i].shape, operands[i].dtype) for i in fetch]
@@ -75,8 +71,8 @@
         sems = [pltpu.SemaphoreType.DMA((len(held),))] if held else []
 
         def kernel(*refs):
-            ins, results = list(refs[:n_in]), list(refs[n_in : n_in + n_out])
-            rest = refs[n_in + n_out :]
+            ins, refs = list(refs[:n_in]), refs[n_in + len(wait) + len(wait_hbm) :]
+            results, rest = list(refs[:n_out]), refs[n_out:]
             own, buffers = rest[:n_scratch], rest[n_scratch : n_scratch + len(held)]
             sem = rest[-1] if held else None
             at = 0
@@ -97,6 +93,8 @@
         def spec(i, hbm):
             return pl.BlockSpec(memory_space=pltpu.HBM if i in hbm else pltpu.VMEM)
 
+        kept = (*store, *raw)
+
         operands = [
             pltpu.with_memory_space_constraint(x, pltpu.HBM) if i in fetch else x
             for i, x in enumerate(operands)
@@ -104,30 +102,37 @@
         return pl.pallas_call(
             kernel,
             out_shape=[
-                pltpu.HBM(*outs[i]) if i in store else jax.ShapeDtypeStruct(*outs[i])
+                pltpu.HBM(*outs[i]) if i in kept else jax.ShapeDtypeStruct(*outs[i])
                 for i in range(n_out)
             ],
             in_specs=[
                 pl.BlockSpec(memory_space=pltpu.SMEM) if i in smem else spec(i, fetch)
                 for i in range(n_in)
-            ],
-            out_specs=[spec(i, store) for i in range(n_out)],
+            ]
+            + [pl.BlockSpec(memory_space=pl.ANY) for _ in wait]
+            + [pl.BlockSpec(memory_space=pltpu.HBM) for _ in wait_hbm],
+            out_specs=[spec(i, kept) for i in range(n_out)],
+            input_output_aliases=dict(alias),
             scratch_shapes=[*scratch, *held, *sems],
             compiler_params=pltpu.CompilerParams(vmem_limit_bytes=limit * MIB),
             cost_estimate=pl.CostEstimate(
                 flops=int(time * 1.1e9), bytes_accessed=MIB, transcendentals=0
             ),
             name=name,
-        )(*operands)
+        )(
+            *operands,
+            *wait,
+            *(pltpu.with_memory_space_constraint(x, pltpu.HBM) for x in wait_hbm),
+        )
 
     return call
 
 
-def move_kernel(*refs):
-    count = len(refs) // 2
-    sem = refs[-1]
+def move_kernel(count, *refs):
+    sources, targets, sem = refs[:count], refs[-1 - count : -1], refs[-1]
     copies = [
-        pltpu.make_async_copy(refs[k], refs[count + k], sem.at[k]) for k in range(count)
+        pltpu.make_async_copy(source, target, sem.at[k])
+        for k, (source, target) in enumerate(zip(sources, targets))
     ]
     for copy in copies:
         copy.start()
@@ -135,31 +140,32 @@
         copy.wait()
 
 
-def moved(arrays, source, target, name):
+def moved(arrays, source, target, name, wait):
     kinds = [(x.shape, x.dtype) for x in arrays]
     if source is pltpu.HBM:
         arrays = [pltpu.with_memory_space_constraint(x, pltpu.HBM) for x in arrays]
     return pl.pallas_call(
-        move_kernel,
+        functools.partial(move_kernel, len(kinds)),
         out_shape=[
             pltpu.HBM(*kind) if target is pltpu.HBM else jax.ShapeDtypeStruct(*kind)
             for kind in kinds
         ],
-        in_specs=[pl.BlockSpec(memory_space=source) for _ in kinds],
+        in_specs=[pl.BlockSpec(memory_space=source) for _ in kinds]
+        + [pl.BlockSpec(memory_space=pl.ANY) for _ in wait],
         out_specs=[pl.BlockSpec(memory_space=target) for _ in kinds],
         scratch_shapes=[pltpu.SemaphoreType.DMA((len(kinds),))],
         compiler_params=pltpu.CompilerParams(vmem_limit_bytes=16 * MIB),
         cost_estimate=pl.CostEstimate(flops=2 * 10**9, bytes_accessed=MIB, transcendentals=0),
         name=name,
-    )(*arrays)
-
-
-def save(*arrays):
-    return moved(arrays, pltpu.VMEM, pltpu.HBM, "save")
-
-
-def load(*arrays):
-    return moved(arrays, pltpu.HBM, pltpu.VMEM, "load")
+    )(*arrays, *wait)
+
+
+def save(*arrays, wait=()):
+    return moved(arrays, pltpu.VMEM, pltpu.HBM, "save", wait)
+
+
+def load(*arrays, wait=()):
+    return moved(arrays, pltpu.HBM, pltpu.VMEM, "load", wait)
 
 
 def swap(values, axis, bit):
@@ -210,31 +216,48 @@
     return jnp.where(lax.rem(me, 2) == 0, me // 2, count - 1 - me // 2)
 
 
-def ring_reduce(grad_w, scalars, blocks_shape):
+def fence_kernel(source, out):
+    out[...] = source[0 : out.shape[0], 0 : out.shape[1]].astype(out.dtype)
+
+
+def fence(source, wait=()):
+    (out,) = kernel_call(fence_kernel, [((16, 128), LOW)], "fence", time=40, wait=wait)(source)
+    return out
+
+
+def add_kernel(*refs):
+    total = refs[0][...].astype(FULL)
+    for ref in refs[1:-1]:
+        total = total + ref[...].astype(FULL)
+    refs[-1][...] = total.astype(refs[-1].dtype)
+
+
+def add(*values, wait=()):
+    kind = (values[0].shape, values[0].dtype)
+    return kernel_call(add_kernel, [kind], "add", time=0.1, wait=wait)(*values)[0]
+
+
+def ring_reduce(top, bottom, rest, shard, fillers, arrived=()):
     count = lax.axis_size("dp")
     right, left = ring_perms(count)
-    shard, width = blocks_shape
-    middle = shard // 32 * 16
-    top, bottom = kernel_call(
-        functools.partial(ring_first_kernel, count),
-        [((middle, width), LOW), ((shard - middle, width), LOW)],
-        "ring_first",
-        smem=(0,),
-    )(scalars, grad_w)
+    width = rest.shape[1]
     ahead = lax.ppermute(top, "dp", right)
     behind = lax.ppermute(bottom, "dp", left)
-    marks = [top]
-    for step in range(count // 2 - 1, 0, -1):
-        ahead, behind = kernel_call(
-            functools.partial(ring_add_kernel, count, step),
-            [((shard, width), LOW), ((shard, width), LOW)],
+    done = ()
+    for index, step in enumerate(range(count // 2 - 1, -1, -1)):
+        if index < len(fillers):
+            done, arrived = fillers[index](fence(rest, arrived))
+        if not step:
+            return rest, ahead, behind
+        block = (shard, width)
+        to_right, to_left, rest = kernel_call(
+            ring_add_kernel,
+            [(block, LOW), (block, LOW), ((rest.shape[0] - 2 * shard, width), LOW)],
             "ring_add",
-            smem=(0,),
-        )(scalars, grad_w, ahead, behind)
-        marks.append(ahead)
-        ahead = lax.ppermute(ahead, "dp", right)
-        behind = lax.ppermute(behind, "dp", left)
-    return ahead, behind, marks
+            wait=done,
+        )(rest, ahead, behind)
+        ahead = lax.ppermute(to_right, "dp", right)
+        behind = lax.ppermute(to_left, "dp", left)
 
 
 def root_of(values):
@@ -294,20 +317,32 @@
         smalls[source] = block[shard:, 0:shard].astype(FULL)
 
 
-def finish(count, scalars, blocks, weights, smalls, small_out):
+def finish_small(count, scalars, blocks, smalls, small_out):
+    smalls[...] = blocks[1][...]
+    top, bottom = blocks[2:]
+    shard = smalls.shape[2]
+    source = ring_source(ring_place(scalars[0], count) + count // 2, count)
+    smalls[source] = bottom[shard - top.shape[0] :, 0:shard].astype(FULL)
+    for d in range(count):
+        small_out[:, d * shard : (d + 1) * shard] = smalls[d]
+
+
+def finish(count, scalars, blocks, weights_out, sem):
+    weights = blocks[0]
     shard = weights.shape[0] // count
-    weights[...] = blocks[0][...]
-    smalls[...] = blocks[1][...]
     top, bottom = blocks[2:]
     source = ring_source(ring_place(scalars[0], count) + count // 2, count)
     middle = top.shape[0]
     start = pl.multiple_of(source * shard, 16)
-    weights[pl.ds(start, middle), :] = top[...]
     rest = shard - middle
-    weights[pl.ds(pl.multiple_of(start + middle, 16), rest), :] = bottom[0:rest, :]
-    smalls[source] = bottom[rest:, 0:shard].astype(FULL)
-    for d in range(count):
-        small_out[:, d * shard : (d + 1) * shard] = smalls[d]
+    weights.wait()
+    weights.held[pl.ds(start, middle), :] = top[...]
+    weights.held[pl.ds(pl.multiple_of(start + middle, 16), rest), :] = bottom[0:rest, :]
+    copy = pltpu.make_async_copy(
+        weights.held.at[pl.ds(start, shard), :], weights_out.at[pl.ds(start, shard), :], sem
+    )
+    copy.start()
+    return copy
 
 
 def positions_of(piece, rows, shape, dim):
@@ -322,11 +357,14 @@
     given = 4 if has_blocks else 2
     blocks = refs[5 : 5 + given]
     outs = refs[5 + given :]
-    keep, keep_far, send, send_far, ones, qkv_out, attended, probs_out, group = outs[:9]
+    heads = len(outs) - (12 if has_blocks else 8)
+    keep, keep_far, send, send_far, ones, qkv_out, attended, group = outs[:8]
+    probs_out = outs[8 : 8 + heads]
+    copy = None
     if has_blocks:
-        weights, small_out, smalls = outs[9:]
-        finish(count, scalars, blocks, weights, smalls, small_out)
-        small = small_out
+        weights_out, small_out, smalls, sem = outs[8 + heads :]
+        finish_small(count, scalars, blocks, smalls, small_out)
+        weights, small = blocks[0], small_out
     else:
         weights, small = blocks
     rows = tokens.shape[0]
@@ -339,6 +377,8 @@
         group[index * rows : (index + 1) * rows, :] = ref[...]
         values = ref[...].astype(FULL)
         ones[index * rows : (index + 1) * rows, :] = (values * root_of(values) * gain).astype(LOW)
+    if has_blocks:
+        copy = finish(count, scalars, blocks, weights_out, sem)
     qkv = dot(ones[...], weights[:, 0 : 3 * local]).astype(LOW)
     qkv_out[...] = qkv
     query_pos = positions_of(piece, rows, (total, 1), 0)
@@ -356,14 +396,19 @@
         v = qkv[:, 2 * local + at : 2 * local + at + HEAD_DIM]
         scores = dot_nt(q, k) * SCALE + bias
         shifted = jnp.exp(scores - jnp.max(scores, axis=1, keepdims=True))
-        probs = shifted * (1.0 / jnp.sum(shifted, axis=1, keepdims=True))
-        probs_out[h] = probs
-        attended[:, at : at + HEAD_DIM] = dot(probs.astype(LOW), v).astype(LOW)
+        probs = (shifted * (1.0 / jnp.sum(shifted, axis=1, keepdims=True))).astype(LOW)
+        probs_out[h][...] = probs
+        attended[:, at : at + HEAD_DIM] = dot(probs, v).astype(LOW)
+    qkv_out.flush()
+    for probs in probs_out:
+        probs.flush()
     w_out_t = weights[:, 3 * local :]
     keep[...] = dot_nt(attended[0:rows, :], w_out_t)
     keep_far[...] = dot_nt(attended[rows : 2 * rows, :], w_out_t)
     send[...] = dot_nt(attended[2 * rows : 3 * rows, :], w_out_t).astype(LOW)
     send_far[...] = dot_nt(attended[3 * rows :, :], w_out_t).astype(LOW)
+    if copy is not None:
+        copy.wait()
 
 
 def middle_kernel(gain_row, tokens, keep, near, far, small, spread, middle, rows):
@@ -381,6 +426,11 @@
 
 GELU_A = 0.7978845608028654
 GELU_B = 0.044715
+
+
+def flush(ref):
+    if isinstance(ref, Stored):
+        ref.flush()
 
 
 def expert_kernel(
@@ -408,6 +458,7 @@
     x[rows:, :] = x_send[...]
     cot[0:rows, :] = cot_keep[...]
     cot[rows:, :] = cot_send[...]
+    flush(x)
     hidden = dot(x[...], w_in[...])
     pulled = dot_nt(cot[...], w_out[...])
     router_t = small[0:experts, :].astype(LOW)
@@ -424,11 +475,13 @@
     slope = half + 0.5 * GELU_A * hidden * (1.0 - wave * wave) * (1.0 + 3.0 * GELU_B * square)
     grad_hidden = (gate * pulled * slope).astype(LOW)
     hidden_out[...] = grad_hidden
+    flush(hidden_out)
     grad_gate = jnp.sum(active.astype(FULL) * pulled, axis=1, keepdims=True)
     grad_logits = (gate * grad_gate * (jnp.where(mine, 1.0, 0.0) - chances)).astype(LOW)
     buffer_out[...] = (gate * cot[...].astype(FULL)).astype(LOW)
     gate_out[...] = gate
     router_out[...] = dot_tn(grad_logits, x[...])
+    flush(router_out)
     part = dot_nt(grad_hidden, w_in[...]) + dot(grad_logits, router_t)
     part_keep[...] = part[0:rows, :]
     part_send[...] = part[rows:, :].astype(LOW)
@@ -443,6 +496,7 @@
     send_far[...] = part[rows:, :].astype(LOW)
     part = first_gate[...] * dot(first[...], w_out[...])
     keep[...] = part[0:rows, :]
+    keep.flush()
     send[...] = part[rows:, :].astype(LOW)
 
 
@@ -458,10 +512,6 @@
         return jnp.concatenate([part[...] for part in parts], axis=0)
 
     out[0] = dot_tn(whole(lefts), whole(rights))
-
-
-def result_kernel(middle, spread, back, out):
-    out[...] = (middle[...] + dot(spread[...], back[...])).astype(LOW)
 
 
 def back_kernel(gain_row, middle, cot, spread, back, small, grad_middle, grad_low, grad_gain):
@@ -480,28 +530,24 @@
 
 def attend_back_kernel(
     experts,
+    heads,
+    scalars,
     own,
     far,
     near,
     near_far,
-    ones,
+    weights,
     qkv,
     attended,
-    probs,
-    weights,
+    ones,
     group,
-    router_one,
-    router_two,
-    gain_two,
-    keep,
-    keep_far,
-    send,
-    send_far,
-    grad_w,
-    payload,
-    grads,
-    joined,
+    *refs,
 ):
+    probs = refs[:heads]
+    router_one, router_two, gain_two, keep, keep_far, send, send_far, payload = refs[
+        heads : heads + 8
+    ]
+    *ring_rows, grad_w, grads, joined, flipped = refs[heads + 8 :]
     rows = own.shape[0]
     local = attended.shape[1]
     joined[0:rows, :] = own[...]
@@ -517,16 +563,32 @@
         v = qkv[:, 2 * local + at : 2 * local + at + HEAD_DIM]
         upstream = grad_attended[:, at : at + HEAD_DIM]
         grad_p = dot_nt(upstream, v)
-        p = probs[h]
+        low = probs[h][...]
+        p = low.astype(FULL)
         inner = jnp.sum(p * grad_p, axis=1, keepdims=True)
         grad_s = (p * (grad_p - inner)).astype(LOW)
         grads[:, at : at + HEAD_DIM] = (dot(grad_s, k) * SCALE).astype(LOW)
-        grads[:, local + at : local + at + HEAD_DIM] = (dot_tn(grad_s, q) * SCALE).astype(LOW)
-        grads[:, 2 * local + at : 2 * local + at + HEAD_DIM] = dot_tn(
-            p.astype(LOW), upstream
-        ).astype(LOW)
+        flipped[at : at + HEAD_DIM, :] = dot_tn(q, grad_s) * SCALE
+        flipped[local + at : local + at + HEAD_DIM, :] = dot_tn(upstream, low)
+    grads[:, local:] = flipped[...].T.astype(LOW)
     grad_w[:, 3 * local :] = dot_tn(joined[...], attended[...]).astype(LOW)
     grad_w[:, 0 : 3 * local] = dot_tn(ones[...], grads[...]).astype(LOW)
+    if ring_rows:
+        top, bottom, rest = ring_rows
+        middle = top.shape[0]
+        shard = middle + bottom.shape[0]
+        count = grad_w.shape[0] // shard
+        place = ring_place(scalars[0], count)
+
+        def start_of(step):
+            return pl.multiple_of(ring_source(place + step, count) * shard, 16)
+
+        start = start_of(count // 2)
+        top[...] = grad_w[pl.ds(start, middle), :]
+        bottom[...] = grad_w[pl.ds(pl.multiple_of(start + middle, 16), shard - middle), :]
+        steps = [sign * k for k in range(count // 2 - 1, 0, -1) for sign in (1, -1)] + [0]
+        for index, step in enumerate(steps):
+            rest[index * shard : (index + 1) * shard, :] = grad_w[pl.ds(start_of(step), shard), :]
     w_qkv = weights[:, 0 : 3 * local]
 
     def normed(values):
@@ -557,53 +619,47 @@
         payload[d] = whole[:, d * shard : (d + 1) * shard]
 
 
-def last_kernel(gain_row, tokens, keep, near, far, grad_middle, small, grad_tokens):
-    rows = tokens.shape[0]
+def last_kernel(
+    experts,
+    tokens,
+    keep,
+    near,
+    far,
+    grad_middle,
+    small,
+    middle,
+    spread,
+    back,
+    grad_tokens,
+    result,
+):
     values = tokens[...].astype(FULL)
     root = root_of(values)
     normed = values * root
     grad_one = keep[...] + near[...].astype(FULL) + far[...].astype(FULL)
-    scaled = grad_one * small[gain_row : gain_row + 1, :]
+    scaled = grad_one * small[experts : experts + 1, :]
     grad_tokens[...] = grad_middle[...] + root * (
         scaled - normed * jnp.mean(scaled * normed, axis=1, keepdims=True)
     )
-
-
-def ring_rows(count, shard, scalars, offset):
-    source = ring_source(ring_place(scalars[0], count) + offset, count)
-    return pl.multiple_of(source * shard, 16)
-
-
-def ring_first_kernel(count, scalars, grad_w, top, bottom):
-    middle = top.shape[0]
-    rest = bottom.shape[0]
-    start = ring_rows(count, middle + rest, scalars, count // 2)
-    top[...] = grad_w[pl.ds(start, middle), :]
-    bottom[...] = grad_w[pl.ds(pl.multiple_of(start + middle, 16), rest), :]
-
-
-def ring_add_kernel(count, step, scalars, grad_w, ahead, behind, to_right, to_left):
+    grad_tokens.flush()
+    result[...] = (middle[...] + dot(spread[...], back[...])).astype(LOW)
+
+
+def ring_add_kernel(rest, ahead, behind, to_right, to_left, left_over):
     shard = to_right.shape[0]
-    right = ring_rows(count, shard, scalars, step)
-    left = ring_rows(count, shard, scalars, -step)
+    left_over[...] = rest[2 * shard :, :]
     if ahead.shape[0] == shard:
-        to_right[...] = (
-            grad_w[pl.ds(right, shard), :].astype(FULL) + ahead[...].astype(FULL)
-        ).astype(LOW)
+        to_right[...] = (rest[0:shard, :].astype(FULL) + ahead[...].astype(FULL)).astype(LOW)
         to_left[...] = (
-            grad_w[pl.ds(left, shard), :].astype(FULL) + behind[...].astype(FULL)
+            rest[shard : 2 * shard, :].astype(FULL) + behind[...].astype(FULL)
         ).astype(LOW)
         return
     middle = ahead.shape[0]
-    rest = shard - middle
-    to_right[0:middle, :] = (
-        grad_w[pl.ds(right, middle), :].astype(FULL) + ahead[...].astype(FULL)
-    ).astype(LOW)
-    to_right[middle:, :] = grad_w[pl.ds(pl.multiple_of(right + middle, 16), rest), :]
-    to_left[0:middle, :] = grad_w[pl.ds(left, middle), :]
+    to_right[0:middle, :] = (rest[0:middle, :].astype(FULL) + ahead[...].astype(FULL)).astype(LOW)
+    to_right[middle:, :] = rest[middle:shard, :]
+    to_left[0:middle, :] = rest[shard : shard + middle, :]
     to_left[middle:, :] = (
-        grad_w[pl.ds(pl.multiple_of(left + middle, 16), rest), :].astype(FULL)
-        + behind[...].astype(FULL)
+        rest[shard + middle : 2 * shard, :].astype(FULL) + behind[...].astype(FULL)
     ).astype(LOW)
 
 
@@ -615,20 +671,25 @@
     out[...] = total[:, 3 * local :].T
 
 
-def ring_last_kernel(count, scalars, grad_w, ahead, behind, query, key, value, out):
-    shard = ahead.shape[0]
-    start = pl.multiple_of(scalars[0] * shard, 16)
-    total = grad_w[pl.ds(start, shard), :].astype(FULL) + (
-        ahead[...].astype(FULL) + behind[...].astype(FULL)
-    )
+def ring_last_kernel(experts, mine, ahead, behind, parts, query, key, value, out, *small):
+    total = mine[...].astype(FULL) + (ahead[...].astype(FULL) + behind[...].astype(FULL))
     write_sums(total, query, key, value, out)
-
-
-def sum_kernel(blocks, query, key, value, out):
+    write_small(experts, parts, *small)
+
+
+def write_small(experts, parts, gain_one, gain_two, router):
+    total = jnp.sum(parts[...], axis=0)
+    router[...] = total[0:experts, :]
+    gain_one[...] = total[experts : experts + 1, :]
+    gain_two[...] = total[experts + 1 : experts + 2, :]
+
+
+def sum_kernel(experts, blocks, parts, query, key, value, out, *small):
     total = blocks[0].astype(FULL)
     for d in range(1, blocks.shape[0]):
         total = total + blocks[d].astype(FULL)
     write_sums(total, query, key, value, out)
+    write_small(experts, parts, *small)
 
 
 def on_device(
@@ -682,17 +743,18 @@
             [((width, 4 * local), LOW), ((owners, small_rows, shard), FULL)],
             "assemble",
             smem=(0,),
+            store=(0,),
         )(scalars, packed, *behind, *ahead)
         blocks = [*partial, top, bottom]
         early = behind[0]
-        scratch = [pltpu.VMEM((owners, small_rows, shard), FULL)]
+        scratch = [pltpu.VMEM((owners, small_rows, shard), FULL), pltpu.SemaphoreType.DMA]
     else:
         gathered = lax.all_gather(packed, "dp", axis=0, tiled=False)
         flat = gathered[:, shard:, :shard].transpose(1, 0, 2).reshape(small_rows, width)
         blocks = [gathered[:, :shard].reshape(width, 4 * local), flat.astype(FULL)]
         early = packed
-    token_far = swap_far(after(tokens, early))
-    token_near = swap_near(after(tokens, early))
+    token_far = swap_far(tokens)
+    token_near = swap_near(tokens)
 
     spread, cot_rows = kernel_call(
         functools.partial(spread_kernel, capacity, slots),
@@ -700,12 +762,14 @@
         "spread",
         smem=(0,),
         fetch=(1, 2),
-        store=(0, 1),
+        store=(0,),
         time=2,
-    )(scalars, routes, after(cotangent, early))
-    token_near_far = swap_near(after(token_far, spread))
-
-    cot_own = exchange(after(cot_rows, blocks[0]).reshape(experts, capacity, width))
+        wait=(early,),
+    )(scalars, routes, cotangent)
+    token_near_far = swap_near(token_far)
+
+    cot_rows = add(cot_rows, wait=(blocks[1],))
+    cot_own = exchange(cot_rows.reshape(experts, capacity, width))
     cot_own = cot_own.reshape(slots, width)
 
     outs = [
@@ -716,57 +780,64 @@
         ((total_rows, width), LOW),
         ((total_rows, 3 * local), LOW),
         ((total_rows, local), LOW),
-        ((heads, total_rows, total_rows), FULL),
         ((total_rows, width), LOW),
     ]
+    outs += [((total_rows, total_rows), LOW)] * heads
+    raw, alias, fetch = [], {}, [1]
     if has_blocks:
         outs += [((width, 4 * local), LOW), ((small_rows, width), FULL)]
+        raw, alias, fetch = [len(outs) - 2], {5: len(outs) - 2}, [1, 5]
     made = kernel_call(
         functools.partial(attend_kernel, owners, sequences, has_blocks),
         outs,
         "attend",
         smem=(0,),
-        fetch=(1,),
+        fetch=fetch,
+        store=(5, *range(8, 8 + heads)),
+        raw=raw,
+        alias=alias,
         scratch=scratch,
         time=4,
     )(scalars, tokens, token_far, token_near, token_near_far, *blocks)
     keep, keep_far, send, send_far = made[:4]
-    weights, small = made[9:] if has_blocks else blocks
-
-    def scatter(keep_far, send, send_far, *others):
+    ones, qkv, attended, group, *probs = made[4 : 8 + heads]
+    weights, small = made[8 + heads :] if has_blocks else blocks
+
+    def scatter(keep_far, send, send_far, wait=()):
         near_far = swap_near(send_far)
         near = swap_near(send)
-        (out,) = kernel_call(far_kernel, [(keep_far.shape, LOW)], "far")(
-            keep_far, after(near_far, *others)
+        (out,) = kernel_call(far_kernel, [(keep_far.shape, LOW)], "far", time=0.1, wait=wait)(
+            keep_far, near_far
         )
         return near, swap_far(out), out
 
-    near, far, mark = scatter(keep_far, send, send_far, cot_own)
-    ones, qkv, attended, probs, group, weights_kept, small_kept = save(
-        after(made[4], mark), *made[5:9], weights, small
-    )
-    tokens_here, spread_here = load(after(tokens, mark), spread)
+    near, far, mark = scatter(keep_far, send, send_far)
+    small_now = small
+    ones, attended, group, small = save(ones, attended, group, small, wait=(mark,))
+    tokens_here, spread_here = load(tokens, spread, wait=(mark, cot_own))
     middle, own_rows = kernel_call(
         functools.partial(middle_kernel, experts + 1),
         [((piece_rows, width), FULL), ((slots, width), LOW)],
         "middle",
-    )(tokens_here, keep, near, after(far, ones, spread_here), small, spread_here)
-    (middle_kept,) = save(after(middle, own_rows))
+        wait_hbm=(ones,),
+    )(tokens_here, keep, near, far, small_now, spread_here)
+    (middle,) = save(middle, wait=(own_rows,))
 
     def over_dp(rows):
         return exchange(rows.reshape(experts, capacity, width)).reshape(slots, width)
 
     own = over_dp(own_rows)
-    cot_far = swap_far(after(cot_own, own_rows))
+    cot_far = swap_far(cot_own)
     cot_near = swap_near(cot_own)
     cot_near_far = swap_near(cot_far)
-    own_far = swap_far(after(own, cot_near_far))
+    own_far = swap_far(own)
     own_near = swap_near(own)
+    (small_expert,) = load(small, wait=(own_rows,))
     weight_in = w_expert_in[0]
     weight_out = w_expert_out[0]
     hidden_size = weight_in.shape[1]
 
-    def expert_part(x_keep, x_send, cot_keep, cot_send):
+    def expert_part(x_keep, x_send, cot_keep, cot_send, store):
         rows = 2 * slots
         return kernel_call(
             functools.partial(expert_kernel, experts),
@@ -782,120 +853,174 @@
             ],
             "expert",
             smem=(0,),
+            store=store,
             time=4,
             scratch=[pltpu.VMEM((rows, width), LOW)],
-        )(scalars, x_keep, x_send, cot_keep, cot_send, weight_in, weight_out, small)
-
-    small = small_kept
+        )(scalars, x_keep, x_send, cot_keep, cot_send, weight_in, weight_out, small_expert)
+
     keep, send, active_one, hidden_one, buffer_one, gate_one, router_one, rows_one = expert_part(
-        own, own_near, cot_own, cot_near
-    )
+        own, own_near, cot_own, cot_near, (3, 6, 7)
+    )
+    own_far = add(own_far, wait=(send,))
     keep_far, send_far, active_two, hidden_two, buffer_two, gate_two, router_two, rows_two = (
-        expert_part(own_far, swap_near(after(own_far, send)), cot_far, cot_near_far)
+        expert_part(own_far, swap_near(own_far), cot_far, cot_near_far, ())
     )
     near, far, mark = scatter(keep_far, send, send_far)
+    rows_two, hidden_two, router_two = save(rows_two, hidden_two, router_two, wait=(mark,))
     forward_keep, forward_send, forward_keep_far, forward_send_far = kernel_call(
         forward_kernel,
         [((slots, width), kind) for kind in (FULL, LOW, FULL, LOW)],
         "forward",
+        store=(0,),
         time=2,
-    )(active_one, gate_one, active_two, gate_two, after(weight_out, mark))
+        wait=(mark,),
+    )(active_one, gate_one, active_two, gate_two, weight_out)
     (grad_expert_out,) = kernel_call(
-        grad_w_kernel, [((1, *weight_out.shape), FULL)], "grad_out", store=(0,), time=3
-    )(active_one, active_two, after(buffer_one, forward_send), buffer_two)
-    (back_rows,) = kernel_call(join_kernel, [((slots, width), LOW)], "join")(
-        keep, near, after(far, grad_expert_out)
-    )
+        grad_w_kernel, [((1, *weight_out.shape), FULL)], "grad_out", store=(0,), time=3, wait=(mark,)
+    )(active_one, active_two, buffer_one, buffer_two)
+    (back_rows,) = kernel_call(
+        join_kernel,
+        [((slots, width), LOW)],
+        "join",
+        wait=(forward_send,),
+        wait_hbm=(grad_expert_out, hidden_two),
+    )(keep, near, far)
     back = over_dp(back_rows)
     out_near, out_far, out_mark = scatter(
-        forward_keep_far, forward_send, after(forward_send_far, back_rows)
+        forward_keep_far, forward_send, forward_send_far, wait=(back_rows,)
     )
     (grad_expert_in,) = kernel_call(
-        grad_w_kernel, [((1, *weight_in.shape), FULL)], "grad_in", store=(0,), time=3
-    )(rows_one, rows_two, after(hidden_one, out_mark), hidden_two)
-    middle_here, cot_here, spread_here, small_here = load(
-        after(middle_kept, out_mark), cotangent, spread, small_kept
-    )
-    (out_rows,) = kernel_call(join_kernel, [((slots, width), LOW)], "join")(
-        forward_keep, out_near, out_far
-    )
+        grad_w_kernel, [((1, *weight_in.shape), FULL)], "grad_in", fetch=range(4), store=(0,), time=3
+    )(rows_one, rows_two, hidden_one, hidden_two)
+    middle_here, cot_here, spread_here, small_here, forward_here = load(
+        middle, cotangent, spread, small, forward_keep, wait=(out_mark,)
+    )
+    (out_rows,) = kernel_call(join_kernel, [((slots, width), LOW)], "join", time=0.1)(
+        forward_here, out_near, out_far
+    )
+    out_back = over_dp(out_rows)
 
     grad_middle, grad_low, grad_gain_two = kernel_call(
         functools.partial(back_kernel, experts + 1),
         [((piece_rows, width), FULL), ((piece_rows, width), LOW), ((1, width), FULL)],
         "back",
-    )(middle_here, cot_here, spread_here, after(back, grad_expert_in), small_here)
+        wait=(out_far,),
+        wait_hbm=(grad_expert_in,),
+    )(middle_here, cot_here, spread_here, back, small_here)
     grad_far = swap_far(grad_low)
     grad_near = swap_near(grad_low)
-    out_back = over_dp(after(out_rows, grad_near))
-    (grad_middle_kept,) = save(after(grad_middle, grad_low))
-    here = load(
-        *(after(ones, grad_low), qkv, attended, probs, weights_kept, group)
-    )
+    (grad_middle,) = save(grad_middle)
+    grad_far = add(grad_far, wait=(out_rows,))
     grad_near_far = swap_near(grad_far)
-    keep, keep_far, send, send_far, grad_w, payload = kernel_call(
-        functools.partial(attend_back_kernel, experts),
-        [
-            ((piece_rows, width), FULL),
-            ((piece_rows, width), FULL),
-            ((piece_rows, width), LOW),
-            ((piece_rows, width), LOW),
-            ((width, 4 * local), LOW),
-            ((owners, small_rows, shard), FULL),
-        ],
+    outs = [
+        ((piece_rows, width), FULL),
+        ((piece_rows, width), FULL),
+        ((piece_rows, width), LOW),
+        ((piece_rows, width), LOW),
+        ((owners, small_rows, shard), FULL),
+    ]
+    middle_row = shard // 32 * 16
+    scratch = [
+        pltpu.VMEM((total_rows, 3 * local), LOW),
+        pltpu.VMEM((total_rows, width), LOW),
+        pltpu.VMEM((2 * local, total_rows), FULL),
+    ]
+    if has_blocks:
+        outs += [
+            ((middle_row, 4 * local), LOW),
+            ((shard - middle_row, 4 * local), LOW),
+            ((width - shard, 4 * local), LOW),
+        ]
+        scratch = [pltpu.VMEM((width, 4 * local), LOW)] + scratch
+    else:
+        outs.append(((width, 4 * local), LOW))
+    keep, keep_far, send, send_far, payload, *grad_w = kernel_call(
+        functools.partial(attend_back_kernel, experts, heads),
+        outs,
         "attend_back",
+        smem=(0,),
+        fetch=range(5, 12 + heads),
         store=(0,),
-        time=5,
-        scratch=[pltpu.VMEM((total_rows, 3 * local), LOW), pltpu.VMEM((total_rows, width), LOW)],
+        time=2,
+        scratch=scratch,
     )(
+        scalars,
         grad_low,
         grad_far,
         grad_near,
         grad_near_far,
-        *here,
-        router_one,
-        router_two,
+        *(weights, qkv, attended, ones, group, *probs, router_one, router_two),
         grad_gain_two,
     )
     last = [((shard, local), FULL)] * 3 + [((local, shard), FULL)]
-    near, far, mark = scatter(keep_far, send, send_far)
-    marks = [mark] * 4
+    held = {}
+
+    near_far, near = swap_near(send_far), swap_near(send)
+
+    def first(mark):
+        total = add(payload, swap(payload, "tensor", 1), wait=(mark,))
+        came = swap(total, "tensor", 2)
+        held["small"] = (total, came)
+        return (total,), (came,)
+
+    def second(mark):
+        total = add(*held["small"], wait=(mark,))
+        held["small"] = exchange(total)
+        return (total,), ()
+
+    def third(mark):
+        (out,) = kernel_call(far_kernel, [(keep_far.shape, LOW)], "far", time=0.1, wait=(mark,))(
+            keep_far, near_far
+        )
+        held["far"] = swap_far(out)
+        return (out,), (held["far"],)
+
+    def fourth(mark):
+        held["last"] = kernel_call(
+            functools.partial(last_kernel, experts),
+            [
+                ((piece_rows, width), FULL),
+                ((piece_rows, width), LOW),
+            ],
+            "last",
+            fetch=(0, 1, 4, 5, 6, 7),
+            store=(0, 1),
+            time=0.3,
+            wait=(mark,),
+        )(
+            *(tokens, keep, near, held["far"], grad_middle, small, middle, spread, out_back)
+        )
+        return (), ()
+
+    fillers = (first, second, third, fourth)
+    last += [((1, shard), FULL), ((1, shard), FULL), ((experts, shard), FULL)]
     if has_blocks:
-        ahead, behind, marks = ring_reduce(grad_w, scalars, (shard, 4 * local))
-        grad_query, grad_key, grad_value, grad_out = kernel_call(
-            functools.partial(ring_last_kernel, owners),
+        parts = ring_reduce(*grad_w, shard, fillers, (out_back,))
+        sums = kernel_call(
+            functools.partial(ring_last_kernel, experts),
             last,
             "ring_last",
-            smem=(0,),
-            store=range(4),
-        )(scalars, grad_w, ahead, behind)
+            store=range(7),
+            wait_hbm=held["last"][:1],
+        )(*parts, held["small"])
     else:
-        grad_query, grad_key, grad_value, grad_out = kernel_call(
-            sum_kernel, last, "sum", store=range(4)
-        )(exchange(grad_w.reshape(owners, shard, 4 * local)))
-    payload = payload + swap(payload, "tensor", 1)
-    payload = payload + swap(payload, "tensor", 2)
-    sums = jnp.sum(after(exchange(after(payload, marks[1], out_back)), marks[2]), axis=0)
-    (grad_tokens,) = kernel_call(
-        functools.partial(last_kernel, experts),
-        [((piece_rows, width), FULL)],
-        "last",
-        fetch=(0, 1, 4, 5),
-        store=(0,),
-    )(tokens, keep, near, far, after(grad_middle_kept, marks[3]), small_kept)
-    (result,) = kernel_call(
-        result_kernel, [((piece_rows, width), LOW)], "result", fetch=(0, 1), store=(0,)
-    )(after(middle_kept, marks[3]), spread, out_back)
+        for filler in fillers:
+            filler(grad_w[0])
+        sums = kernel_call(
+            functools.partial(sum_kernel, experts), last, "sum", store=range(7)
+        )(exchange(grad_w[0].reshape(owners, shard, 4 * local)), held["small"])
+    grad_query, grad_key, grad_value, grad_out, grad_norm_attn, grad_norm_moe, grad_router = sums
+    grad_tokens, result = held["last"]
     return (
         result,
         grad_tokens,
-        sums[experts],
+        grad_norm_attn.reshape(shard),
         grad_query,
         grad_key,
         grad_value,
         grad_out,
-        sums[experts + 1],
-        sums[:experts].T,
+        grad_norm_moe.reshape(shard),
+        grad_router.T,
         grad_expert_in,
         grad_expert_out,
     )

time: 166 us -> 153 us (0.922)
  local copies, waits for them, and re-layouts: 14.2 us -> 0.89 us
  Pallas kernels: 49.5 us -> 51.6 us
    unnamed x73 -> x11, local copies, waits for them, and re-layouts: 13 us -> 0.88 us
    ppermute x26, waiting for transfers between devices: 23.4 us -> 15.8 us  [swap(): return lax.ppermute(values, axis, [(i, i ^ bit) for i in range(count)])]
    ppermute x3, waiting for transfers between devices: 5.71 us -> 0.01 us  [ring_gather(): ahead.append(lax.ppermute(ahead[-1], 'dp', left))]
    ppermute x3, starting transfers between devices: 6.15 us -> 0.56 us  [ring_gather(): ahead.append(lax.ppermute(ahead[-1], 'dp', left))]
    ppermute x3, starting transfers between devices: 1.05 us -> 6.57 us  [ring_gather(): behind.append(lax.ppermute(behind[-1], 'dp', right))]
    ppermute x3, waiting for transfers between devices: 0.01 us -> 5.35 us  [ring_gather(): behind.append(lax.ppermute(behind[-1], 'dp', right))]
    ppermute x6, waiting for transfers between devices: 0.02 us -> 4.72 us  [the longest x3 2.48 us: ring_reduce(): ahead = lax.ppermute(to_right, 'dp', right)]
    all_to_all x5, waiting for transfers between devices: 7.45 us -> 10.2 us  [exchange(): return lax.all_to_all(buffer, 'dp', split_axis=0, concat_axis=0, tiled=True)]
  transfers between devices with their start and end apart: 47 -> 47, of which waited for: 19 -> 19; matrix products, arithmetic and copies ran while one was open for 2% -> 1% of each run, Pallas kernels for 25% -> 29%
where the time goes in v3:
time: 153 us
  starting transfers between devices  58.9 us (38%)
  Pallas kernels  51.6 us (34%)
  waiting for transfers between devices  39.9 us (26%)
    pallas_call x32, Pallas kernels, call(): pl.pallas_call(kernel, out_shape=[pltpu.HBM(*outs[i]) if i in kept else j...  44.4 us
    all_to_all x5, starting transfers between devices, exchange(): return lax.all_to_all(buffer, 'dp', split_axis=0, concat_axis=0, tiled=True)  25.2 us
    ppermute x26, starting transfers between devices, swap(): return lax.ppermute(values, axis, [(i, i ^ bit) for i in range(count)])  16 us
    ppermute x26, waiting for transfers between devices, swap(): return lax.ppermute(values, axis, [(i, i ^ bit) for i in range(count)])  15.8 us
    all_to_all x5, waiting for transfers between devices, exchange(): return lax.all_to_all(buffer, 'dp', split_axis=0, concat_axis=0, tiled=True)  10.2 us
    pallas_call x7, Pallas kernels, moved(): pl.pallas_call(functools.partial(move_kernel, len(kinds)), out_shape=[plt...  7.19 us
    ppermute x3, starting transfers between devices, ring_gather(): behind.append(lax.ppermute(behind[-1], 'dp', right))  6.57 us
    ppermute x3, waiting for transfers between devices, ring_gather(): behind.append(lax.ppermute(behind[-1], 'dp', right))  5.35 us
  transfers between devices with their start and end apart: 47, of which 19 were waited for; matrix products, arithmetic and copies ran while one was open for 1% of the time, Pallas kernels for 29%

profile of v3, /device:TPU:0, one launch (start us, length us, event | category | flops | bytes accessed | tf_op | source)
XLA Modules:
  0.0 152.7 jit_solution(7883381099760637114)
XLA Ops:
  1.9 3.1 %collective-permute-start = (bf16[112,768]{1,0:T(8,128)(2,1)S(1)}, bf16[112,768]{1,0:T(8,128)(2,1)S(1)}, u32[]{:S(2)}, u32[]{:S(2)}) collective-permute-start(bf16[112,768]{1,0:T(8,128)(2,1)S(1)} %pack.1.refs_1_), channel_id=1, source_target_pairs={{0,8},{8,16},{16,24},{24,28},{28,20},{20,12},{12,4},{4,0},{1,9},{9... | collective-permute-start | bytes 516104 | tf_op jit(solution)/shard_map/ppermute | solution.py:207
  6.9 2.3 %collective-permute-done.refs_3_.refs_2_ = bf16[112,768]{1,0:T(8,128)(2,1)S(1)} collective-permute-done((bf16[112,768]{1,0:T(8,128)(2,1)S(1)}, bf16[112,768]{1,0:T(8,128)(2,1)S(1)}, u32[]{:S(2)}, u32[]{:S(2)}) %collective-permute-start) | collective-permute-done | bytes 172064 | tf_op jit(solution)/shard_map/ppermute | solution.py:207
  12.7 2.1 %collective-permute-done.4.refs_3_ = bf16[112,768]{1,0:T(8,128)(2,1)S(1)} collective-permute-done((bf16[112,768]{1,0:T(8,128)(2,1)S(1)}, bf16[112,768]{1,0:T(8,128)(2,1)S(1)}, u32[]{:S(2)}, u32[]{:S(2)}) %collective-permute-start.4) | collective-permute-done | bytes 172064 | tf_op jit(solution)/shard_map/ppermute | solution.py:207
  16.8 2.5 %spread.1 = (bf16[128,192]{1,0:T(8,128)(2,1)}, bf16[192,768]{1,0:T(8,128)(2,1)S(1)}) custom-call(s32[5]{0:T(128)S(1)} %pad_add_fusion.refs_0_, s32[512,1]{1,0:T(8,128)} %copy.25.refs_1_, bf16[128,768]{1,0:T(8,128)(2,1)} %refs_1_.6, bf16[112,768]{1,0:T(8,128)(2,1)S(1)} %collective-permute-done.refs_3_.refs_2_), custom_call_target="tpu_custom_call" | custom-call | flops 2200000000 | bytes 1048576 | tf_op jit(solution)/shard_map/spread/pallas_call | solution.py:102
  25.1 5.9 %all-to-all-start = ((bf16[8,24,768]{2,1,0:T(8,128)(2,1)}), bf16[8,24,768]{2,1,0:T(8,128)(2,1)S(1)}, u32[]{:S(2)}, u32[]{:S(2)}) async-start(bf16[8,24,768]{2,1,0:T(8,128)(2,1)} %bitcast.6), calls=%async_computation | async-start | bytes 589824 | tf_op jit(solution)/shard_map/all_to_all | solution.py:177
  31.0 6.1 %attend.1 = (f32[128,768]{1,0:T(8,128)S(1)}, f32[128,768]{1,0:T(8,128)S(1)}, bf16[128,768]{1,0:T(8,128)(2,1)S(1)}, bf16[128,768]{1,0:T(8,128)(2,1)S(1)}, bf16[51...) custom-call(s32[5]{0:T(128)S(1)} %pad_add_fusion.refs_0_, ...), custom_call_target="tpu_custom_call", output_to_operand_aliasing={{11}: (5, {})} | custom-call | flops 4400000000 | bytes 1048576 | tf_op jit(solution)/shard_map/attend/pallas_call | solution.py:102
  42.5 3.2 %collective-permute-done.13.refs_3_ = bf16[128,768]{1,0:T(8,128)(2,1)S(1)} collective-permute-done((bf16[128,768]{1,0:T(8,128)(2,1)S(1)}, bf16[128,768]{1,0:T(8,128)(2,1)S(1)}, u32[]{:S(2)}, u32[]{:S(2)}) %collective-permute-start.13) | collective-permute-done | bytes 196640 | tf_op jit(solution)/shard_map/ppermute | solution.py:173
  46.8 6.0 %all-to-all-start.1 = ((bf16[8,24,768]{2,1,0:T(8,128)(2,1)}), bf16[8,24,768]{2,1,0:T(8,128)(2,1)S(1)}, u32[]{:S(2)}, u32[]{:S(2)}) async-start(bf16[8,24,768]{2,1,0:T(8,128)(2,1)} %bitcast.8), calls=%async_computation.1 | async-start | bytes 589824 | tf_op jit(solution)/shard_map/all_to_all | solution.py:177
  54.3 7.5 %all-to-all-done.1 = bf16[8,24,768]{2,1,0:T(8,128)(2,1)S(1)} async-done(((bf16[8,24,768]{2,1,0:T(8,128)(2,1)}), bf16[8,24,768]{2,1,0:T(8,128)(2,1)S(1)}, u32[]{:S(2)}, u32[]{:S(2)}) %all-to-all-start.1) | async-done | bytes 294944 | tf_op jit(solution)/shard_map/all_to_all | solution.py:177
  64.9 3.7 %expert.2 = (f32[192,768]{1,0:T(8,128)S(1)}, bf16[192,768]{1,0:T(8,128)(2,1)S(1)}, bf16[384,768]{1,0:T(8,128)(2,1)S(1)}, bf16[384,768]{1,0:T(8,128)(2,1)}, bf16[...) custom-call(s32[5]{0:T(128)S(1)} %pad_add_fusion.refs_0_, ...), custom_call_target="tpu_custom_call" | custom-call | flops 4400000000 | bytes 1048576 | tf_op jit(solution)/shard_map/expert/pallas_call | solution.py:102
  68.6 3.7 %collective-permute-done.16.refs_0_ = bf16[192,768]{1,0:T(8,128)(2,1)S(1)} collective-permute-done((bf16[192,768]{1,0:T(8,128)(2,1)S(1)}, bf16[192,768]{1,0:T(8,128)(2,1)S(1)}, u32[]{:S(2)}, u32[]{:S(2)}) %collective-permute-start.16) | collective-permute-done | bytes 294944 | tf_op jit(solution)/shard_map/ppermute | solution.py:173
  74.0 3.5 %expert.3 = (f32[192,768]{1,0:T(8,128)S(1)}, bf16[192,768]{1,0:T(8,128)(2,1)S(1)}, bf16[384,768]{1,0:T(8,128)(2,1)S(1)}, bf16[384,768]{1,0:T(8,128)(2,1)S(1)}, b...) custom-call(s32[5]{0:T(128)S(1)} %pad_add_fusion.refs_0_, ...), custom_call_target="tpu_custom_call" | custom-call | flops 4400000000 | bytes 1048576 | tf_op jit(solution)/shard_map/expert/pallas_call | solution.py:102
  82.8 2.5 %grad_out.1.refs_4_ = f32[1,768,768]{2,1,0:T(8,128)} custom-call(bf16[384,768]{1,0:T(8,128)(2,1)S(1)} %get-tuple-element.111.refs_0_, bf16[384,768]{1,0:T(8,128)(2,1)S(1)} %get-tuple-element.114.refs_2_.refs_1_, bf16[384,768]{1,0:T(8,128)(2,1)S(1)} %get-tuple-element.123.refs_2_, bf16[384,768]{1,0:T(8,128)(2,1)S(1)} %get-tuple-element.124.refs_3_, ...), custom_call_target="tpu_custom_call" | custom-call | flops 3300000000 | bytes 1048576 | tf_op jit(solution)/shard_map/grad_out/pallas_call | solution.py:102
  89.2 3.6 %all-to-all-start.2 = ((bf16[8,24,768]{2,1,0:T(8,128)(2,1)}), bf16[8,24,768]{2,1,0:T(8,128)(2,1)S(1)}, u32[]{:S(2)}, u32[]{:S(2)}) async-start(bf16[8,24,768]{2,1,0:T(8,128)(2,1)} %bitcast.12), calls=%async_computation.2 | async-start | bytes 589824 | tf_op jit(solution)/shard_map/all_to_all | solution.py:177
  95.4 4.2 %grad_in.1.refs_6_ = f32[1,768,768]{2,1,0:T(8,128)} custom-call(bf16[384,768]{1,0:T(8,128)(2,1)} %get-tuple-element.133.refs_0_, bf16[384,768]{1,0:T(8,128)(2,1)} %get-tuple-element.134.refs_1_, bf16[384,768]{1,0:T(8,128)(2,1)} %get-tuple-element.135.refs_2_, bf16[384,768]{1,0:T(8,128)(2,1)} %get-tuple-element.128.refs_5_.refs_3_), custom_call_target="tpu_custom_call" | custom-call | flops 3300000000 | bytes 1048576 | tf_op jit(solution)/shard_map/grad_in/pallas_call | solution.py:102
  100.9 2.3 %collective-permute-done.24.refs_5_.refs_2_ = bf16[192,768]{1,0:T(8,128)(2,1)S(1)} collective-permute-done((bf16[192,768]{1,0:T(8,128)(2,1)S(1)}, bf16[192,768]{1,0:T(8,128)(2,1)S(1)}, u32[]{:S(2)}, u32[]{:S(2)}) %collective-permute-start.24) | collective-permute-done | bytes 294944 | tf_op jit(solution)/shard_map/ppermute | solution.py:173
  106.0 6.0 %all-to-all-start.3 = ((bf16[8,24,768]{2,1,0:T(8,128)(2,1)}), bf16[8,24,768]{2,1,0:T(8,128)(2,1)S(1)}, u32[]{:S(2)}, u32[]{:S(2)}) async-start(bf16[8,24,768]{2,1,0:T(8,128)(2,1)} %bitcast.14), calls=%async_computation.3 | async-start | bytes 589824 | tf_op jit(solution)/shard_map/all_to_all | solution.py:177
  113.7 8.9 %attend_back.1 = (f32[128,768]{1,0:T(8,128)}, f32[128,768]{1,0:T(8,128)S(1)}, bf16[128,768]{1,0:T(8,128)(2,1)S(1)}, bf16[128,768]{1,0:T(8,128)(2,1)S(1)}, f32[8,...) custom-call(s32[5]{0:T(128)S(1)} %pad_add_fusion.refs_0_, ...), custom_call_target="tpu_custom_call" | custom-call | flops 2200000000 | bytes 1048576 | tf_op jit(solution)/shard_map/attend_back/pallas_call | solution.py:102
  123.0 2.0 %collective-permute-start.31 = (bf16[48,768]{1,0:T(8,128)(2,1)S(1)}, bf16[48,768]{1,0:T(8,128)(2,1)S(1)}, u32[]{:S(2)}, u32[]{:S(2)}) collective-permute-start(bf16[48,768]{1,0:T(8,128)(2,1)S(1)} %get-tuple-element.153), channel_id=1, source_target_pairs={{0,8},{8,16},{16,24},{24,28},{28,20},{20,12},{12,4},{4,0},{1,9},{9... | collective-permute-start | bytes 221192 | tf_op jit(solution)/shard_map/ppermute | solution.py:244
  132.2 2.5 %collective-permute-done.34.refs_1_ = bf16[96,768]{1,0:T(8,128)(2,1)S(1)} collective-permute-done((bf16[96,768]{1,0:T(8,128)(2,1)S(1)}, bf16[96,768]{1,0:T(8,128)(2,1)S(1)}, u32[]{:S(2)}, u32[]{:S(2)}) %collective-permute-start.34) | collective-permute-done | bytes 147488 | tf_op jit(solution)/shard_map/ppermute | solution.py:259
  139.8 3.7 %all-to-all-start.4 = ((f32[8,16,96]{2,1,0:T(8,128)}), f32[8,16,96]{2,1,0:T(8,128)S(1)}, u32[]{:S(2)}, u32[]{:S(2)}) async-start(f32[8,16,96]{2,1,0:T(8,128)} %add.13.refs_3_), calls=%async_computation.4 | async-start | bytes 131072 | tf_op jit(solution)/shard_map/all_to_all | solution.py:177
  143.6 2.1 %collective-permute-start.40 = (bf16[96,768]{1,0:T(8,128)(2,1)S(1)}, bf16[96,768]{1,0:T(8,128)(2,1)S(1)}, u32[]{:S(2)}, u32[]{:S(2)}) collective-permute-start(bf16[96,768]{1,0:T(8,128)(2,1)S(1)} %get-tuple-element.166), channel_id=1, source_target_pairs={{0,8},{8,16},{16,24},{24,28},{28,20},{20,12},{12,4},{4,0},{1,9},{9... | collective-permute-start | bytes 442376 | tf_op jit(solution)/shard_map/ppermute | solution.py:259
  145.7 2.3 %last.1 = (f32[128,768]{1,0:T(8,128)}, bf16[128,768]{1,0:T(8,128)(2,1)}) custom-call(bf16[128,768]{1,0:T(8,128)(2,1)} %refs_0_.5, f32[128,768]{1,0:T(8,128)} %get-tuple-element.148.refs_1_, bf16[128,768]{1,0:T(8,128)(2,1)S(1)} %collective-permute-done.29.refs_2_, bf16[128,768]{1,0:T(8,128)(2,1)S(1)} %collective-permute-done.37.refs_1_.refs_3_, ...), custom_call_target="tpu_custom_call" | custom-call | flops 330000000 | bytes 1048576 | tf_op jit(solution)/shard_map/last/pallas_call | solution.py:102
  148.1 2.7 %all-to-all-done.4.refs_3_ = f32[8,16,96]{2,1,0:T(8,128)S(1)} async-done(((f32[8,16,96]{2,1,0:T(8,128)}), f32[8,16,96]{2,1,0:T(8,128)S(1)}, u32[]{:S(2)}, u32[]{:S(2)}) %all-to-all-start.4) | async-done | bytes 49184 | tf_op jit(solution)/shard_map/all_to_all | solution.py:177
  (123 shorter events, 58.9 us)
Async XLA Ops:
  1.9 7.4 %collective-permute-start = (bf16[112,768]{1,0:T(8,128)(2,1)S(1)}, bf16[112,768]{1,0:T(8,128)(2,1)S(1)}, u32[]{:S(2)}, u32[]{:S(2)}) collective-permute-start(bf16[112,768]{1,0:T(8,128)(2,1)S(1)} %pack.1.refs_1_), channel_id=1, source_target_pairs={{0,8},{8,16},{16,24},{24,28},{28,20},{20,12},{12,4},{4,0},{1,9},{9... | collective-permute-start | bytes 516104 | tf_op jit(solution)/shard_map/ppermute | solution.py:207
  5.0 7.3 %collective-permute-start.1 = (bf16[128,768]{1,0:T(8,128)(2,1)S(1)}, bf16[128,768]{1,0:T(8,128)(2,1)S(1)}, u32[]{:S(2)}, u32[]{:S(2)}) collective-permute-start(bf16[128,768]{1,0:T(8,128)(2,1)S(1)} %copy-done.2), channel_id=1, source_target_pairs={{0,2},{1,3},{2,0},{3,1},{4,6},{5,7},{6,4},{7,5},{8,10},{9,11},{10,... | collective-permute-start | bytes 589832 | tf_op jit(solution)/shard_map/ppermute | solution.py:173
  11.3 19.7 %collective-permute-start.2 = (bf16[128,768]{1,0:T(8,128)(2,1)S(1)}, bf16[128,768]{1,0:T(8,128)(2,1)S(1)}, u32[]{:S(2)}, u32[]{:S(2)}) collective-permute-start(bf16[128,768]{1,0:T(8,128)(2,1)S(1)} %copy-done.2), channel_id=1, source_target_pairs={{0,1},{1,0},{2,3},{3,2},{4,5},{5,4},{6,7},{7,6},{8,9},{9,8},{10,11... | collective-permute-start | bytes 589832 | tf_op jit(solution)/shard_map/ppermute | solution.py:173
  12.2 18.8 %collective-permute-start.3 = (bf16[128,768]{1,0:T(8,128)(2,1)S(1)}, bf16[128,768]{1,0:T(8,128)(2,1)S(1)}, u32[]{:S(2)}, u32[]{:S(2)}) collective-permute-start(bf16[128,768]{1,0:T(8,128)(2,1)S(1)} %collective-permute-done.1.refs_2_), channel_id=1, source_target_pairs={{0,1},{1,0},{2,3},{3,2},{4,5},{5,4},{6,7},{7,6},{8,9},{9,8},{10,11... | collective-permute-start | bytes 589832 | tf_op jit(solution)/shard_map/ppermute | solution.py:173
  20.3 10.6 %collective-permute-start.9 = (bf16[48,768]{1,0:T(8,128)(2,1)S(1)}, bf16[48,768]{1,0:T(8,128)(2,1)S(1)}, u32[]{:S(2)}, u32[]{:S(2)}) collective-permute-start(bf16[48,768]{1,0:T(8,128)(2,1)S(1)} %slice.8), channel_id=1, source_target_pairs={{0,8},{8,16},{16,24},{24,28},{28,20},{20,12},{12,4},{4,0},{1,9},{9... | collective-permute-start | bytes 221192 | tf_op jit(solution)/shard_map/ppermute | solution.py:210
  22.2 8.8 %collective-permute-start.10 = (bf16[64,768]{1,0:T(8,128)(2,1)S(1)}, bf16[64,768]{1,0:T(8,128)(2,1)S(1)}, u32[]{:S(2)}, u32[]{:S(2)}) collective-permute-start(bf16[64,768]{1,0:T(8,128)(2,1)S(1)} %slice.9), channel_id=1, source_target_pairs={{8,0},{16,8},{24,16},{28,24},{20,28},{12,20},{4,12},{0,4},{9,1},{1... | collective-permute-start | bytes 294920 | tf_op jit(solution)/shard_map/ppermute | solution.py:211
  25.1 16.4 %all-to-all-start = ((bf16[8,24,768]{2,1,0:T(8,128)(2,1)}), bf16[8,24,768]{2,1,0:T(8,128)(2,1)S(1)}, u32[]{:S(2)}, u32[]{:S(2)}) async-start(bf16[8,24,768]{2,1,0:T(8,128)(2,1)} %bitcast.6), calls=%async_computation | async-start | bytes 589824 | tf_op jit(solution)/shard_map/all_to_all | solution.py:177
  46.8 15.0 %all-to-all-start.1 = ((bf16[8,24,768]{2,1,0:T(8,128)(2,1)}), bf16[8,24,768]{2,1,0:T(8,128)(2,1)S(1)}, u32[]{:S(2)}, u32[]{:S(2)}) async-start(bf16[8,24,768]{2,1,0:T(8,128)(2,1)} %bitcast.8), calls=%async_computation.1 | async-start | bytes 589824 | tf_op jit(solution)/shard_map/all_to_all | solution.py:177
  52.7 10.0 %collective-permute-start.18 = (bf16[192,768]{1,0:T(8,128)(2,1)S(1)}, bf16[192,768]{1,0:T(8,128)(2,1)S(1)}, u32[]{:S(2)}, u32[]{:S(2)}) collective-permute-start(bf16[192,768]{1,0:T(8,128)(2,1)S(1)} %bitcast.22), channel_id=1, source_target_pairs={{0,2},{1,3},{2,0},{3,1},{4,6},{5,7},{6,4},{7,5},{8,10},{9,11},{10,... | collective-permute-start | bytes 884744 | tf_op jit(solution)/shard_map/ppermute | solution.py:173
  54.3 10.6 %collective-permute-start.15 = (bf16[192,768]{1,0:T(8,128)(2,1)S(1)}, bf16[192,768]{1,0:T(8,128)(2,1)S(1)}, u32[]{:S(2)}, u32[]{:S(2)}) collective-permute-start(bf16[192,768]{1,0:T(8,128)(2,1)S(1)} %bitcast.23), channel_id=1, source_target_pairs={{0,1},{1,0},{2,3},{3,2},{4,5},{5,4},{6,7},{7,6},{8,9},{9,8},{10,11... | collective-permute-start | bytes 884744 | tf_op jit(solution)/shard_map/ppermute | solution.py:173
  62.8 9.7 %collective-permute-start.19 = (bf16[192,768]{1,0:T(8,128)(2,1)S(1)}, bf16[192,768]{1,0:T(8,128)(2,1)S(1)}, u32[]{:S(2)}, u32[]{:S(2)}) collective-permute-start(bf16[192,768]{1,0:T(8,128)(2,1)S(1)} %collective-permute-done.18.refs_3_), channel_id=1, source_target_pairs={{0,1},{1,0},{2,3},{3,2},{4,5},{5,4},{6,7},{7,6},{8,9},{9,8},{10,11... | collective-permute-start | bytes 884744 | tf_op jit(solution)/shard_map/ppermute | solution.py:173
  63.3 9.0 %collective-permute-start.16 = (bf16[192,768]{1,0:T(8,128)(2,1)S(1)}, bf16[192,768]{1,0:T(8,128)(2,1)S(1)}, u32[]{:S(2)}, u32[]{:S(2)}) collective-permute-start(bf16[192,768]{1,0:T(8,128)(2,1)S(1)} %bitcast.26), channel_id=1, source_target_pairs={{0,2},{1,3},{2,0},{3,1},{4,6},{5,7},{6,4},{7,5},{8,10},{9,11},{10,... | collective-permute-start | bytes 884744 | tf_op jit(solution)/shard_map/ppermute | solution.py:173
  77.8 8.7 %collective-permute-start.22 = (bf16[192,768]{1,0:T(8,128)(2,1)S(1)}, bf16[192,768]{1,0:T(8,128)(2,1)S(1)}, u32[]{:S(2)}, u32[]{:S(2)}) collective-permute-start(bf16[192,768]{1,0:T(8,128)(2,1)S(1)} %get-tuple-element.113.refs_1_), channel_id=1, source_target_pairs={{0,1},{1,0},{2,3},{3,2},{4,5},{5,4},{6,7},{7,6},{8,9},{9,8},{10,11... | collective-permute-start | bytes 884744 | tf_op jit(solution)/shard_map/ppermute | solution.py:173
  79.3 9.1 %collective-permute-start.23 = (bf16[192,768]{1,0:T(8,128)(2,1)S(1)}, bf16[192,768]{1,0:T(8,128)(2,1)S(1)}, u32[]{:S(2)}, u32[]{:S(2)}) collective-permute-start(bf16[192,768]{1,0:T(8,128)(2,1)S(1)} %far.5.refs_5_.refs_4_.refs_3_), channel_id=1, source_target_pairs={{0,2},{1,3},{2,0},{3,1},{4,6},{5,7},{6,4},{7,5},{8,10},{9,11},{10,... | collective-permute-start | bytes 884744 | tf_op jit(solution)/shard_map/ppermute | solution.py:173
  82.8 10.9 %collective-permute-start.21 = (bf16[192,768]{1,0:T(8,128)(2,1)S(1)}, bf16[192,768]{1,0:T(8,128)(2,1)S(1)}, u32[]{:S(2)}, u32[]{:S(2)}) collective-permute-start(bf16[192,768]{1,0:T(8,128)(2,1)S(1)} %get-tuple-element.120), channel_id=1, source_target_pairs={{0,1},{1,0},{2,3},{3,2},{4,5},{5,4},{6,7},{7,6},{8,9},{9,8},{10,11... | collective-permute-start | bytes 884744 | tf_op jit(solution)/shard_map/ppermute | solution.py:173
  89.2 14.1 %all-to-all-start.2 = ((bf16[8,24,768]{2,1,0:T(8,128)(2,1)}), bf16[8,24,768]{2,1,0:T(8,128)(2,1)S(1)}, u32[]{:S(2)}, u32[]{:S(2)}) async-start(bf16[8,24,768]{2,1,0:T(8,128)(2,1)} %bitcast.12), calls=%async_computation.2 | async-start | bytes 589824 | tf_op jit(solution)/shard_map/all_to_all | solution.py:177
  93.6 11.6 %collective-permute-start.26 = (bf16[192,768]{1,0:T(8,128)(2,1)S(1)}, bf16[192,768]{1,0:T(8,128)(2,1)S(1)}, u32[]{:S(2)}, u32[]{:S(2)}) collective-permute-start(bf16[192,768]{1,0:T(8,128)(2,1)S(1)} %get-tuple-element.122.refs_3_), channel_id=1, source_target_pairs={{0,1},{1,0},{2,3},{3,2},{4,5},{5,4},{6,7},{7,6},{8,9},{9,8},{10,11... | collective-permute-start | bytes 884744 | tf_op jit(solution)/shard_map/ppermute | solution.py:173
  93.8 9.5 %collective-permute-start.24 = (bf16[192,768]{1,0:T(8,128)(2,1)S(1)}, bf16[192,768]{1,0:T(8,128)(2,1)S(1)}, u32[]{:S(2)}, u32[]{:S(2)}) collective-permute-start(bf16[192,768]{1,0:T(8,128)(2,1)S(1)} %far.6.refs_5_), channel_id=1, source_target_pairs={{0,2},{1,3},{2,0},{3,1},{4,6},{5,7},{6,4},{7,5},{8,10},{9,11},{10,... | collective-permute-start | bytes 884744 | tf_op jit(solution)/shard_map/ppermute | solution.py:173
  103.6 8.4 %collective-permute-start.25 = (bf16[128,768]{1,0:T(8,128)(2,1)S(1)}, bf16[128,768]{1,0:T(8,128)(2,1)S(1)}, u32[]{:S(2)}, u32[]{:S(2)}) collective-permute-start(bf16[128,768]{1,0:T(8,128)(2,1)S(1)} %get-tuple-element.136.refs_1_), channel_id=1, source_target_pairs={{0,2},{1,3},{2,0},{3,1},{4,6},{5,7},{6,4},{7,5},{8,10},{9,11},{10,... | collective-permute-start | bytes 589832 | tf_op jit(solution)/shard_map/ppermute | solution.py:173
  106.0 19.1 %all-to-all-start.3 = ((bf16[8,24,768]{2,1,0:T(8,128)(2,1)}), bf16[8,24,768]{2,1,0:T(8,128)(2,1)S(1)}, u32[]{:S(2)}, u32[]{:S(2)}) async-start(bf16[8,24,768]{2,1,0:T(8,128)(2,1)} %bitcast.14), calls=%async_computation.3 | async-start | bytes 589824 | tf_op jit(solution)/shard_map/all_to_all | solution.py:177
  125.1 13.3 %collective-permute-start.30 = (bf16[128,768]{1,0:T(8,128)(2,1)S(1)}, bf16[128,768]{1,0:T(8,128)(2,1)S(1)}, u32[]{:S(2)}, u32[]{:S(2)}) collective-permute-start(bf16[128,768]{1,0:T(8,128)(2,1)S(1)} %get-tuple-element.151), channel_id=1, source_target_pairs={{0,1},{1,0},{2,3},{3,2},{4,5},{5,4},{6,7},{7,6},{8,9},{9,8},{10,11... | collective-permute-start | bytes 589832 | tf_op jit(solution)/shard_map/ppermute | solution.py:173
  136.3 7.2 %collective-permute-start.38 = (bf16[96,768]{1,0:T(8,128)(2,1)S(1)}, bf16[96,768]{1,0:T(8,128)(2,1)S(1)}, u32[]{:S(2)}, u32[]{:S(2)}) collective-permute-start(bf16[96,768]{1,0:T(8,128)(2,1)S(1)} %get-tuple-element.161), channel_id=1, source_target_pairs={{0,8},{8,16},{16,24},{24,28},{28,20},{20,12},{12,4},{4,0},{1,9},{9... | collective-permute-start | bytes 442376 | tf_op jit(solution)/shard_map/ppermute | solution.py:259
  138.4 7.3 %collective-permute-start.37 = (bf16[128,768]{1,0:T(8,128)(2,1)S(1)}, bf16[128,768]{1,0:T(8,128)(2,1)S(1)}, u32[]{:S(2)}, u32[]{:S(2)}) collective-permute-start(bf16[128,768]{1,0:T(8,128)(2,1)S(1)} %far.7.refs_3_), channel_id=1, source_target_pairs={{0,2},{1,3},{2,0},{3,1},{4,6},{5,7},{6,4},{7,5},{8,10},{9,11},{10,... | collective-permute-start | bytes 589832 | tf_op jit(solution)/shard_map/ppermute | solution.py:173
  139.8 11.0 %all-to-all-start.4 = ((f32[8,16,96]{2,1,0:T(8,128)}), f32[8,16,96]{2,1,0:T(8,128)S(1)}, u32[]{:S(2)}, u32[]{:S(2)}) async-start(f32[8,16,96]{2,1,0:T(8,128)} %add.13.refs_3_), calls=%async_computation.4 | async-start | bytes 131072 | tf_op jit(solution)/shard_map/all_to_all | solution.py:177
  (28 other events, 137.3 us)

commit v4 on v3

--- a/solution.py
+++ b/solution.py
@@ -29,16 +29,17 @@
 
 
 class Fetched:
-    def __init__(self, ref, held, sem):
-        self.held, self.waiting = held, True
+    def __init__(self, ref, held, sem, late):
+        self.held, self.waiting, self.late = held, True, late
         self.copy = pltpu.make_async_copy(ref, held, sem)
-        self.copy.start()
         self.shape = held.shape
 
     def wait(self):
         if self.waiting:
             self.copy.wait()
             self.waiting = False
+            while self.late:
+                self.late.pop(0).copy.start()
 
     def __getitem__(self, index):
         self.wait()
@@ -63,7 +64,7 @@
             self.copy.start()
 
 
-def kernel_call(body, outs, name, fetch=(), store=(), smem=(), time=1, limit=24, scratch=(), raw=(), alias=(), wait=(), wait_hbm=()):
+def kernel_call(body, outs, name, fetch=(), store=(), smem=(), time=1, limit=24, scratch=(), raw=(), alias=(), wait=(), wait_hbm=(), first=99):
     def call(*operands):
         n_in, n_out, n_scratch = len(operands), len(outs), len(scratch)
         held = [pltpu.VMEM(operands[i].shape, operands[i].dtype) for i in fetch]
@@ -75,9 +76,13 @@
             results, rest = list(refs[:n_out]), refs[n_out:]
             own, buffers = rest[:n_scratch], rest[n_scratch : n_scratch + len(held)]
             sem = rest[-1] if held else None
-            at = 0
+            at, late = 0, []
             for i in fetch:
-                ins[i] = Fetched(ins[i], buffers[at], sem.at[at])
+                ins[i] = Fetched(ins[i], buffers[at], sem.at[at], late)
+                if at < first:
+                    ins[i].copy.start()
+                else:
+                    late.append(ins[i])
                 at += 1
             for i in store:
                 results[i] = Stored(results[i], buffers[at], sem.at[at])
@@ -232,9 +237,9 @@
     refs[-1][...] = total.astype(refs[-1].dtype)
 
 
-def add(*values, wait=()):
+def add(*values, wait=(), wait_hbm=()):
     kind = (values[0].shape, values[0].dtype)
-    return kernel_call(add_kernel, [kind], "add", time=0.1, wait=wait)(*values)[0]
+    return kernel_call(add_kernel, [kind], "add", time=0.1, wait=wait, wait_hbm=wait_hbm)(*values)[0]
 
 
 def ring_reduce(top, bottom, rest, shard, fillers, arrived=()):
@@ -243,10 +248,10 @@
     width = rest.shape[1]
     ahead = lax.ppermute(top, "dp", right)
     behind = lax.ppermute(bottom, "dp", left)
-    done = ()
+    done, kept = (), ()
     for index, step in enumerate(range(count // 2 - 1, -1, -1)):
         if index < len(fillers):
-            done, arrived = fillers[index](fence(rest, arrived))
+            done, arrived, kept = fillers[index](fence(rest, arrived))
         if not step:
             return rest, ahead, behind
         block = (shard, width)
@@ -255,6 +260,7 @@
             [(block, LOW), (block, LOW), ((rest.shape[0] - 2 * shard, width), LOW)],
             "ring_add",
             wait=done,
+            wait_hbm=kept,
         )(rest, ahead, behind)
         ahead = lax.ppermute(to_right, "dp", right)
         behind = lax.ppermute(to_left, "dp", left)
@@ -373,7 +379,7 @@
     experts = count
     gain = small[experts : experts + 1, :]
     piece = scalars[1]
-    for index, ref in enumerate((tokens, far, near, near_far)):
+    for index, ref in ((1, far), (2, near), (3, near_far), (0, tokens)):
         group[index * rows : (index + 1) * rows, :] = ref[...]
         values = ref[...].astype(FULL)
         ones[index * rows : (index + 1) * rows, :] = (values * root_of(values) * gain).astype(LOW)
@@ -381,6 +387,7 @@
         copy = finish(count, scalars, blocks, weights_out, sem)
     qkv = dot(ones[...], weights[:, 0 : 3 * local]).astype(LOW)
     qkv_out[...] = qkv
+    qkv_out.flush()
     query_pos = positions_of(piece, rows, (total, 1), 0)
     key_pos = positions_of(piece, rows, (1, total), 1)
     start = jnp.zeros((total, 1), jnp.int32)
@@ -399,7 +406,6 @@
         probs = (shifted * (1.0 / jnp.sum(shifted, axis=1, keepdims=True))).astype(LOW)
         probs_out[h][...] = probs
         attended[:, at : at + HEAD_DIM] = dot(probs, v).astype(LOW)
-    qkv_out.flush()
     for probs in probs_out:
         probs.flush()
     w_out_t = weights[:, 3 * local :]
@@ -529,7 +535,6 @@
 
 
 def attend_back_kernel(
-    experts,
     heads,
     scalars,
     own,
@@ -538,16 +543,10 @@
     near_far,
     weights,
     qkv,
-    attended,
-    ones,
-    group,
     *refs,
 ):
-    probs = refs[:heads]
-    router_one, router_two, gain_two, keep, keep_far, send, send_far, payload = refs[
-        heads : heads + 8
-    ]
-    *ring_rows, grad_w, grads, joined, flipped = refs[heads + 8 :]
+    probs, (attended, ones, grads) = refs[:heads], refs[heads : heads + 3]
+    *ring_rows, grad_w, joined, flipped = refs[heads + 3 :]
     rows = own.shape[0]
     local = attended.shape[1]
     joined[0:rows, :] = own[...]
@@ -556,7 +555,7 @@
     joined[3 * rows :, :] = near_far[...]
     w_out_t = weights[:, 3 * local :]
     grad_attended = dot(joined[...], w_out_t).astype(LOW)
-    for h in range(local // HEAD_DIM):
+    for h in range(heads):
         at = h * HEAD_DIM
         q = qkv[:, at : at + HEAD_DIM]
         k = qkv[:, local + at : local + at + HEAD_DIM]
@@ -589,22 +588,34 @@
         steps = [sign * k for k in range(count // 2 - 1, 0, -1) for sign in (1, -1)] + [0]
         for index, step in enumerate(steps):
             rest[index * shard : (index + 1) * shard, :] = grad_w[pl.ds(start_of(step), shard), :]
-    w_qkv = weights[:, 0 : 3 * local]
-
-    def normed(values):
-        values = values.astype(FULL)
-        return values * root_of(values)
-
+
+
+def grad_one_kernel(
+    experts,
+    grads,
+    weights,
+    group,
+    router_one,
+    router_two,
+    gain_two,
+    keep,
+    keep_far,
+    send,
+    send_far,
+    payload,
+):
+    rows = keep.shape[0]
+    w_qkv = weights[:, 0 : grads.shape[1]]
     gain_one = None
     for index, out in enumerate((keep, keep_far, send, send_far)):
-        part = dot_nt(grads[index * rows : (index + 1) * rows, :], w_qkv)
+        at = slice(index * rows, (index + 1) * rows)
+        part = dot_nt(grads[at, :], w_qkv)
         out[...] = part.astype(out.dtype)
+        values = group[at, :].astype(FULL)
+        gain = jnp.sum(part * (values * root_of(values)), axis=0, keepdims=True)
+        gain_one = gain if gain_one is None else gain_one + gain
         if index == 0:
-            out.flush()
-        gain = jnp.sum(
-            part * normed(group[index * rows : (index + 1) * rows, :]), axis=0, keepdims=True
-        )
-        gain_one = gain if gain_one is None else gain_one + gain
+            keep.flush()
     owners, height, shard = payload.shape
     whole = jnp.concatenate(
         [
@@ -830,9 +841,10 @@
     cot_far = swap_far(cot_own)
     cot_near = swap_near(cot_own)
     cot_near_far = swap_near(cot_far)
+    (small_expert,) = load(small, wait=(own_rows,))
+    own = add(own, wait=(small_expert, cot_far), wait_hbm=(middle,))
     own_far = swap_far(own)
     own_near = swap_near(own)
-    (small_expert,) = load(small, wait=(own_rows,))
     weight_in = w_expert_in[0]
     weight_out = w_expert_out[0]
     hidden_size = weight_in.shape[1]
@@ -859,13 +871,14 @@
         )(scalars, x_keep, x_send, cot_keep, cot_send, weight_in, weight_out, small_expert)
 
     keep, send, active_one, hidden_one, buffer_one, gate_one, router_one, rows_one = expert_part(
-        own, own_near, cot_own, cot_near, (3, 6, 7)
+        own, own_near, cot_own, cot_near, (0, 3, 6, 7)
     )
     own_far = add(own_far, wait=(send,))
     keep_far, send_far, active_two, hidden_two, buffer_two, gate_two, router_two, rows_two = (
         expert_part(own_far, swap_near(own_far), cot_far, cot_near_far, ())
     )
     near, far, mark = scatter(keep_far, send, send_far)
+    (keep,) = load(keep, wait=(mark,))
     rows_two, hidden_two, router_two = save(rows_two, hidden_two, router_two, wait=(mark,))
     forward_keep, forward_send, forward_keep_far, forward_send_far = kernel_call(
         forward_kernel,
@@ -909,19 +922,11 @@
     )(middle_here, cot_here, spread_here, back, small_here)
     grad_far = swap_far(grad_low)
     grad_near = swap_near(grad_low)
-    (grad_middle,) = save(grad_middle)
     grad_far = add(grad_far, wait=(out_rows,))
     grad_near_far = swap_near(grad_far)
-    outs = [
-        ((piece_rows, width), FULL),
-        ((piece_rows, width), FULL),
-        ((piece_rows, width), LOW),
-        ((piece_rows, width), LOW),
-        ((owners, small_rows, shard), FULL),
-    ]
+    outs = [((total_rows, 3 * local), LOW)]
     middle_row = shard // 32 * 16
     scratch = [
-        pltpu.VMEM((total_rows, 3 * local), LOW),
         pltpu.VMEM((total_rows, width), LOW),
         pltpu.VMEM((2 * local, total_rows), FULL),
     ]
@@ -934,46 +939,54 @@
         scratch = [pltpu.VMEM((width, 4 * local), LOW)] + scratch
     else:
         outs.append(((width, 4 * local), LOW))
-    keep, keep_far, send, send_far, payload, *grad_w = kernel_call(
-        functools.partial(attend_back_kernel, experts, heads),
+    grads, *grad_w = kernel_call(
+        functools.partial(attend_back_kernel, heads),
         outs,
         "attend_back",
         smem=(0,),
-        fetch=range(5, 12 + heads),
-        store=(0,),
+        fetch=range(5, 9 + heads),
+        first=2 + heads,
         time=2,
         scratch=scratch,
     )(
-        scalars,
-        grad_low,
-        grad_far,
-        grad_near,
-        grad_near_far,
-        *(weights, qkv, attended, ones, group, *probs, router_one, router_two),
-        grad_gain_two,
+        *(scalars, grad_low, grad_far, grad_near, grad_near_far),
+        *(weights, qkv, *probs, attended, ones),
     )
     last = [((shard, local), FULL)] * 3 + [((local, shard), FULL)]
     held = {}
 
-    near_far, near = swap_near(send_far), swap_near(send)
-
     def first(mark):
-        total = add(payload, swap(payload, "tensor", 1), wait=(mark,))
+        keep, keep_far, send, send_far, payload = kernel_call(
+            functools.partial(grad_one_kernel, experts),
+            [((piece_rows, width), kind) for kind in (FULL, FULL, LOW, LOW)]
+            + [((owners, small_rows, shard), FULL)],
+            "grad_one",
+            fetch=(1, 2, 3, 4),
+            store=(0,),
+            time=0.2,
+            wait=(mark,),
+        )(grads, weights, group, router_one, router_two, grad_gain_two)
+        held["keep"], held["keep_far"] = keep, keep_far
+        held["near_far"], held["near"] = swap_near(send_far), swap_near(send)
+        held["small"] = (payload, swap(payload, "tensor", 1))
+        return (send,), (), ()
+
+    def second(mark):
+        out_shape = [(held["keep_far"].shape, LOW)]
+        (out,) = kernel_call(far_kernel, out_shape, "far", time=0.1, wait=(mark,))(
+            held["keep_far"], held["near_far"]
+        )
+        held["far"] = swap_far(out)
+        total = add(*held["small"], wait=(mark,))
         came = swap(total, "tensor", 2)
         held["small"] = (total, came)
-        return (total,), (came,)
-
-    def second(mark):
+        held["middle"] = save(grad_middle, wait=(mark,))
+        return (out, total), (came,), held["middle"]
+
+    def third(mark):
         total = add(*held["small"], wait=(mark,))
         held["small"] = exchange(total)
-        return (total,), ()
-
-    def third(mark):
-        (out,) = kernel_call(far_kernel, [(keep_far.shape, LOW)], "far", time=0.1, wait=(mark,))(
-            keep_far, near_far
-        )
-        held["far"] = swap_far(out)
-        return (out,), (held["far"],)
+        return (total,), (held["far"],), ()
 
     def fourth(mark):
         held["last"] = kernel_call(
@@ -988,9 +1001,10 @@
             time=0.3,
             wait=(mark,),
         )(
-            *(tokens, keep, near, held["far"], grad_middle, small, middle, spread, out_back)
+            *(tokens, held["keep"], held["near"], held["far"]),
+            *(*held["middle"], small, middle, spread, out_back),
         )
-        return (), ()
+        return (), (), ()
 
     fillers = (first, second, third, fourth)
     last += [((1, shard), FULL), ((1, shard), FULL), ((experts, shard), FULL)]

time: 153 us -> 150 us (0.980)
  waiting for transfers between devices: 39.9 us -> 29.7 us
  starting transfers between devices: 58.9 us -> 62 us
  Pallas kernels: 51.6 us -> 54.1 us
    all_to_all x5, waiting for transfers between devices: 10.2 us -> 3.46 us  [exchange(): return lax.all_to_all(buffer, 'dp', split_axis=0, concat_axis=0, tiled=True)]
    ppermute x1, waiting for transfers between devices: 2 us -> 0.01 us  [ring_reduce(): ahead = lax.ppermute(top, 'dp', right)]
    all_to_all x5, starting transfers between devices: 25.2 us -> 27.1 us  [exchange(): return lax.all_to_all(buffer, 'dp', split_axis=0, concat_axis=0, tiled=True)]
    ppermute x26, waiting for transfers between devices: 15.8 us -> 17.5 us  [swap(): return lax.ppermute(values, axis, [(i, i ^ bit) for i in range(count)])]
    ppermute x3, waiting for transfers between devices: 2.48 us -> 0.85 us  [ring_reduce(): ahead = lax.ppermute(to_right, 'dp', right)]
    pallas_call x32 -> x34, Pallas kernels: 44.4 us -> 46 us  [call(): pl.pallas_call(kernel, out_shape=[pltpu.HBM(*outs[i]) if i in kept else j...]
    pallas_call x7 -> x8, Pallas kernels: 7.19 us -> 8.1 us  [moved(): pl.pallas_call(functools.partial(move_kernel, len(kinds)), out_shape=[plt...]
  transfers between devices with their start and end apart: 47 -> 47, of which waited for: 19 -> 19; matrix products, arithmetic and copies ran while one was open for 1% -> 1% of each run, Pallas kernels for 29% -> 32%
where the time goes in v4:
time: 150 us; the launch traced here: 149 us
  starting transfers between devices  62 us (41%)
  Pallas kernels  54.1 us (36%)
  waiting for transfers between devices  29.7 us (20%)
  local copies, waits for them, and re-layouts  2.16 us (1%)
    pallas_call x34, Pallas kernels, call(): pl.pallas_call(kernel, out_shape=[pltpu.HBM(*outs[i]) if i in kept else j...  46 us
    all_to_all x5, starting transfers between devices, exchange(): return lax.all_to_all(buffer, 'dp', split_axis=0, concat_axis=0, tiled=True)  27.1 us
    ppermute x26, waiting for transfers between devices, swap(): return lax.ppermute(values, axis, [(i, i ^ bit) for i in range(count)])  17.5 us
    ppermute x26, starting transfers between devices, swap(): return lax.ppermute(values, axis, [(i, i ^ bit) for i in range(count)])  17.1 us
    pallas_call x8, Pallas kernels, moved(): pl.pallas_call(functools.partial(move_kernel, len(kinds)), out_shape=[plt...  8.1 us
    ppermute x3, starting transfers between devices, ring_gather(): behind.append(lax.ppermute(behind[-1], 'dp', right))  6.57 us
    ppermute x3, waiting for transfers between devices, ring_gather(): behind.append(lax.ppermute(behind[-1], 'dp', right))  5.35 us
    ppermute x3, starting transfers between devices, ring_reduce(): ahead = lax.ppermute(to_right, 'dp', right)  5.1 us
  transfers between devices with their start and end apart: 47, of which 19 were waited for; matrix products, arithmetic and copies ran while one was open for 1% of the time, Pallas kernels for 32%

profile of v4, /device:TPU:0, one launch (start us, length us, event | category | flops | bytes accessed | tf_op | source)
XLA Modules:
  0.0 149.3 jit_solution(4312950779157745380)
XLA Ops:
  1.9 3.1 %collective-permute-start = (bf16[112,768]{1,0:T(8,128)(2,1)S(1)}, bf16[112,768]{1,0:T(8,128)(2,1)S(1)}, u32[]{:S(2)}, u32[]{:S(2)}) collective-permute-start(bf16[112,768]{1,0:T(8,128)(2,1)S(1)} %pack.1.refs_1_), channel_id=1, source_target_pairs={{0,8},{8,16},{16,24},{24,28},{28,20},{20,12},{12,4},{4,0},{1,9},{9... | collective-permute-start | bytes 516104 | tf_op jit(solution)/shard_map/ppermute | solution.py:212
  5.0 2.0 %collective-permute-start.1 = (bf16[128,768]{1,0:T(8,128)(2,1)S(1)}, bf16[128,768]{1,0:T(8,128)(2,1)S(1)}, u32[]{:S(2)}, u32[]{:S(2)}) collective-permute-start(bf16[128,768]{1,0:T(8,128)(2,1)S(1)} %copy-done.3), channel_id=1, source_target_pairs={{0,2},{1,3},{2,0},{3,1},{4,6},{5,7},{6,4},{7,5},{8,10},{9,11},{10,... | collective-permute-start | bytes 589832 | tf_op jit(solution)/shard_map/ppermute | solution.py:178
  6.9 2.3 %collective-permute-done.refs_3_.refs_2_ = bf16[112,768]{1,0:T(8,128)(2,1)S(1)} collective-permute-done((bf16[112,768]{1,0:T(8,128)(2,1)S(1)}, bf16[112,768]{1,0:T(8,128)(2,1)S(1)}, u32[]{:S(2)}, u32[]{:S(2)}) %collective-permute-start) | collective-permute-done | bytes 172064 | tf_op jit(solution)/shard_map/ppermute | solution.py:212
  12.7 2.1 %collective-permute-done.4.refs_3_ = bf16[112,768]{1,0:T(8,128)(2,1)S(1)} collective-permute-done((bf16[112,768]{1,0:T(8,128)(2,1)S(1)}, bf16[112,768]{1,0:T(8,128)(2,1)S(1)}, u32[]{:S(2)}, u32[]{:S(2)}) %collective-permute-start.4) | collective-permute-done | bytes 172064 | tf_op jit(solution)/shard_map/ppermute | solution.py:212
  16.8 2.5 %spread.1 = (bf16[128,192]{1,0:T(8,128)(2,1)}, bf16[192,768]{1,0:T(8,128)(2,1)S(1)}) custom-call(s32[5]{0:T(128)S(1)} %pad_add_fusion.refs_0_, s32[512,1]{1,0:T(8,128)} %copy.25.refs_1_, bf16[128,768]{1,0:T(8,128)(2,1)} %refs_1_.6, bf16[112,768]{1,0:T(8,128)(2,1)S(1)} %collective-permute-done.refs_3_.refs_2_), custom_call_target="tpu_custom_call" | custom-call | flops 2200000000 | bytes 1048576 | tf_op jit(solution)/shard_map/spread/pallas_call | solution.py:107
  25.0 5.9 %all-to-all-start = ((bf16[8,24,768]{2,1,0:T(8,128)(2,1)}), bf16[8,24,768]{2,1,0:T(8,128)(2,1)S(1)}, u32[]{:S(2)}, u32[]{:S(2)}) async-start(bf16[8,24,768]{2,1,0:T(8,128)(2,1)} %bitcast.6), calls=%async_computation | async-start | bytes 589824 | tf_op jit(solution)/shard_map/all_to_all | solution.py:182
  31.0 5.0 %attend.1 = (f32[128,768]{1,0:T(8,128)S(1)}, f32[128,768]{1,0:T(8,128)S(1)}, bf16[128,768]{1,0:T(8,128)(2,1)S(1)}, bf16[128,768]{1,0:T(8,128)(2,1)S(1)}, bf16[51...) custom-call(s32[5]{0:T(128)S(1)} %pad_add_fusion.refs_0_, ...), custom_call_target="tpu_custom_call", output_to_operand_aliasing={{11}: (5, {})} | custom-call | flops 4400000000 | bytes 1048576 | tf_op jit(solution)/shard_map/attend/pallas_call | solution.py:107
  41.4 3.2 %collective-permute-done.13.refs_3_ = bf16[128,768]{1,0:T(8,128)(2,1)S(1)} collective-permute-done((bf16[128,768]{1,0:T(8,128)(2,1)S(1)}, bf16[128,768]{1,0:T(8,128)(2,1)S(1)}, u32[]{:S(2)}, u32[]{:S(2)}) %collective-permute-start.13) | collective-permute-done | bytes 196640 | tf_op jit(solution)/shard_map/ppermute | solution.py:178
  45.7 6.0 %all-to-all-start.1 = ((bf16[8,24,768]{2,1,0:T(8,128)(2,1)}), bf16[8,24,768]{2,1,0:T(8,128)(2,1)S(1)}, u32[]{:S(2)}, u32[]{:S(2)}) async-start(bf16[8,24,768]{2,1,0:T(8,128)(2,1)} %bitcast.8), calls=%async_computation.1 | async-start | bytes 589824 | tf_op jit(solution)/shard_map/all_to_all | solution.py:182
  54.8 4.8 %collective-permute-done.14.refs_2_.refs_3_ = bf16[192,768]{1,0:T(8,128)(2,1)S(1)} collective-permute-done((bf16[192,768]{1,0:T(8,128)(2,1)S(1)}, bf16[192,768]{1,0:T(8,128)(2,1)S(1)}, u32[]{:S(2)}, u32[]{:S(2)}) %collective-permute-start.14) | collective-permute-done | bytes 294944 | tf_op jit(solution)/shard_map/ppermute | solution.py:178
  64.1 4.6 %expert.2 = (f32[192,768]{1,0:T(8,128)}, bf16[192,768]{1,0:T(8,128)(2,1)S(1)}, bf16[384,768]{1,0:T(8,128)(2,1)S(1)}, bf16[384,768]{1,0:T(8,128)(2,1)}, bf16[384,...) custom-call(s32[5]{0:T(128)S(1)} %pad_add_fusion.refs_0_, ...), custom_call_target="tpu_custom_call" | custom-call | flops 4400000000 | bytes 1048576 | tf_op jit(solution)/shard_map/expert/pallas_call | solution.py:107
  72.0 3.6 %expert.3 = (f32[192,768]{1,0:T(8,128)S(1)}, bf16[192,768]{1,0:T(8,128)(2,1)S(1)}, bf16[384,768]{1,0:T(8,128)(2,1)S(1)}, bf16[384,768]{1,0:T(8,128)(2,1)S(1)}, b...) custom-call(s32[5]{0:T(128)S(1)} %pad_add_fusion.refs_0_, ...), custom_call_target="tpu_custom_call" | custom-call | flops 4400000000 | bytes 1048576 | tf_op jit(solution)/shard_map/expert/pallas_call | solution.py:107
  80.9 2.5 %grad_out.1.refs_4_ = f32[1,768,768]{2,1,0:T(8,128)} custom-call(bf16[384,768]{1,0:T(8,128)(2,1)S(1)} %get-tuple-element.112.refs_0_, bf16[384,768]{1,0:T(8,128)(2,1)S(1)} %get-tuple-element.115.refs_2_.refs_1_, bf16[384,768]{1,0:T(8,128)(2,1)S(1)} %get-tuple-element.124.refs_2_, bf16[384,768]{1,0:T(8,128)(2,1)S(1)} %get-tuple-element.125.refs_3_, ...), custom_call_target="tpu_custom_call" | custom-call | flops 3300000000 | bytes 1048576 | tf_op jit(solution)/shard_map/grad_out/pallas_call | solution.py:107
  87.2 4.6 %all-to-all-start.2 = ((bf16[8,24,768]{2,1,0:T(8,128)(2,1)}), bf16[8,24,768]{2,1,0:T(8,128)(2,1)S(1)}, u32[]{:S(2)}, u32[]{:S(2)}) async-start(bf16[8,24,768]{2,1,0:T(8,128)(2,1)} %bitcast.12), calls=%async_computation.2 | async-start | bytes 589824 | tf_op jit(solution)/shard_map/all_to_all | solution.py:182
  93.5 4.2 %grad_in.1.refs_6_ = f32[1,768,768]{2,1,0:T(8,128)} custom-call(bf16[384,768]{1,0:T(8,128)(2,1)} %get-tuple-element.134.refs_0_, bf16[384,768]{1,0:T(8,128)(2,1)} %get-tuple-element.135.refs_1_, bf16[384,768]{1,0:T(8,128)(2,1)} %get-tuple-element.136.refs_2_, bf16[384,768]{1,0:T(8,128)(2,1)} %get-tuple-element.129.refs_5_.refs_3_), custom_call_target="tpu_custom_call" | custom-call | flops 3300000000 | bytes 1048576 | tf_op jit(solution)/shard_map/grad_in/pallas_call | solution.py:107
  99.0 2.3 %collective-permute-done.24.refs_5_.refs_2_ = bf16[192,768]{1,0:T(8,128)(2,1)S(1)} collective-permute-done((bf16[192,768]{1,0:T(8,128)(2,1)S(1)}, bf16[192,768]{1,0:T(8,128)(2,1)S(1)}, u32[]{:S(2)}, u32[]{:S(2)}) %collective-permute-start.24) | collective-permute-done | bytes 294944 | tf_op jit(solution)/shard_map/ppermute | solution.py:178
  104.2 6.0 %all-to-all-start.3 = ((bf16[8,24,768]{2,1,0:T(8,128)(2,1)}), bf16[8,24,768]{2,1,0:T(8,128)(2,1)S(1)}, u32[]{:S(2)}, u32[]{:S(2)}) async-start(bf16[8,24,768]{2,1,0:T(8,128)(2,1)} %bitcast.14), calls=%async_computation.3 | async-start | bytes 589824 | tf_op jit(solution)/shard_map/all_to_all | solution.py:182
  111.9 7.5 %attend_back.1 = (bf16[512,576]{1,0:T(8,128)(2,1)S(1)}, bf16[48,768]{1,0:T(8,128)(2,1)S(1)}, bf16[48,768]{1,0:T(8,128)(2,1)S(1)}, bf16[672,768]{1,0:T(8,128)(2,1)S(1)}) custom-call(s32[5]{0:T(128)S(1)} %pad_add_fusion.refs_0_, bf16[128,768]{1,0:T(8,128)(2,1)S(1)} %get-tuple-element.137.refs_1_, bf16[128,768]{1,0:T(8,128)(2,1)S(1)} %add.13.refs_2_, ...), custom_call_target="tpu_custom_call" | custom-call | flops 2200000000 | bytes 1048576 | tf_op jit(solution)/shard_map/attend_back/pallas_call | solution.py:107
  119.4 2.1 %collective-permute-start.31 = (bf16[48,768]{1,0:T(8,128)(2,1)S(1)}, bf16[48,768]{1,0:T(8,128)(2,1)S(1)}, u32[]{:S(2)}, u32[]{:S(2)}) collective-permute-start(bf16[48,768]{1,0:T(8,128)(2,1)S(1)} %get-tuple-element.155), channel_id=1, source_target_pairs={{0,8},{8,16},{16,24},{24,28},{28,20},{20,12},{12,4},{4,0},{1,9},{9... | collective-permute-start | bytes 221192 | tf_op jit(solution)/shard_map/ppermute | solution.py:249
  121.6 3.1 %grad_one.1 = (f32[128,768]{1,0:T(8,128)}, f32[128,768]{1,0:T(8,128)S(1)}, bf16[128,768]{1,0:T(8,128)(2,1)S(1)}, bf16[128,768]{1,0:T(8,128)(2,1)S(1)}, f32[8,16,96]{2,1,0:T(8,128)S(1)}) custom-call(bf16[512,576]{1,0:T(8,128)(2,1)S(1)} %get-tuple-element.145.refs_0_, bf16[768,768]{1,0:T(8,128)(2,1)} %get-tuple-element.139.refs_5_.refs_1_, ...), custom_call_target="tpu_custom_call" | custom-call | flops 220000000 | bytes 1048576 | tf_op jit(solution)/shard_map/grad_one/pallas_call | solution.py:107
  136.2 4.5 %all-to-all-start.4 = ((f32[8,16,96]{2,1,0:T(8,128)}), f32[8,16,96]{2,1,0:T(8,128)S(1)}, u32[]{:S(2)}, u32[]{:S(2)}) async-start(f32[8,16,96]{2,1,0:T(8,128)} %add.15.refs_3_), calls=%async_computation.4 | async-start | bytes 131072 | tf_op jit(solution)/shard_map/all_to_all | solution.py:182
  140.9 2.1 %collective-permute-start.40 = (bf16[96,768]{1,0:T(8,128)(2,1)S(1)}, bf16[96,768]{1,0:T(8,128)(2,1)S(1)}, u32[]{:S(2)}, u32[]{:S(2)}) collective-permute-start(bf16[96,768]{1,0:T(8,128)(2,1)S(1)} %get-tuple-element.168), channel_id=1, source_target_pairs={{0,8},{8,16},{16,24},{24,28},{28,20},{20,12},{12,4},{4,0},{1,9},{9... | collective-permute-start | bytes 442376 | tf_op jit(solution)/shard_map/ppermute | solution.py:265
  143.0 2.3 %last.1 = (f32[128,768]{1,0:T(8,128)}, bf16[128,768]{1,0:T(8,128)(2,1)}) custom-call(bf16[128,768]{1,0:T(8,128)(2,1)} %refs_0_.5, f32[128,768]{1,0:T(8,128)} %get-tuple-element.151.refs_1_, bf16[128,768]{1,0:T(8,128)(2,1)S(1)} %collective-permute-done.29.refs_2_, bf16[128,768]{1,0:T(8,128)(2,1)S(1)} %collective-permute-done.33.refs_1_.refs_3_, ...), custom_call_target="tpu_custom_call" | custom-call | flops 330000000 | bytes 1048576 | tf_op jit(solution)/shard_map/last/pallas_call | solution.py:107
  145.3 2.3 %all-to-all-done.4.refs_3_ = f32[8,16,96]{2,1,0:T(8,128)S(1)} async-done(((f32[8,16,96]{2,1,0:T(8,128)}), f32[8,16,96]{2,1,0:T(8,128)S(1)}, u32[]{:S(2)}, u32[]{:S(2)}) %all-to-all-start.4) | async-done | bytes 49184 | tf_op jit(solution)/shard_map/all_to_all | solution.py:182
  (128 shorter events, 59.4 us)
Async XLA Ops:
  1.9 7.4 %collective-permute-start = (bf16[112,768]{1,0:T(8,128)(2,1)S(1)}, bf16[112,768]{1,0:T(8,128)(2,1)S(1)}, u32[]{:S(2)}, u32[]{:S(2)}) collective-permute-start(bf16[112,768]{1,0:T(8,128)(2,1)S(1)} %pack.1.refs_1_), channel_id=1, source_target_pairs={{0,8},{8,16},{16,24},{24,28},{28,20},{20,12},{12,4},{4,0},{1,9},{9... | collective-permute-start | bytes 516104 | tf_op jit(solution)/shard_map/ppermute | solution.py:212
  11.3 19.7 %collective-permute-start.2 = (bf16[128,768]{1,0:T(8,128)(2,1)S(1)}, bf16[128,768]{1,0:T(8,128)(2,1)S(1)}, u32[]{:S(2)}, u32[]{:S(2)}) collective-permute-start(bf16[128,768]{1,0:T(8,128)(2,1)S(1)} %copy-done.3), channel_id=1, source_target_pairs={{0,1},{1,0},{2,3},{3,2},{4,5},{5,4},{6,7},{7,6},{8,9},{9,8},{10,11... | collective-permute-start | bytes 589832 | tf_op jit(solution)/shard_map/ppermute | solution.py:178
  12.2 18.7 %collective-permute-start.3 = (bf16[128,768]{1,0:T(8,128)(2,1)S(1)}, bf16[128,768]{1,0:T(8,128)(2,1)S(1)}, u32[]{:S(2)}, u32[]{:S(2)}) collective-permute-start(bf16[128,768]{1,0:T(8,128)(2,1)S(1)} %collective-permute-done.1.refs_2_), channel_id=1, source_target_pairs={{0,1},{1,0},{2,3},{3,2},{4,5},{5,4},{6,7},{7,6},{8,9},{9,8},{10,11... | collective-permute-start | bytes 589832 | tf_op jit(solution)/shard_map/ppermute | solution.py:178
  20.3 10.6 %collective-permute-start.9 = (bf16[48,768]{1,0:T(8,128)(2,1)S(1)}, bf16[48,768]{1,0:T(8,128)(2,1)S(1)}, u32[]{:S(2)}, u32[]{:S(2)}) collective-permute-start(bf16[48,768]{1,0:T(8,128)(2,1)S(1)} %slice.8), channel_id=1, source_target_pairs={{0,8},{8,16},{16,24},{24,28},{28,20},{20,12},{12,4},{4,0},{1,9},{9... | collective-permute-start | bytes 221192 | tf_op jit(solution)/shard_map/ppermute | solution.py:215
  22.2 8.7 %collective-permute-start.10 = (bf16[64,768]{1,0:T(8,128)(2,1)S(1)}, bf16[64,768]{1,0:T(8,128)(2,1)S(1)}, u32[]{:S(2)}, u32[]{:S(2)}) collective-permute-start(bf16[64,768]{1,0:T(8,128)(2,1)S(1)} %slice.9), channel_id=1, source_target_pairs={{8,0},{16,8},{24,16},{28,24},{20,28},{12,20},{4,12},{0,4},{9,1},{1... | collective-permute-start | bytes 294920 | tf_op jit(solution)/shard_map/ppermute | solution.py:216
  25.0 15.4 %all-to-all-start = ((bf16[8,24,768]{2,1,0:T(8,128)(2,1)}), bf16[8,24,768]{2,1,0:T(8,128)(2,1)S(1)}, u32[]{:S(2)}, u32[]{:S(2)}) async-start(bf16[8,24,768]{2,1,0:T(8,128)(2,1)} %bitcast.6), calls=%async_computation | async-start | bytes 589824 | tf_op jit(solution)/shard_map/all_to_all | solution.py:182
  45.7 15.0 %all-to-all-start.1 = ((bf16[8,24,768]{2,1,0:T(8,128)(2,1)}), bf16[8,24,768]{2,1,0:T(8,128)(2,1)S(1)}, u32[]{:S(2)}, u32[]{:S(2)}) async-start(bf16[8,24,768]{2,1,0:T(8,128)(2,1)} %bitcast.8), calls=%async_computation.1 | async-start | bytes 589824 | tf_op jit(solution)/shard_map/all_to_all | solution.py:182
  51.7 7.9 %collective-permute-start.14 = (bf16[192,768]{1,0:T(8,128)(2,1)S(1)}, bf16[192,768]{1,0:T(8,128)(2,1)S(1)}, u32[]{:S(2)}, u32[]{:S(2)}) collective-permute-start(bf16[192,768]{1,0:T(8,128)(2,1)S(1)} %bitcast.23), channel_id=1, source_target_pairs={{0,2},{1,3},{2,0},{3,1},{4,6},{5,7},{6,4},{7,5},{8,10},{9,11},{10,... | collective-permute-start | bytes 884744 | tf_op jit(solution)/shard_map/ppermute | solution.py:178
  53.2 9.6 %collective-permute-start.16 = (bf16[192,768]{1,0:T(8,128)(2,1)S(1)}, bf16[192,768]{1,0:T(8,128)(2,1)S(1)}, u32[]{:S(2)}, u32[]{:S(2)}) collective-permute-start(bf16[192,768]{1,0:T(8,128)(2,1)S(1)} %bitcast.24), channel_id=1, source_target_pairs={{0,1},{1,0},{2,3},{3,2},{4,5},{5,4},{6,7},{7,6},{8,9},{9,8},{10,11... | collective-permute-start | bytes 884744 | tf_op jit(solution)/shard_map/ppermute | solution.py:178
  60.8 9.6 %collective-permute-start.19 = (bf16[192,768]{1,0:T(8,128)(2,1)S(1)}, bf16[192,768]{1,0:T(8,128)(2,1)S(1)}, u32[]{:S(2)}, u32[]{:S(2)}) collective-permute-start(bf16[192,768]{1,0:T(8,128)(2,1)S(1)} %collective-permute-done.14.refs_2_.refs_3_), channel_id=1, source_target_pairs={{0,1},{1,0},{2,3},{3,2},{4,5},{5,4},{6,7},{7,6},{8,9},{9,8},{10,11... | collective-permute-start | bytes 884744 | tf_op jit(solution)/shard_map/ppermute | solution.py:178
  61.3 9.0 %collective-permute-start.17 = (bf16[192,768]{1,0:T(8,128)(2,1)S(1)}, bf16[192,768]{1,0:T(8,128)(2,1)S(1)}, u32[]{:S(2)}, u32[]{:S(2)}) collective-permute-start(bf16[192,768]{1,0:T(8,128)(2,1)S(1)} %add.11.refs_1_), channel_id=1, source_target_pairs={{0,2},{1,3},{2,0},{3,1},{4,6},{5,7},{6,4},{7,5},{8,10},{9,11},{10,... | collective-permute-start | bytes 884744 | tf_op jit(solution)/shard_map/ppermute | solution.py:178
  75.8 9.8 %collective-permute-start.22 = (bf16[192,768]{1,0:T(8,128)(2,1)S(1)}, bf16[192,768]{1,0:T(8,128)(2,1)S(1)}, u32[]{:S(2)}, u32[]{:S(2)}) collective-permute-start(bf16[192,768]{1,0:T(8,128)(2,1)S(1)} %get-tuple-element.114.refs_1_), channel_id=1, source_target_pairs={{0,1},{1,0},{2,3},{3,2},{4,5},{5,4},{6,7},{7,6},{8,9},{9,8},{10,11... | collective-permute-start | bytes 884744 | tf_op jit(solution)/shard_map/ppermute | solution.py:178
  77.3 9.1 %collective-permute-start.23 = (bf16[192,768]{1,0:T(8,128)(2,1)S(1)}, bf16[192,768]{1,0:T(8,128)(2,1)S(1)}, u32[]{:S(2)}, u32[]{:S(2)}) collective-permute-start(bf16[192,768]{1,0:T(8,128)(2,1)S(1)} %far.5.refs_5_.refs_1_.refs_4_.refs_3_), channel_id=1, source_target_pairs={{0,2},{1,3},{2,0},{3,1},{4,6},{5,7},{6,4},{7,5},{8,10},{9,11},{10,... | collective-permute-start | bytes 884744 | tf_op jit(solution)/shard_map/ppermute | solution.py:178
  80.8 11.1 %collective-permute-start.21 = (bf16[192,768]{1,0:T(8,128)(2,1)S(1)}, bf16[192,768]{1,0:T(8,128)(2,1)S(1)}, u32[]{:S(2)}, u32[]{:S(2)}) collective-permute-start(bf16[192,768]{1,0:T(8,128)(2,1)S(1)} %get-tuple-element.121), channel_id=1, source_target_pairs={{0,1},{1,0},{2,3},{3,2},{4,5},{5,4},{6,7},{7,6},{8,9},{9,8},{10,11... | collective-permute-start | bytes 884744 | tf_op jit(solution)/shard_map/ppermute | solution.py:178
  87.2 14.2 %all-to-all-start.2 = ((bf16[8,24,768]{2,1,0:T(8,128)(2,1)}), bf16[8,24,768]{2,1,0:T(8,128)(2,1)S(1)}, u32[]{:S(2)}, u32[]{:S(2)}) async-start(bf16[8,24,768]{2,1,0:T(8,128)(2,1)} %bitcast.12), calls=%async_computation.2 | async-start | bytes 589824 | tf_op jit(solution)/shard_map/all_to_all | solution.py:182
  91.8 11.5 %collective-permute-start.26 = (bf16[192,768]{1,0:T(8,128)(2,1)S(1)}, bf16[192,768]{1,0:T(8,128)(2,1)S(1)}, u32[]{:S(2)}, u32[]{:S(2)}) collective-permute-start(bf16[192,768]{1,0:T(8,128)(2,1)S(1)} %get-tuple-element.123.refs_3_), channel_id=1, source_target_pairs={{0,1},{1,0},{2,3},{3,2},{4,5},{5,4},{6,7},{7,6},{8,9},{9,8},{10,11... | collective-permute-start | bytes 884744 | tf_op jit(solution)/shard_map/ppermute | solution.py:178
  91.9 9.5 %collective-permute-start.24 = (bf16[192,768]{1,0:T(8,128)(2,1)S(1)}, bf16[192,768]{1,0:T(8,128)(2,1)S(1)}, u32[]{:S(2)}, u32[]{:S(2)}) collective-permute-start(bf16[192,768]{1,0:T(8,128)(2,1)S(1)} %far.6.refs_5_), channel_id=1, source_target_pairs={{0,2},{1,3},{2,0},{3,1},{4,6},{5,7},{6,4},{7,5},{8,10},{9,11},{10,... | collective-permute-start | bytes 884744 | tf_op jit(solution)/shard_map/ppermute | solution.py:178
  101.8 8.4 %collective-permute-start.25 = (bf16[128,768]{1,0:T(8,128)(2,1)S(1)}, bf16[128,768]{1,0:T(8,128)(2,1)S(1)}, u32[]{:S(2)}, u32[]{:S(2)}) collective-permute-start(bf16[128,768]{1,0:T(8,128)(2,1)S(1)} %get-tuple-element.137.refs_1_), channel_id=1, source_target_pairs={{0,2},{1,3},{2,0},{3,1},{4,6},{5,7},{6,4},{7,5},{8,10},{9,11},{10,... | collective-permute-start | bytes 589832 | tf_op jit(solution)/shard_map/ppermute | solution.py:178
  104.2 17.4 %all-to-all-start.3 = ((bf16[8,24,768]{2,1,0:T(8,128)(2,1)}), bf16[8,24,768]{2,1,0:T(8,128)(2,1)S(1)}, u32[]{:S(2)}, u32[]{:S(2)}) async-start(bf16[8,24,768]{2,1,0:T(8,128)(2,1)} %bitcast.14), calls=%async_computation.3 | async-start | bytes 589824 | tf_op jit(solution)/shard_map/all_to_all | solution.py:182
  125.2 17.8 %collective-permute-start.29 = (bf16[128,768]{1,0:T(8,128)(2,1)S(1)}, bf16[128,768]{1,0:T(8,128)(2,1)S(1)}, u32[]{:S(2)}, u32[]{:S(2)}) collective-permute-start(bf16[128,768]{1,0:T(8,128)(2,1)S(1)} %get-tuple-element.152.refs_3_), channel_id=1, source_target_pairs={{0,1},{1,0},{2,3},{3,2},{4,5},{5,4},{6,7},{7,6},{8,9},{9,8},{10,11... | collective-permute-start | bytes 589832 | tf_op jit(solution)/shard_map/ppermute | solution.py:178
  128.0 7.5 %collective-permute-start.39 = (f32[8,16,96]{2,1,0:T(8,128)S(1)}, f32[8,16,96]{2,1,0:T(8,128)S(1)}, u32[]{:S(2)}, u32[]{:S(2)}) collective-permute-start(f32[8,16,96]{2,1,0:T(8,128)S(1)} %add.14.refs_4_.refs_0_), channel_id=1, source_target_pairs={{0,2},{1,3},{2,0},{3,1},{4,6},{5,7},{6,4},{7,5},{8,10},{9,11},{10,... | collective-permute-start | bytes 147464 | tf_op jit(solution)/shard_map/ppermute | solution.py:178
  129.5 13.5 %collective-permute-start.33 = (bf16[128,768]{1,0:T(8,128)(2,1)S(1)}, bf16[128,768]{1,0:T(8,128)(2,1)S(1)}, u32[]{:S(2)}, u32[]{:S(2)}) collective-permute-start(bf16[128,768]{1,0:T(8,128)(2,1)S(1)} %far.7.refs_3_), channel_id=1, source_target_pairs={{0,2},{1,3},{2,0},{3,1},{4,6},{5,7},{6,4},{7,5},{8,10},{9,11},{10,... | collective-permute-start | bytes 589832 | tf_op jit(solution)/shard_map/ppermute | solution.py:178
  133.5 7.3 %collective-permute-start.37 = (bf16[96,768]{1,0:T(8,128)(2,1)S(1)}, bf16[96,768]{1,0:T(8,128)(2,1)S(1)}, u32[]{:S(2)}, u32[]{:S(2)}) collective-permute-start(bf16[96,768]{1,0:T(8,128)(2,1)S(1)} %get-tuple-element.163), channel_id=1, source_target_pairs={{0,8},{8,16},{16,24},{24,28},{28,20},{20,12},{12,4},{4,0},{1,9},{9... | collective-permute-start | bytes 442376 | tf_op jit(solution)/shard_map/ppermute | solution.py:265
  136.2 11.5 %all-to-all-start.4 = ((f32[8,16,96]{2,1,0:T(8,128)}), f32[8,16,96]{2,1,0:T(8,128)S(1)}, u32[]{:S(2)}, u32[]{:S(2)}) async-start(f32[8,16,96]{2,1,0:T(8,128)} %add.15.refs_3_), calls=%async_computation.4 | async-start | bytes 131072 | tf_op jit(solution)/shard_map/all_to_all | solution.py:182
  (29 other events, 149.6 us)

commit v5 on v4

--- a/solution.py
+++ b/solution.py
@@ -64,7 +64,7 @@
             self.copy.start()
 
 
-def kernel_call(body, outs, name, fetch=(), store=(), smem=(), time=1, limit=24, scratch=(), raw=(), alias=(), wait=(), wait_hbm=(), first=99):
+def kernel_call(body, outs, name, fetch=(), store=(), smem=(), time=1, limit=24, scratch=(), wait=(), wait_hbm=(), first=99):
     def call(*operands):
         n_in, n_out, n_scratch = len(operands), len(outs), len(scratch)
         held = [pltpu.VMEM(operands[i].shape, operands[i].dtype) for i in fetch]
@@ -98,7 +98,6 @@
         def spec(i, hbm):
             return pl.BlockSpec(memory_space=pltpu.HBM if i in hbm else pltpu.VMEM)
 
-        kept = (*store, *raw)
 
         operands = [
             pltpu.with_memory_space_constraint(x, pltpu.HBM) if i in fetch else x
@@ -107,7 +106,7 @@
         return pl.pallas_call(
             kernel,
             out_shape=[
-                pltpu.HBM(*outs[i]) if i in kept else jax.ShapeDtypeStruct(*outs[i])
+                pltpu.HBM(*outs[i]) if i in store else jax.ShapeDtypeStruct(*outs[i])
                 for i in range(n_out)
             ],
             in_specs=[
@@ -116,8 +115,7 @@
             ]
             + [pl.BlockSpec(memory_space=pl.ANY) for _ in wait]
             + [pl.BlockSpec(memory_space=pltpu.HBM) for _ in wait_hbm],
-            out_specs=[spec(i, kept) for i in range(n_out)],
-            input_output_aliases=dict(alias),
+            out_specs=[spec(i, store) for i in range(n_out)],
             scratch_shapes=[*scratch, *held, *sems],
             compiler_params=pltpu.CompilerParams(vmem_limit_bytes=limit * MIB),
             cost_estimate=pl.CostEstimate(
@@ -180,9 +178,6 @@
 
 def exchange(buffer):
     return lax.all_to_all(buffer, "dp", split_axis=0, concat_axis=0, tiled=True)
-
-
-OFFSETS = (0, 2, 1, 3)
 
 
 def swap_far(rows):
@@ -333,22 +328,16 @@
         small_out[:, d * shard : (d + 1) * shard] = smalls[d]
 
 
-def finish(count, scalars, blocks, weights_out, sem):
-    weights = blocks[0]
+def finish(count, scalars, blocks, weights):
     shard = weights.shape[0] // count
+    weights[...] = blocks[0][...]
     top, bottom = blocks[2:]
     source = ring_source(ring_place(scalars[0], count) + count // 2, count)
     middle = top.shape[0]
     start = pl.multiple_of(source * shard, 16)
     rest = shard - middle
-    weights.wait()
-    weights.held[pl.ds(start, middle), :] = top[...]
-    weights.held[pl.ds(pl.multiple_of(start + middle, 16), rest), :] = bottom[0:rest, :]
-    copy = pltpu.make_async_copy(
-        weights.held.at[pl.ds(start, shard), :], weights_out.at[pl.ds(start, shard), :], sem
-    )
-    copy.start()
-    return copy
+    weights[pl.ds(start, middle), :] = top[...]
+    weights[pl.ds(pl.multiple_of(start + middle, 16), rest), :] = bottom[0:rest, :]
 
 
 def positions_of(piece, rows, shape, dim):
@@ -363,14 +352,12 @@
     given = 4 if has_blocks else 2
     blocks = refs[5 : 5 + given]
     outs = refs[5 + given :]
-    heads = len(outs) - (12 if has_blocks else 8)
+    heads = len(outs) - (11 if has_blocks else 8)
     keep, keep_far, send, send_far, ones, qkv_out, attended, group = outs[:8]
     probs_out = outs[8 : 8 + heads]
-    copy = None
     if has_blocks:
-        weights_out, small_out, smalls, sem = outs[8 + heads :]
-        finish_small(count, scalars, blocks, smalls, small_out)
-        weights, small = blocks[0], small_out
+        weights, small, smalls = outs[8 + heads :]
+        finish_small(count, scalars, blocks, smalls, small)
     else:
         weights, small = blocks
     rows = tokens.shape[0]
@@ -384,7 +371,7 @@
         values = ref[...].astype(FULL)
         ones[index * rows : (index + 1) * rows, :] = (values * root_of(values) * gain).astype(LOW)
     if has_blocks:
-        copy = finish(count, scalars, blocks, weights_out, sem)
+        finish(count, scalars, blocks, weights)
     qkv = dot(ones[...], weights[:, 0 : 3 * local]).astype(LOW)
     qkv_out[...] = qkv
     qkv_out.flush()
@@ -413,8 +400,6 @@
     keep_far[...] = dot_nt(attended[rows : 2 * rows, :], w_out_t)
     send[...] = dot_nt(attended[2 * rows : 3 * rows, :], w_out_t).astype(LOW)
     send_far[...] = dot_nt(attended[3 * rows :, :], w_out_t).astype(LOW)
-    if copy is not None:
-        copy.wait()
 
 
 def middle_kernel(gain_row, tokens, keep, near, far, small, spread, middle, rows):
@@ -541,18 +526,20 @@
     far,
     near,
     near_far,
+    attended,
     weights,
     qkv,
     *refs,
 ):
-    probs, (attended, ones, grads) = refs[:heads], refs[heads : heads + 3]
-    *ring_rows, grad_w, joined, flipped = refs[heads + 3 :]
+    probs, (ones, grads) = refs[:heads], refs[heads : heads + 2]
+    *ring_rows, grad_w, joined, flipped = refs[heads + 2 :]
     rows = own.shape[0]
     local = attended.shape[1]
     joined[0:rows, :] = own[...]
     joined[rows : 2 * rows, :] = far[...]
     joined[2 * rows : 3 * rows, :] = near[...]
     joined[3 * rows :, :] = near_far[...]
+    grad_w[:, 3 * local :] = dot_tn(joined[...], attended[...]).astype(LOW)
     w_out_t = weights[:, 3 * local :]
     grad_attended = dot(joined[...], w_out_t).astype(LOW)
     for h in range(heads):
@@ -570,7 +557,6 @@
         flipped[at : at + HEAD_DIM, :] = dot_tn(q, grad_s) * SCALE
         flipped[local + at : local + at + HEAD_DIM, :] = dot_tn(upstream, low)
     grads[:, local:] = flipped[...].T.astype(LOW)
-    grad_w[:, 3 * local :] = dot_tn(joined[...], attended[...]).astype(LOW)
     grad_w[:, 0 : 3 * local] = dot_tn(ones[...], grads[...]).astype(LOW)
     if ring_rows:
         top, bottom, rest = ring_rows
@@ -754,16 +740,15 @@
             [((width, 4 * local), LOW), ((owners, small_rows, shard), FULL)],
             "assemble",
             smem=(0,),
-            store=(0,),
         )(scalars, packed, *behind, *ahead)
         blocks = [*partial, top, bottom]
-        early = behind[0]
-        scratch = [pltpu.VMEM((owners, small_rows, shard), FULL), pltpu.SemaphoreType.DMA]
+        early, late = behind[0], (ahead[-1], behind[-1])
+        scratch = [pltpu.VMEM((owners, small_rows, shard), FULL)]
     else:
         gathered = lax.all_gather(packed, "dp", axis=0, tiled=False)
         flat = gathered[:, shard:, :shard].transpose(1, 0, 2).reshape(small_rows, width)
         blocks = [gathered[:, :shard].reshape(width, 4 * local), flat.astype(FULL)]
-        early = packed
+        early, late = packed, (blocks[1],)
     token_far = swap_far(tokens)
     token_near = swap_near(tokens)
 
@@ -779,7 +764,7 @@
     )(scalars, routes, cotangent)
     token_near_far = swap_near(token_far)
 
-    cot_rows = add(cot_rows, wait=(blocks[1],))
+    cot_rows = add(cot_rows, wait=late)
     cot_own = exchange(cot_rows.reshape(experts, capacity, width))
     cot_own = cot_own.reshape(slots, width)
 
@@ -794,19 +779,15 @@
         ((total_rows, width), LOW),
     ]
     outs += [((total_rows, total_rows), LOW)] * heads
-    raw, alias, fetch = [], {}, [1]
     if has_blocks:
         outs += [((width, 4 * local), LOW), ((small_rows, width), FULL)]
-        raw, alias, fetch = [len(outs) - 2], {5: len(outs) - 2}, [1, 5]
     made = kernel_call(
         functools.partial(attend_kernel, owners, sequences, has_blocks),
         outs,
         "attend",
         smem=(0,),
-        fetch=fetch,
+        fetch=(1,),
         store=(5, *range(8, 8 + heads)),
-        raw=raw,
-        alias=alias,
         scratch=scratch,
         time=4,
     )(scalars, tokens, token_far, token_near, token_near_far, *blocks)
@@ -824,7 +805,9 @@
 
     near, far, mark = scatter(keep_far, send, send_far)
     small_now = small
-    ones, attended, group, small = save(ones, attended, group, small, wait=(mark,))
+    ones, attended, group, small, weights = save(
+        ones, attended, group, small, weights, wait=(mark,)
+    )
     tokens_here, spread_here = load(tokens, spread, wait=(mark, cot_own))
     middle, own_rows = kernel_call(
         functools.partial(middle_kernel, experts + 1),
@@ -945,12 +928,12 @@
         "attend_back",
         smem=(0,),
         fetch=range(5, 9 + heads),
-        first=2 + heads,
+        first=3 + heads,
         time=2,
         scratch=scratch,
     )(
         *(scalars, grad_low, grad_far, grad_near, grad_near_far),
-        *(weights, qkv, *probs, attended, ones),
+        *(attended, weights, qkv, *probs, ones),
     )
     last = [((shard, local), FULL)] * 3 + [((local, shard), FULL)]
     held = {}

time: 150 us -> 149 us (level)
  no operation moved by 1% of the time
where the time goes in v5:
time: 149 us; the launch traced here: 148 us
  starting transfers between devices  62 us (42%)
  Pallas kernels  53.5 us (36%)
  waiting for transfers between devices  29.3 us (20%)
  local copies, waits for them, and re-layouts  2.16 us (1%)
    pallas_call x34, Pallas kernels, call(): pl.pallas_call(kernel, out_shape=[pltpu.HBM(*outs[i]) if i in store else...  45 us
    all_to_all x5, starting transfers between devices, exchange(): return lax.all_to_all(buffer, 'dp', split_axis=0, concat_axis=0, tiled=True)  27.1 us
    ppermute x26, starting transfers between devices, swap(): return lax.ppermute(values, axis, [(i, i ^ bit) for i in range(count)])  17.1 us
    ppermute x26, waiting for transfers between devices, swap(): return lax.ppermute(values, axis, [(i, i ^ bit) for i in range(count)])  17 us
    pallas_call x8, Pallas kernels, moved(): pl.pallas_call(functools.partial(move_kernel, len(kinds)), out_shape=[plt...  8.53 us
    ppermute x3, starting transfers between devices, ring_gather(): behind.append(lax.ppermute(behind[-1], 'dp', right))  6.57 us
    ppermute x3, waiting for transfers between devices, ring_gather(): behind.append(lax.ppermute(behind[-1], 'dp', right))  5.35 us
    ppermute x3, starting transfers between devices, ring_reduce(): ahead = lax.ppermute(to_right, 'dp', right)  5.09 us
  transfers between devices with their start and end apart: 47, of which 19 were waited for; matrix products, arithmetic and copies ran while one was open for 1% of the time, Pallas kernels for 32%

profile of v5, /device:TPU:0, one launch (start us, length us, event | category | flops | bytes accessed | tf_op | source)
XLA Modules:
  0.0 148.3 jit_solution(7729692523294334614)
XLA Ops:
  1.9 3.1 %collective-permute-start = (bf16[112,768]{1,0:T(8,128)(2,1)S(1)}, bf16[112,768]{1,0:T(8,128)(2,1)S(1)}, u32[]{:S(2)}, u32[]{:S(2)}) collective-permute-start(bf16[112,768]{1,0:T(8,128)(2,1)S(1)} %pack.1.refs_1_), channel_id=1, source_target_pairs={{0,8},{8,16},{16,24},{24,28},{28,20},{20,12},{12,4},{4,0},{1,9},{9... | collective-permute-start | bytes 516104 | tf_op jit(solution)/shard_map/ppermute | solution.py:207
  5.0 2.0 %collective-permute-start.1 = (bf16[128,768]{1,0:T(8,128)(2,1)S(1)}, bf16[128,768]{1,0:T(8,128)(2,1)S(1)}, u32[]{:S(2)}, u32[]{:S(2)}) collective-permute-start(bf16[128,768]{1,0:T(8,128)(2,1)S(1)} %copy-done.3), channel_id=1, source_target_pairs={{0,2},{1,3},{2,0},{3,1},{4,6},{5,7},{6,4},{7,5},{8,10},{9,11},{10,... | collective-permute-start | bytes 589832 | tf_op jit(solution)/shard_map/ppermute | solution.py:176
  6.9 2.3 %collective-permute-done.refs_3_.refs_2_ = bf16[112,768]{1,0:T(8,128)(2,1)S(1)} collective-permute-done((bf16[112,768]{1,0:T(8,128)(2,1)S(1)}, bf16[112,768]{1,0:T(8,128)(2,1)S(1)}, u32[]{:S(2)}, u32[]{:S(2)}) %collective-permute-start) | collective-permute-done | bytes 172064 | tf_op jit(solution)/shard_map/ppermute | solution.py:207
  12.7 2.1 %collective-permute-done.4.refs_3_ = bf16[112,768]{1,0:T(8,128)(2,1)S(1)} collective-permute-done((bf16[112,768]{1,0:T(8,128)(2,1)S(1)}, bf16[112,768]{1,0:T(8,128)(2,1)S(1)}, u32[]{:S(2)}, u32[]{:S(2)}) %collective-permute-start.4) | collective-permute-done | bytes 172064 | tf_op jit(solution)/shard_map/ppermute | solution.py:207
  16.8 2.5 %spread.1 = (bf16[128,192]{1,0:T(8,128)(2,1)}, bf16[192,768]{1,0:T(8,128)(2,1)S(1)}) custom-call(s32[5]{0:T(128)S(1)} %pad_add_fusion.refs_0_, s32[512,1]{1,0:T(8,128)} %copy.24.refs_1_, bf16[128,768]{1,0:T(8,128)(2,1)} %refs_1_.6, bf16[112,768]{1,0:T(8,128)(2,1)S(1)} %collective-permute-done.refs_3_.refs_2_), custom_call_target="tpu_custom_call" | custom-call | flops 2200000000 | bytes 1048576 | tf_op jit(solution)/shard_map/spread/pallas_call | solution.py:106
  23.4 5.9 %all-to-all-start = ((bf16[8,24,768]{2,1,0:T(8,128)(2,1)}), bf16[8,24,768]{2,1,0:T(8,128)(2,1)S(1)}, u32[]{:S(2)}, u32[]{:S(2)}) async-start(bf16[8,24,768]{2,1,0:T(8,128)(2,1)} %bitcast.6), calls=%async_computation | async-start | bytes 589824 | tf_op jit(solution)/shard_map/all_to_all | solution.py:180
  29.9 5.6 %attend.1 = (f32[128,768]{1,0:T(8,128)S(1)}, f32[128,768]{1,0:T(8,128)S(1)}, bf16[128,768]{1,0:T(8,128)(2,1)S(1)}, bf16[128,768]{1,0:T(8,128)(2,1)S(1)}, bf16[51...) custom-call(s32[5]{0:T(128)S(1)} %pad_add_fusion.refs_0_, ...), custom_call_target="tpu_custom_call" | custom-call | flops 4400000000 | bytes 1048576 | tf_op jit(solution)/shard_map/attend/pallas_call | solution.py:106
  41.3 2.7 %collective-permute-done.13.refs_3_ = bf16[128,768]{1,0:T(8,128)(2,1)S(1)} collective-permute-done((bf16[128,768]{1,0:T(8,128)(2,1)S(1)}, bf16[128,768]{1,0:T(8,128)(2,1)S(1)}, u32[]{:S(2)}, u32[]{:S(2)}) %collective-permute-start.13) | collective-permute-done | bytes 196640 | tf_op jit(solution)/shard_map/ppermute | solution.py:176
  45.2 6.0 %all-to-all-start.1 = ((bf16[8,24,768]{2,1,0:T(8,128)(2,1)}), bf16[8,24,768]{2,1,0:T(8,128)(2,1)S(1)}, u32[]{:S(2)}, u32[]{:S(2)}) async-start(bf16[8,24,768]{2,1,0:T(8,128)(2,1)} %bitcast.8), calls=%async_computation.1 | async-start | bytes 589824 | tf_op jit(solution)/shard_map/all_to_all | solution.py:180
  54.3 4.8 %collective-permute-done.14.refs_2_.refs_3_ = bf16[192,768]{1,0:T(8,128)(2,1)S(1)} collective-permute-done((bf16[192,768]{1,0:T(8,128)(2,1)S(1)}, bf16[192,768]{1,0:T(8,128)(2,1)S(1)}, u32[]{:S(2)}, u32[]{:S(2)}) %collective-permute-start.14) | collective-permute-done | bytes 294944 | tf_op jit(solution)/shard_map/ppermute | solution.py:176
  63.7 4.6 %expert.2 = (f32[192,768]{1,0:T(8,128)}, bf16[192,768]{1,0:T(8,128)(2,1)S(1)}, bf16[384,768]{1,0:T(8,128)(2,1)S(1)}, bf16[384,768]{1,0:T(8,128)(2,1)}, bf16[384,...) custom-call(s32[5]{0:T(128)S(1)} %pad_add_fusion.refs_0_, ...), custom_call_target="tpu_custom_call" | custom-call | flops 4400000000 | bytes 1048576 | tf_op jit(solution)/shard_map/expert/pallas_call | solution.py:106
  71.5 3.6 %expert.3 = (f32[192,768]{1,0:T(8,128)S(1)}, bf16[192,768]{1,0:T(8,128)(2,1)S(1)}, bf16[384,768]{1,0:T(8,128)(2,1)S(1)}, bf16[384,768]{1,0:T(8,128)(2,1)S(1)}, b...) custom-call(s32[5]{0:T(128)S(1)} %pad_add_fusion.refs_0_, ...), custom_call_target="tpu_custom_call" | custom-call | flops 4400000000 | bytes 1048576 | tf_op jit(solution)/shard_map/expert/pallas_call | solution.py:106
  80.4 2.5 %grad_out.1.refs_4_ = f32[1,768,768]{2,1,0:T(8,128)} custom-call(bf16[384,768]{1,0:T(8,128)(2,1)S(1)} %get-tuple-element.114.refs_0_, bf16[384,768]{1,0:T(8,128)(2,1)S(1)} %get-tuple-element.117.refs_2_.refs_1_, bf16[384,768]{1,0:T(8,128)(2,1)S(1)} %get-tuple-element.126.refs_2_, bf16[384,768]{1,0:T(8,128)(2,1)S(1)} %get-tuple-element.127.refs_3_, ...), custom_call_target="tpu_custom_call" | custom-call | flops 3300000000 | bytes 1048576 | tf_op jit(solution)/shard_map/grad_out/pallas_call | solution.py:106
  86.8 4.6 %all-to-all-start.2 = ((bf16[8,24,768]{2,1,0:T(8,128)(2,1)}), bf16[8,24,768]{2,1,0:T(8,128)(2,1)S(1)}, u32[]{:S(2)}, u32[]{:S(2)}) async-start(bf16[8,24,768]{2,1,0:T(8,128)(2,1)} %bitcast.12), calls=%async_computation.2 | async-start | bytes 589824 | tf_op jit(solution)/shard_map/all_to_all | solution.py:180
  93.0 4.2 %grad_in.1.refs_6_ = f32[1,768,768]{2,1,0:T(8,128)} custom-call(bf16[384,768]{1,0:T(8,128)(2,1)} %get-tuple-element.136.refs_0_, bf16[384,768]{1,0:T(8,128)(2,1)} %get-tuple-element.137.refs_1_, bf16[384,768]{1,0:T(8,128)(2,1)} %get-tuple-element.138.refs_2_, bf16[384,768]{1,0:T(8,128)(2,1)} %get-tuple-element.131.refs_5_.refs_3_), custom_call_target="tpu_custom_call" | custom-call | flops 3300000000 | bytes 1048576 | tf_op jit(solution)/shard_map/grad_in/pallas_call | solution.py:106
  98.6 2.3 %collective-permute-done.24.refs_5_.refs_2_ = bf16[192,768]{1,0:T(8,128)(2,1)S(1)} collective-permute-done((bf16[192,768]{1,0:T(8,128)(2,1)S(1)}, bf16[192,768]{1,0:T(8,128)(2,1)S(1)}, u32[]{:S(2)}, u32[]{:S(2)}) %collective-permute-start.24) | collective-permute-done | bytes 294944 | tf_op jit(solution)/shard_map/ppermute | solution.py:176
  103.7 6.0 %all-to-all-start.3 = ((bf16[8,24,768]{2,1,0:T(8,128)(2,1)}), bf16[8,24,768]{2,1,0:T(8,128)(2,1)S(1)}, u32[]{:S(2)}, u32[]{:S(2)}) async-start(bf16[8,24,768]{2,1,0:T(8,128)(2,1)} %bitcast.14), calls=%async_computation.3 | async-start | bytes 589824 | tf_op jit(solution)/shard_map/all_to_all | solution.py:180
  111.4 7.0 %attend_back.1 = (bf16[512,576]{1,0:T(8,128)(2,1)S(1)}, bf16[48,768]{1,0:T(8,128)(2,1)S(1)}, bf16[48,768]{1,0:T(8,128)(2,1)S(1)}, bf16[672,768]{1,0:T(8,128)(2,1)S(1)}) custom-call(s32[5]{0:T(128)S(1)} %pad_add_fusion.refs_0_, bf16[128,768]{1,0:T(8,128)(2,1)S(1)} %get-tuple-element.139.refs_1_, bf16[128,768]{1,0:T(8,128)(2,1)S(1)} %add.13.refs_2_, ...), custom_call_target="tpu_custom_call" | custom-call | flops 2200000000 | bytes 1048576 | tf_op jit(solution)/shard_map/attend_back/pallas_call | solution.py:106
  118.4 2.1 %collective-permute-start.31 = (bf16[48,768]{1,0:T(8,128)(2,1)S(1)}, bf16[48,768]{1,0:T(8,128)(2,1)S(1)}, u32[]{:S(2)}, u32[]{:S(2)}) collective-permute-start(bf16[48,768]{1,0:T(8,128)(2,1)S(1)} %get-tuple-element.157), channel_id=1, source_target_pairs={{0,8},{8,16},{16,24},{24,28},{28,20},{20,12},{12,4},{4,0},{1,9},{9... | collective-permute-start | bytes 221192 | tf_op jit(solution)/shard_map/ppermute | solution.py:244
  120.6 3.1 %grad_one.1 = (f32[128,768]{1,0:T(8,128)}, f32[128,768]{1,0:T(8,128)S(1)}, bf16[128,768]{1,0:T(8,128)(2,1)S(1)}, bf16[128,768]{1,0:T(8,128)(2,1)S(1)}, f32[8,16,96]{2,1,0:T(8,128)S(1)}) custom-call(bf16[512,576]{1,0:T(8,128)(2,1)S(1)} %get-tuple-element.147.refs_0_, bf16[768,768]{1,0:T(8,128)(2,1)} %get-tuple-element.142.refs_6_.refs_1_, ...), custom_call_target="tpu_custom_call" | custom-call | flops 220000000 | bytes 1048576 | tf_op jit(solution)/shard_map/grad_one/pallas_call | solution.py:106
  135.2 4.5 %all-to-all-start.4 = ((f32[8,16,96]{2,1,0:T(8,128)}), f32[8,16,96]{2,1,0:T(8,128)S(1)}, u32[]{:S(2)}, u32[]{:S(2)}) async-start(f32[8,16,96]{2,1,0:T(8,128)} %add.15.refs_3_), calls=%async_computation.4 | async-start | bytes 131072 | tf_op jit(solution)/shard_map/all_to_all | solution.py:180
  139.9 2.1 %collective-permute-start.40 = (bf16[96,768]{1,0:T(8,128)(2,1)S(1)}, bf16[96,768]{1,0:T(8,128)(2,1)S(1)}, u32[]{:S(2)}, u32[]{:S(2)}) collective-permute-start(bf16[96,768]{1,0:T(8,128)(2,1)S(1)} %get-tuple-element.170), channel_id=1, source_target_pairs={{0,8},{8,16},{16,24},{24,28},{28,20},{20,12},{12,4},{4,0},{1,9},{9... | collective-permute-start | bytes 442376 | tf_op jit(solution)/shard_map/ppermute | solution.py:260
  142.0 2.3 %last.1 = (f32[128,768]{1,0:T(8,128)}, bf16[128,768]{1,0:T(8,128)(2,1)}) custom-call(bf16[128,768]{1,0:T(8,128)(2,1)} %refs_0_.5, f32[128,768]{1,0:T(8,128)} %get-tuple-element.153.refs_1_, bf16[128,768]{1,0:T(8,128)(2,1)S(1)} %collective-permute-done.29.refs_2_, bf16[128,768]{1,0:T(8,128)(2,1)S(1)} %collective-permute-done.33.refs_1_.refs_3_, ...), custom_call_target="tpu_custom_call" | custom-call | flops 330000000 | bytes 1048576 | tf_op jit(solution)/shard_map/last/pallas_call | solution.py:106
  144.4 2.3 %all-to-all-done.4.refs_3_ = f32[8,16,96]{2,1,0:T(8,128)S(1)} async-done(((f32[8,16,96]{2,1,0:T(8,128)}), f32[8,16,96]{2,1,0:T(8,128)S(1)}, u32[]{:S(2)}, u32[]{:S(2)}) %all-to-all-start.4) | async-done | bytes 49184 | tf_op jit(solution)/shard_map/all_to_all | solution.py:180
  (128 shorter events, 58.8 us)
Async XLA Ops:
  1.9 7.4 %collective-permute-start = (bf16[112,768]{1,0:T(8,128)(2,1)S(1)}, bf16[112,768]{1,0:T(8,128)(2,1)S(1)}, u32[]{:S(2)}, u32[]{:S(2)}) collective-permute-start(bf16[112,768]{1,0:T(8,128)(2,1)S(1)} %pack.1.refs_1_), channel_id=1, source_target_pairs={{0,8},{8,16},{16,24},{24,28},{28,20},{20,12},{12,4},{4,0},{1,9},{9... | collective-permute-start | bytes 516104 | tf_op jit(solution)/shard_map/ppermute | solution.py:207
  5.0 7.3 %collective-permute-start.1 = (bf16[128,768]{1,0:T(8,128)(2,1)S(1)}, bf16[128,768]{1,0:T(8,128)(2,1)S(1)}, u32[]{:S(2)}, u32[]{:S(2)}) collective-permute-start(bf16[128,768]{1,0:T(8,128)(2,1)S(1)} %copy-done.3), channel_id=1, source_target_pairs={{0,2},{1,3},{2,0},{3,1},{4,6},{5,7},{6,4},{7,5},{8,10},{9,11},{10,... | collective-permute-start | bytes 589832 | tf_op jit(solution)/shard_map/ppermute | solution.py:176
  11.3 18.6 %collective-permute-start.2 = (bf16[128,768]{1,0:T(8,128)(2,1)S(1)}, bf16[128,768]{1,0:T(8,128)(2,1)S(1)}, u32[]{:S(2)}, u32[]{:S(2)}) collective-permute-start(bf16[128,768]{1,0:T(8,128)(2,1)S(1)} %copy-done.3), channel_id=1, source_target_pairs={{0,1},{1,0},{2,3},{3,2},{4,5},{5,4},{6,7},{7,6},{8,9},{9,8},{10,11... | collective-permute-start | bytes 589832 | tf_op jit(solution)/shard_map/ppermute | solution.py:176
  12.2 17.7 %collective-permute-start.3 = (bf16[128,768]{1,0:T(8,128)(2,1)S(1)}, bf16[128,768]{1,0:T(8,128)(2,1)S(1)}, u32[]{:S(2)}, u32[]{:S(2)}) collective-permute-start(bf16[128,768]{1,0:T(8,128)(2,1)S(1)} %collective-permute-done.1.refs_2_), channel_id=1, source_target_pairs={{0,1},{1,0},{2,3},{3,2},{4,5},{5,4},{6,7},{7,6},{8,9},{9,8},{10,11... | collective-permute-start | bytes 589832 | tf_op jit(solution)/shard_map/ppermute | solution.py:176
  20.3 9.6 %collective-permute-start.9 = (bf16[48,768]{1,0:T(8,128)(2,1)S(1)}, bf16[48,768]{1,0:T(8,128)(2,1)S(1)}, u32[]{:S(2)}, u32[]{:S(2)}) collective-permute-start(bf16[48,768]{1,0:T(8,128)(2,1)S(1)} %slice.8), channel_id=1, source_target_pairs={{0,8},{8,16},{16,24},{24,28},{28,20},{20,12},{12,4},{4,0},{1,9},{9... | collective-permute-start | bytes 221192 | tf_op jit(solution)/shard_map/ppermute | solution.py:210
  22.2 7.7 %collective-permute-start.10 = (bf16[64,768]{1,0:T(8,128)(2,1)S(1)}, bf16[64,768]{1,0:T(8,128)(2,1)S(1)}, u32[]{:S(2)}, u32[]{:S(2)}) collective-permute-start(bf16[64,768]{1,0:T(8,128)(2,1)S(1)} %slice.9), channel_id=1, source_target_pairs={{8,0},{16,8},{24,16},{28,24},{20,28},{12,20},{4,12},{0,4},{9,1},{1... | collective-permute-start | bytes 294920 | tf_op jit(solution)/shard_map/ppermute | solution.py:211
  23.4 17.0 %all-to-all-start = ((bf16[8,24,768]{2,1,0:T(8,128)(2,1)}), bf16[8,24,768]{2,1,0:T(8,128)(2,1)S(1)}, u32[]{:S(2)}, u32[]{:S(2)}) async-start(bf16[8,24,768]{2,1,0:T(8,128)(2,1)} %bitcast.6), calls=%async_computation | async-start | bytes 589824 | tf_op jit(solution)/shard_map/all_to_all | solution.py:180
  45.2 15.0 %all-to-all-start.1 = ((bf16[8,24,768]{2,1,0:T(8,128)(2,1)}), bf16[8,24,768]{2,1,0:T(8,128)(2,1)S(1)}, u32[]{:S(2)}, u32[]{:S(2)}) async-start(bf16[8,24,768]{2,1,0:T(8,128)(2,1)} %bitcast.8), calls=%async_computation.1 | async-start | bytes 589824 | tf_op jit(solution)/shard_map/all_to_all | solution.py:180
  51.2 7.9 %collective-permute-start.14 = (bf16[192,768]{1,0:T(8,128)(2,1)S(1)}, bf16[192,768]{1,0:T(8,128)(2,1)S(1)}, u32[]{:S(2)}, u32[]{:S(2)}) collective-permute-start(bf16[192,768]{1,0:T(8,128)(2,1)S(1)} %bitcast.23), channel_id=1, source_target_pairs={{0,2},{1,3},{2,0},{3,1},{4,6},{5,7},{6,4},{7,5},{8,10},{9,11},{10,... | collective-permute-start | bytes 884744 | tf_op jit(solution)/shard_map/ppermute | solution.py:176
  52.7 9.6 %collective-permute-start.16 = (bf16[192,768]{1,0:T(8,128)(2,1)S(1)}, bf16[192,768]{1,0:T(8,128)(2,1)S(1)}, u32[]{:S(2)}, u32[]{:S(2)}) collective-permute-start(bf16[192,768]{1,0:T(8,128)(2,1)S(1)} %bitcast.24), channel_id=1, source_target_pairs={{0,1},{1,0},{2,3},{3,2},{4,5},{5,4},{6,7},{7,6},{8,9},{9,8},{10,11... | collective-permute-start | bytes 884744 | tf_op jit(solution)/shard_map/ppermute | solution.py:176
  60.3 9.6 %collective-permute-start.19 = (bf16[192,768]{1,0:T(8,128)(2,1)S(1)}, bf16[192,768]{1,0:T(8,128)(2,1)S(1)}, u32[]{:S(2)}, u32[]{:S(2)}) collective-permute-start(bf16[192,768]{1,0:T(8,128)(2,1)S(1)} %collective-permute-done.14.refs_2_.refs_3_), channel_id=1, source_target_pairs={{0,1},{1,0},{2,3},{3,2},{4,5},{5,4},{6,7},{7,6},{8,9},{9,8},{10,11... | collective-permute-start | bytes 884744 | tf_op jit(solution)/shard_map/ppermute | solution.py:176
  60.8 9.0 %collective-permute-start.17 = (bf16[192,768]{1,0:T(8,128)(2,1)S(1)}, bf16[192,768]{1,0:T(8,128)(2,1)S(1)}, u32[]{:S(2)}, u32[]{:S(2)}) collective-permute-start(bf16[192,768]{1,0:T(8,128)(2,1)S(1)} %add.11.refs_1_), channel_id=1, source_target_pairs={{0,2},{1,3},{2,0},{3,1},{4,6},{5,7},{6,4},{7,5},{8,10},{9,11},{10,... | collective-permute-start | bytes 884744 | tf_op jit(solution)/shard_map/ppermute | solution.py:176
  75.3 9.8 %collective-permute-start.22 = (bf16[192,768]{1,0:T(8,128)(2,1)S(1)}, bf16[192,768]{1,0:T(8,128)(2,1)S(1)}, u32[]{:S(2)}, u32[]{:S(2)}) collective-permute-start(bf16[192,768]{1,0:T(8,128)(2,1)S(1)} %get-tuple-element.116.refs_1_), channel_id=1, source_target_pairs={{0,1},{1,0},{2,3},{3,2},{4,5},{5,4},{6,7},{7,6},{8,9},{9,8},{10,11... | collective-permute-start | bytes 884744 | tf_op jit(solution)/shard_map/ppermute | solution.py:176
  76.8 9.1 %collective-permute-start.23 = (bf16[192,768]{1,0:T(8,128)(2,1)S(1)}, bf16[192,768]{1,0:T(8,128)(2,1)S(1)}, u32[]{:S(2)}, u32[]{:S(2)}) collective-permute-start(bf16[192,768]{1,0:T(8,128)(2,1)S(1)} %far.5.refs_5_.refs_1_.refs_4_.refs_3_), channel_id=1, source_target_pairs={{0,2},{1,3},{2,0},{3,1},{4,6},{5,7},{6,4},{7,5},{8,10},{9,11},{10,... | collective-permute-start | bytes 884744 | tf_op jit(solution)/shard_map/ppermute | solution.py:176
  80.3 11.1 %collective-permute-start.21 = (bf16[192,768]{1,0:T(8,128)(2,1)S(1)}, bf16[192,768]{1,0:T(8,128)(2,1)S(1)}, u32[]{:S(2)}, u32[]{:S(2)}) collective-permute-start(bf16[192,768]{1,0:T(8,128)(2,1)S(1)} %get-tuple-element.123), channel_id=1, source_target_pairs={{0,1},{1,0},{2,3},{3,2},{4,5},{5,4},{6,7},{7,6},{8,9},{9,8},{10,11... | collective-permute-start | bytes 884744 | tf_op jit(solution)/shard_map/ppermute | solution.py:176
  86.8 14.2 %all-to-all-start.2 = ((bf16[8,24,768]{2,1,0:T(8,128)(2,1)}), bf16[8,24,768]{2,1,0:T(8,128)(2,1)S(1)}, u32[]{:S(2)}, u32[]{:S(2)}) async-start(bf16[8,24,768]{2,1,0:T(8,128)(2,1)} %bitcast.12), calls=%async_computation.2 | async-start | bytes 589824 | tf_op jit(solution)/shard_map/all_to_all | solution.py:180
  91.4 11.5 %collective-permute-start.26 = (bf16[192,768]{1,0:T(8,128)(2,1)S(1)}, bf16[192,768]{1,0:T(8,128)(2,1)S(1)}, u32[]{:S(2)}, u32[]{:S(2)}) collective-permute-start(bf16[192,768]{1,0:T(8,128)(2,1)S(1)} %get-tuple-element.125.refs_3_), channel_id=1, source_target_pairs={{0,1},{1,0},{2,3},{3,2},{4,5},{5,4},{6,7},{7,6},{8,9},{9,8},{10,11... | collective-permute-start | bytes 884744 | tf_op jit(solution)/shard_map/ppermute | solution.py:176
  91.5 9.5 %collective-permute-start.24 = (bf16[192,768]{1,0:T(8,128)(2,1)S(1)}, bf16[192,768]{1,0:T(8,128)(2,1)S(1)}, u32[]{:S(2)}, u32[]{:S(2)}) collective-permute-start(bf16[192,768]{1,0:T(8,128)(2,1)S(1)} %far.6.refs_5_), channel_id=1, source_target_pairs={{0,2},{1,3},{2,0},{3,1},{4,6},{5,7},{6,4},{7,5},{8,10},{9,11},{10,... | collective-permute-start | bytes 884744 | tf_op jit(solution)/shard_map/ppermute | solution.py:176
  101.3 8.4 %collective-permute-start.25 = (bf16[128,768]{1,0:T(8,128)(2,1)S(1)}, bf16[128,768]{1,0:T(8,128)(2,1)S(1)}, u32[]{:S(2)}, u32[]{:S(2)}) collective-permute-start(bf16[128,768]{1,0:T(8,128)(2,1)S(1)} %get-tuple-element.139.refs_1_), channel_id=1, source_target_pairs={{0,2},{1,3},{2,0},{3,1},{4,6},{5,7},{6,4},{7,5},{8,10},{9,11},{10,... | collective-permute-start | bytes 589832 | tf_op jit(solution)/shard_map/ppermute | solution.py:176
  103.7 16.9 %all-to-all-start.3 = ((bf16[8,24,768]{2,1,0:T(8,128)(2,1)}), bf16[8,24,768]{2,1,0:T(8,128)(2,1)S(1)}, u32[]{:S(2)}, u32[]{:S(2)}) async-start(bf16[8,24,768]{2,1,0:T(8,128)(2,1)} %bitcast.14), calls=%async_computation.3 | async-start | bytes 589824 | tf_op jit(solution)/shard_map/all_to_all | solution.py:180
  124.2 17.8 %collective-permute-start.29 = (bf16[128,768]{1,0:T(8,128)(2,1)S(1)}, bf16[128,768]{1,0:T(8,128)(2,1)S(1)}, u32[]{:S(2)}, u32[]{:S(2)}) collective-permute-start(bf16[128,768]{1,0:T(8,128)(2,1)S(1)} %get-tuple-element.154.refs_3_), channel_id=1, source_target_pairs={{0,1},{1,0},{2,3},{3,2},{4,5},{5,4},{6,7},{7,6},{8,9},{9,8},{10,11... | collective-permute-start | bytes 589832 | tf_op jit(solution)/shard_map/ppermute | solution.py:176
  127.1 7.5 %collective-permute-start.39 = (f32[8,16,96]{2,1,0:T(8,128)S(1)}, f32[8,16,96]{2,1,0:T(8,128)S(1)}, u32[]{:S(2)}, u32[]{:S(2)}) collective-permute-start(f32[8,16,96]{2,1,0:T(8,128)S(1)} %add.14.refs_4_.refs_0_), channel_id=1, source_target_pairs={{0,2},{1,3},{2,0},{3,1},{4,6},{5,7},{6,4},{7,5},{8,10},{9,11},{10,... | collective-permute-start | bytes 147464 | tf_op jit(solution)/shard_map/ppermute | solution.py:176
  128.5 13.5 %collective-permute-start.33 = (bf16[128,768]{1,0:T(8,128)(2,1)S(1)}, bf16[128,768]{1,0:T(8,128)(2,1)S(1)}, u32[]{:S(2)}, u32[]{:S(2)}) collective-permute-start(bf16[128,768]{1,0:T(8,128)(2,1)S(1)} %far.7.refs_3_), channel_id=1, source_target_pairs={{0,2},{1,3},{2,0},{3,1},{4,6},{5,7},{6,4},{7,5},{8,10},{9,11},{10,... | collective-permute-start | bytes 589832 | tf_op jit(solution)/shard_map/ppermute | solution.py:176
  135.2 11.5 %all-to-all-start.4 = ((f32[8,16,96]{2,1,0:T(8,128)}), f32[8,16,96]{2,1,0:T(8,128)S(1)}, u32[]{:S(2)}, u32[]{:S(2)}) async-start(f32[8,16,96]{2,1,0:T(8,128)} %add.15.refs_3_), calls=%async_computation.4 | async-start | bytes 131072 | tf_op jit(solution)/shard_map/all_to_all | solution.py:180
  (29 other events, 150.0 us)

commit v6 on v5

--- a/solution.py
+++ b/solution.py
@@ -945,6 +945,7 @@
             + [((owners, small_rows, shard), FULL)],
             "grad_one",
             fetch=(1, 2, 3, 4),
+            first=1,
             store=(0,),
             time=0.2,
             wait=(mark,),

time: 149 us -> 150 us (level)
  transfers between devices with their start and end apart: 47 -> 47, of which waited for: 19 -> 18; matrix products, arithmetic and copies ran while one was open for 1% -> 1% of each run, Pallas kernels for 32% -> 32%
where the time goes in v6:
time: 150 us; the launch traced here: 149 us
  starting transfers between devices  62 us (41%)
  Pallas kernels  54.2 us (36%)
  waiting for transfers between devices  29.3 us (20%)
  local copies, waits for them, and re-layouts  2.16 us (1%)
    pallas_call x34, Pallas kernels, call(): pl.pallas_call(kernel, out_shape=[pltpu.HBM(*outs[i]) if i in store else...  45.6 us
    all_to_all x5, starting transfers between devices, exchange(): return lax.all_to_all(buffer, 'dp', split_axis=0, concat_axis=0, tiled=True)  27.1 us
    ppermute x26, starting transfers between devices, swap(): return lax.ppermute(values, axis, [(i, i ^ bit) for i in range(count)])  17.1 us
    ppermute x26, waiting for transfers between devices, swap(): return lax.ppermute(values, axis, [(i, i ^ bit) for i in range(count)])  17 us
    pallas_call x8, Pallas kernels, moved(): pl.pallas_call(functools.partial(move_kernel, len(kinds)), out_shape=[plt...  8.53 us
    ppermute x3, starting transfers between devices, ring_gather(): behind.append(lax.ppermute(behind[-1], 'dp', right))  6.57 us
    ppermute x3, starting transfers between devices, ring_reduce(): ahead = lax.ppermute(to_right, 'dp', right)  5.6 us
    ppermute x3, waiting for transfers between devices, ring_gather(): behind.append(lax.ppermute(behind[-1], 'dp', right))  5.35 us
  transfers between devices with their start and end apart: 47, of which 18 were waited for; matrix products, arithmetic and copies ran while one was open for 1% of the time, Pallas kernels for 32%

profile of v6, /device:TPU:0, one launch (start us, length us, event | category | flops | bytes accessed | tf_op | source)
XLA Modules:
  0.0 149.0 jit_solution(3185261676623090787)
XLA Ops:
  1.9 3.1 %collective-permute-start = (bf16[112,768]{1,0:T(8,128)(2,1)S(1)}, bf16[112,768]{1,0:T(8,128)(2,1)S(1)}, u32[]{:S(2)}, u32[]{:S(2)}) collective-permute-start(bf16[112,768]{1,0:T(8,128)(2,1)S(1)} %pack.1.refs_1_), channel_id=1, source_target_pairs={{0,8},{8,16},{16,24},{24,28},{28,20},{20,12},{12,4},{4,0},{1,9},{9... | collective-permute-start | bytes 516104 | tf_op jit(solution)/shard_map/ppermute | solution.py:207
  6.9 2.3 %collective-permute-done.refs_3_.refs_2_ = bf16[112,768]{1,0:T(8,128)(2,1)S(1)} collective-permute-done((bf16[112,768]{1,0:T(8,128)(2,1)S(1)}, bf16[112,768]{1,0:T(8,128)(2,1)S(1)}, u32[]{:S(2)}, u32[]{:S(2)}) %collective-permute-start) | collective-permute-done | bytes 172064 | tf_op jit(solution)/shard_map/ppermute | solution.py:207
  12.7 2.1 %collective-permute-done.4.refs_3_ = bf16[112,768]{1,0:T(8,128)(2,1)S(1)} collective-permute-done((bf16[112,768]{1,0:T(8,128)(2,1)S(1)}, bf16[112,768]{1,0:T(8,128)(2,1)S(1)}, u32[]{:S(2)}, u32[]{:S(2)}) %collective-permute-start.4) | collective-permute-done | bytes 172064 | tf_op jit(solution)/shard_map/ppermute | solution.py:207
  16.8 2.5 %spread.1 = (bf16[128,192]{1,0:T(8,128)(2,1)}, bf16[192,768]{1,0:T(8,128)(2,1)S(1)}) custom-call(s32[5]{0:T(128)S(1)} %pad_add_fusion.refs_0_, s32[512,1]{1,0:T(8,128)} %copy.24.refs_1_, bf16[128,768]{1,0:T(8,128)(2,1)} %refs_1_.6, bf16[112,768]{1,0:T(8,128)(2,1)S(1)} %collective-permute-done.refs_3_.refs_2_), custom_call_target="tpu_custom_call" | custom-call | flops 2200000000 | bytes 1048576 | tf_op jit(solution)/shard_map/spread/pallas_call | solution.py:106
  23.4 5.9 %all-to-all-start = ((bf16[8,24,768]{2,1,0:T(8,128)(2,1)}), bf16[8,24,768]{2,1,0:T(8,128)(2,1)S(1)}, u32[]{:S(2)}, u32[]{:S(2)}) async-start(bf16[8,24,768]{2,1,0:T(8,128)(2,1)} %bitcast.6), calls=%async_computation | async-start | bytes 589824 | tf_op jit(solution)/shard_map/all_to_all | solution.py:180
  29.9 5.6 %attend.1 = (f32[128,768]{1,0:T(8,128)S(1)}, f32[128,768]{1,0:T(8,128)S(1)}, bf16[128,768]{1,0:T(8,128)(2,1)S(1)}, bf16[128,768]{1,0:T(8,128)(2,1)S(1)}, bf16[51...) custom-call(s32[5]{0:T(128)S(1)} %pad_add_fusion.refs_0_, ...), custom_call_target="tpu_custom_call" | custom-call | flops 4400000000 | bytes 1048576 | tf_op jit(solution)/shard_map/attend/pallas_call | solution.py:106
  41.3 2.7 %collective-permute-done.13.refs_3_ = bf16[128,768]{1,0:T(8,128)(2,1)S(1)} collective-permute-done((bf16[128,768]{1,0:T(8,128)(2,1)S(1)}, bf16[128,768]{1,0:T(8,128)(2,1)S(1)}, u32[]{:S(2)}, u32[]{:S(2)}) %collective-permute-start.13) | collective-permute-done | bytes 196640 | tf_op jit(solution)/shard_map/ppermute | solution.py:176
  45.2 6.0 %all-to-all-start.1 = ((bf16[8,24,768]{2,1,0:T(8,128)(2,1)}), bf16[8,24,768]{2,1,0:T(8,128)(2,1)S(1)}, u32[]{:S(2)}, u32[]{:S(2)}) async-start(bf16[8,24,768]{2,1,0:T(8,128)(2,1)} %bitcast.8), calls=%async_computation.1 | async-start | bytes 589824 | tf_op jit(solution)/shard_map/all_to_all | solution.py:180
  54.3 4.8 %collective-permute-done.14.refs_2_.refs_3_ = bf16[192,768]{1,0:T(8,128)(2,1)S(1)} collective-permute-done((bf16[192,768]{1,0:T(8,128)(2,1)S(1)}, bf16[192,768]{1,0:T(8,128)(2,1)S(1)}, u32[]{:S(2)}, u32[]{:S(2)}) %collective-permute-start.14) | collective-permute-done | bytes 294944 | tf_op jit(solution)/shard_map/ppermute | solution.py:176
  63.7 4.6 %expert.2 = (f32[192,768]{1,0:T(8,128)}, bf16[192,768]{1,0:T(8,128)(2,1)S(1)}, bf16[384,768]{1,0:T(8,128)(2,1)S(1)}, bf16[384,768]{1,0:T(8,128)(2,1)}, bf16[384,...) custom-call(s32[5]{0:T(128)S(1)} %pad_add_fusion.refs_0_, ...), custom_call_target="tpu_custom_call" | custom-call | flops 4400000000 | bytes 1048576 | tf_op jit(solution)/shard_map/expert/pallas_call | solution.py:106
  71.5 3.6 %expert.3 = (f32[192,768]{1,0:T(8,128)S(1)}, bf16[192,768]{1,0:T(8,128)(2,1)S(1)}, bf16[384,768]{1,0:T(8,128)(2,1)S(1)}, bf16[384,768]{1,0:T(8,128)(2,1)S(1)}, b...) custom-call(s32[5]{0:T(128)S(1)} %pad_add_fusion.refs_0_, ...), custom_call_target="tpu_custom_call" | custom-call | flops 4400000000 | bytes 1048576 | tf_op jit(solution)/shard_map/expert/pallas_call | solution.py:106
  80.4 2.5 %grad_out.1.refs_4_ = f32[1,768,768]{2,1,0:T(8,128)} custom-call(bf16[384,768]{1,0:T(8,128)(2,1)S(1)} %get-tuple-element.114.refs_0_, bf16[384,768]{1,0:T(8,128)(2,1)S(1)} %get-tuple-element.117.refs_2_.refs_1_, bf16[384,768]{1,0:T(8,128)(2,1)S(1)} %get-tuple-element.126.refs_2_, bf16[384,768]{1,0:T(8,128)(2,1)S(1)} %get-tuple-element.127.refs_3_, ...), custom_call_target="tpu_custom_call" | custom-call | flops 3300000000 | bytes 1048576 | tf_op jit(solution)/shard_map/grad_out/pallas_call | solution.py:106
  86.8 4.6 %all-to-all-start.2 = ((bf16[8,24,768]{2,1,0:T(8,128)(2,1)}), bf16[8,24,768]{2,1,0:T(8,128)(2,1)S(1)}, u32[]{:S(2)}, u32[]{:S(2)}) async-start(bf16[8,24,768]{2,1,0:T(8,128)(2,1)} %bitcast.12), calls=%async_computation.2 | async-start | bytes 589824 | tf_op jit(solution)/shard_map/all_to_all | solution.py:180
  93.0 4.2 %grad_in.1.refs_6_ = f32[1,768,768]{2,1,0:T(8,128)} custom-call(bf16[384,768]{1,0:T(8,128)(2,1)} %get-tuple-element.136.refs_0_, bf16[384,768]{1,0:T(8,128)(2,1)} %get-tuple-element.137.refs_1_, bf16[384,768]{1,0:T(8,128)(2,1)} %get-tuple-element.138.refs_2_, bf16[384,768]{1,0:T(8,128)(2,1)} %get-tuple-element.131.refs_5_.refs_3_), custom_call_target="tpu_custom_call" | custom-call | flops 3300000000 | bytes 1048576 | tf_op jit(solution)/shard_map/grad_in/pallas_call | solution.py:106
  98.6 2.3 %collective-permute-done.24.refs_5_.refs_2_ = bf16[192,768]{1,0:T(8,128)(2,1)S(1)} collective-permute-done((bf16[192,768]{1,0:T(8,128)(2,1)S(1)}, bf16[192,768]{1,0:T(8,128)(2,1)S(1)}, u32[]{:S(2)}, u32[]{:S(2)}) %collective-permute-start.24) | collective-permute-done | bytes 294944 | tf_op jit(solution)/shard_map/ppermute | solution.py:176
  103.7 6.0 %all-to-all-start.3 = ((bf16[8,24,768]{2,1,0:T(8,128)(2,1)}), bf16[8,24,768]{2,1,0:T(8,128)(2,1)S(1)}, u32[]{:S(2)}, u32[]{:S(2)}) async-start(bf16[8,24,768]{2,1,0:T(8,128)(2,1)} %bitcast.14), calls=%async_computation.3 | async-start | bytes 589824 | tf_op jit(solution)/shard_map/all_to_all | solution.py:180
  111.4 7.0 %attend_back.1 = (bf16[512,576]{1,0:T(8,128)(2,1)S(1)}, bf16[48,768]{1,0:T(8,128)(2,1)S(1)}, bf16[48,768]{1,0:T(8,128)(2,1)S(1)}, bf16[672,768]{1,0:T(8,128)(2,1)S(1)}) custom-call(s32[5]{0:T(128)S(1)} %pad_add_fusion.refs_0_, bf16[128,768]{1,0:T(8,128)(2,1)S(1)} %get-tuple-element.139.refs_1_, bf16[128,768]{1,0:T(8,128)(2,1)S(1)} %add.13.refs_2_, ...), custom_call_target="tpu_custom_call" | custom-call | flops 2200000000 | bytes 1048576 | tf_op jit(solution)/shard_map/attend_back/pallas_call | solution.py:106
  118.4 2.1 %collective-permute-start.31 = (bf16[48,768]{1,0:T(8,128)(2,1)S(1)}, bf16[48,768]{1,0:T(8,128)(2,1)S(1)}, u32[]{:S(2)}, u32[]{:S(2)}) collective-permute-start(bf16[48,768]{1,0:T(8,128)(2,1)S(1)} %get-tuple-element.157), channel_id=1, source_target_pairs={{0,8},{8,16},{16,24},{24,28},{28,20},{20,12},{12,4},{4,0},{1,9},{9... | collective-permute-start | bytes 221192 | tf_op jit(solution)/shard_map/ppermute | solution.py:244
  120.6 3.7 %grad_one.1 = (f32[128,768]{1,0:T(8,128)}, f32[128,768]{1,0:T(8,128)S(1)}, bf16[128,768]{1,0:T(8,128)(2,1)S(1)}, bf16[128,768]{1,0:T(8,128)(2,1)S(1)}, f32[8,16,96]{2,1,0:T(8,128)S(1)}) custom-call(bf16[512,576]{1,0:T(8,128)(2,1)S(1)} %get-tuple-element.147.refs_0_, bf16[768,768]{1,0:T(8,128)(2,1)} %get-tuple-element.142.refs_6_.refs_1_, ...), custom_call_target="tpu_custom_call" | custom-call | flops 220000000 | bytes 1048576 | tf_op jit(solution)/shard_map/grad_one/pallas_call | solution.py:106
  125.1 2.0 %collective-permute-start.34 = (bf16[96,768]{1,0:T(8,128)(2,1)S(1)}, bf16[96,768]{1,0:T(8,128)(2,1)S(1)}, u32[]{:S(2)}, u32[]{:S(2)}) collective-permute-start(bf16[96,768]{1,0:T(8,128)(2,1)S(1)} %get-tuple-element.161), channel_id=1, source_target_pairs={{0,8},{8,16},{16,24},{24,28},{28,20},{20,12},{12,4},{4,0},{1,9},{9... | collective-permute-start | bytes 442376 | tf_op jit(solution)/shard_map/ppermute | solution.py:260
  135.8 4.5 %all-to-all-start.4 = ((f32[8,16,96]{2,1,0:T(8,128)}), f32[8,16,96]{2,1,0:T(8,128)S(1)}, u32[]{:S(2)}, u32[]{:S(2)}) async-start(f32[8,16,96]{2,1,0:T(8,128)} %add.15.refs_3_), calls=%async_computation.4 | async-start | bytes 131072 | tf_op jit(solution)/shard_map/all_to_all | solution.py:180
  140.5 2.1 %collective-permute-start.40 = (bf16[96,768]{1,0:T(8,128)(2,1)S(1)}, bf16[96,768]{1,0:T(8,128)(2,1)S(1)}, u32[]{:S(2)}, u32[]{:S(2)}) collective-permute-start(bf16[96,768]{1,0:T(8,128)(2,1)S(1)} %get-tuple-element.170), channel_id=1, source_target_pairs={{0,8},{8,16},{16,24},{24,28},{28,20},{20,12},{12,4},{4,0},{1,9},{9... | collective-permute-start | bytes 442376 | tf_op jit(solution)/shard_map/ppermute | solution.py:260
  142.6 2.3 %last.1 = (f32[128,768]{1,0:T(8,128)}, bf16[128,768]{1,0:T(8,128)(2,1)}) custom-call(bf16[128,768]{1,0:T(8,128)(2,1)} %refs_0_.5, f32[128,768]{1,0:T(8,128)} %get-tuple-element.153.refs_1_, bf16[128,768]{1,0:T(8,128)(2,1)S(1)} %collective-permute-done.29.refs_2_, bf16[128,768]{1,0:T(8,128)(2,1)S(1)} %collective-permute-done.33.refs_1_.refs_3_, ...), custom_call_target="tpu_custom_call" | custom-call | flops 330000000 | bytes 1048576 | tf_op jit(solution)/shard_map/last/pallas_call | solution.py:106
  145.0 2.3 %all-to-all-done.4.refs_3_ = f32[8,16,96]{2,1,0:T(8,128)S(1)} async-done(((f32[8,16,96]{2,1,0:T(8,128)}), f32[8,16,96]{2,1,0:T(8,128)S(1)}, u32[]{:S(2)}, u32[]{:S(2)}) %all-to-all-start.4) | async-done | bytes 49184 | tf_op jit(solution)/shard_map/all_to_all | solution.py:180
  (128 shorter events, 58.7 us)
Async XLA Ops:
  1.9 7.4 %collective-permute-start = (bf16[112,768]{1,0:T(8,128)(2,1)S(1)}, bf16[112,768]{1,0:T(8,128)(2,1)S(1)}, u32[]{:S(2)}, u32[]{:S(2)}) collective-permute-start(bf16[112,768]{1,0:T(8,128)(2,1)S(1)} %pack.1.refs_1_), channel_id=1, source_target_pairs={{0,8},{8,16},{16,24},{24,28},{28,20},{20,12},{12,4},{4,0},{1,9},{9... | collective-permute-start | bytes 516104 | tf_op jit(solution)/shard_map/ppermute | solution.py:207
  11.3 18.6 %collective-permute-start.2 = (bf16[128,768]{1,0:T(8,128)(2,1)S(1)}, bf16[128,768]{1,0:T(8,128)(2,1)S(1)}, u32[]{:S(2)}, u32[]{:S(2)}) collective-permute-start(bf16[128,768]{1,0:T(8,128)(2,1)S(1)} %copy-done.3), channel_id=1, source_target_pairs={{0,1},{1,0},{2,3},{3,2},{4,5},{5,4},{6,7},{7,6},{8,9},{9,8},{10,11... | collective-permute-start | bytes 589832 | tf_op jit(solution)/shard_map/ppermute | solution.py:176
  12.2 17.7 %collective-permute-start.3 = (bf16[128,768]{1,0:T(8,128)(2,1)S(1)}, bf16[128,768]{1,0:T(8,128)(2,1)S(1)}, u32[]{:S(2)}, u32[]{:S(2)}) collective-permute-start(bf16[128,768]{1,0:T(8,128)(2,1)S(1)} %collective-permute-done.1.refs_2_), channel_id=1, source_target_pairs={{0,1},{1,0},{2,3},{3,2},{4,5},{5,4},{6,7},{7,6},{8,9},{9,8},{10,11... | collective-permute-start | bytes 589832 | tf_op jit(solution)/shard_map/ppermute | solution.py:176
  20.3 9.6 %collective-permute-start.9 = (bf16[48,768]{1,0:T(8,128)(2,1)S(1)}, bf16[48,768]{1,0:T(8,128)(2,1)S(1)}, u32[]{:S(2)}, u32[]{:S(2)}) collective-permute-start(bf16[48,768]{1,0:T(8,128)(2,1)S(1)} %slice.8), channel_id=1, source_target_pairs={{0,8},{8,16},{16,24},{24,28},{28,20},{20,12},{12,4},{4,0},{1,9},{9... | collective-permute-start | bytes 221192 | tf_op jit(solution)/shard_map/ppermute | solution.py:210
  22.2 7.7 %collective-permute-start.10 = (bf16[64,768]{1,0:T(8,128)(2,1)S(1)}, bf16[64,768]{1,0:T(8,128)(2,1)S(1)}, u32[]{:S(2)}, u32[]{:S(2)}) collective-permute-start(bf16[64,768]{1,0:T(8,128)(2,1)S(1)} %slice.9), channel_id=1, source_target_pairs={{8,0},{16,8},{24,16},{28,24},{20,28},{12,20},{4,12},{0,4},{9,1},{1... | collective-permute-start | bytes 294920 | tf_op jit(solution)/shard_map/ppermute | solution.py:211
  23.4 17.0 %all-to-all-start = ((bf16[8,24,768]{2,1,0:T(8,128)(2,1)}), bf16[8,24,768]{2,1,0:T(8,128)(2,1)S(1)}, u32[]{:S(2)}, u32[]{:S(2)}) async-start(bf16[8,24,768]{2,1,0:T(8,128)(2,1)} %bitcast.6), calls=%async_computation | async-start | bytes 589824 | tf_op jit(solution)/shard_map/all_to_all | solution.py:180
  45.2 15.0 %all-to-all-start.1 = ((bf16[8,24,768]{2,1,0:T(8,128)(2,1)}), bf16[8,24,768]{2,1,0:T(8,128)(2,1)S(1)}, u32[]{:S(2)}, u32[]{:S(2)}) async-start(bf16[8,24,768]{2,1,0:T(8,128)(2,1)} %bitcast.8), calls=%async_computation.1 | async-start | bytes 589824 | tf_op jit(solution)/shard_map/all_to_all | solution.py:180
  51.2 7.9 %collective-permute-start.14 = (bf16[192,768]{1,0:T(8,128)(2,1)S(1)}, bf16[192,768]{1,0:T(8,128)(2,1)S(1)}, u32[]{:S(2)}, u32[]{:S(2)}) collective-permute-start(bf16[192,768]{1,0:T(8,128)(2,1)S(1)} %bitcast.23), channel_id=1, source_target_pairs={{0,2},{1,3},{2,0},{3,1},{4,6},{5,7},{6,4},{7,5},{8,10},{9,11},{10,... | collective-permute-start | bytes 884744 | tf_op jit(solution)/shard_map/ppermute | solution.py:176
  52.7 9.6 %collective-permute-start.16 = (bf16[192,768]{1,0:T(8,128)(2,1)S(1)}, bf16[192,768]{1,0:T(8,128)(2,1)S(1)}, u32[]{:S(2)}, u32[]{:S(2)}) collective-permute-start(bf16[192,768]{1,0:T(8,128)(2,1)S(1)} %bitcast.24), channel_id=1, source_target_pairs={{0,1},{1,0},{2,3},{3,2},{4,5},{5,4},{6,7},{7,6},{8,9},{9,8},{10,11... | collective-permute-start | bytes 884744 | tf_op jit(solution)/shard_map/ppermute | solution.py:176
  60.3 9.6 %collective-permute-start.19 = (bf16[192,768]{1,0:T(8,128)(2,1)S(1)}, bf16[192,768]{1,0:T(8,128)(2,1)S(1)}, u32[]{:S(2)}, u32[]{:S(2)}) collective-permute-start(bf16[192,768]{1,0:T(8,128)(2,1)S(1)} %collective-permute-done.14.refs_2_.refs_3_), channel_id=1, source_target_pairs={{0,1},{1,0},{2,3},{3,2},{4,5},{5,4},{6,7},{7,6},{8,9},{9,8},{10,11... | collective-permute-start | bytes 884744 | tf_op jit(solution)/shard_map/ppermute | solution.py:176
  60.8 9.0 %collective-permute-start.17 = (bf16[192,768]{1,0:T(8,128)(2,1)S(1)}, bf16[192,768]{1,0:T(8,128)(2,1)S(1)}, u32[]{:S(2)}, u32[]{:S(2)}) collective-permute-start(bf16[192,768]{1,0:T(8,128)(2,1)S(1)} %add.11.refs_1_), channel_id=1, source_target_pairs={{0,2},{1,3},{2,0},{3,1},{4,6},{5,7},{6,4},{7,5},{8,10},{9,11},{10,... | collective-permute-start | bytes 884744 | tf_op jit(solution)/shard_map/ppermute | solution.py:176
  75.3 9.8 %collective-permute-start.22 = (bf16[192,768]{1,0:T(8,128)(2,1)S(1)}, bf16[192,768]{1,0:T(8,128)(2,1)S(1)}, u32[]{:S(2)}, u32[]{:S(2)}) collective-permute-start(bf16[192,768]{1,0:T(8,128)(2,1)S(1)} %get-tuple-element.116.refs_1_), channel_id=1, source_target_pairs={{0,1},{1,0},{2,3},{3,2},{4,5},{5,4},{6,7},{7,6},{8,9},{9,8},{10,11... | collective-permute-start | bytes 884744 | tf_op jit(solution)/shard_map/ppermute | solution.py:176
  76.8 9.1 %collective-permute-start.23 = (bf16[192,768]{1,0:T(8,128)(2,1)S(1)}, bf16[192,768]{1,0:T(8,128)(2,1)S(1)}, u32[]{:S(2)}, u32[]{:S(2)}) collective-permute-start(bf16[192,768]{1,0:T(8,128)(2,1)S(1)} %far.5.refs_5_.refs_1_.refs_4_.refs_3_), channel_id=1, source_target_pairs={{0,2},{1,3},{2,0},{3,1},{4,6},{5,7},{6,4},{7,5},{8,10},{9,11},{10,... | collective-permute-start | bytes 884744 | tf_op jit(solution)/shard_map/ppermute | solution.py:176
  80.3 11.1 %collective-permute-start.21 = (bf16[192,768]{1,0:T(8,128)(2,1)S(1)}, bf16[192,768]{1,0:T(8,128)(2,1)S(1)}, u32[]{:S(2)}, u32[]{:S(2)}) collective-permute-start(bf16[192,768]{1,0:T(8,128)(2,1)S(1)} %get-tuple-element.123), channel_id=1, source_target_pairs={{0,1},{1,0},{2,3},{3,2},{4,5},{5,4},{6,7},{7,6},{8,9},{9,8},{10,11... | collective-permute-start | bytes 884744 | tf_op jit(solution)/shard_map/ppermute | solution.py:176
  86.8 14.2 %all-to-all-start.2 = ((bf16[8,24,768]{2,1,0:T(8,128)(2,1)}), bf16[8,24,768]{2,1,0:T(8,128)(2,1)S(1)}, u32[]{:S(2)}, u32[]{:S(2)}) async-start(bf16[8,24,768]{2,1,0:T(8,128)(2,1)} %bitcast.12), calls=%async_computation.2 | async-start | bytes 589824 | tf_op jit(solution)/shard_map/all_to_all | solution.py:180
  91.4 11.5 %collective-permute-start.26 = (bf16[192,768]{1,0:T(8,128)(2,1)S(1)}, bf16[192,768]{1,0:T(8,128)(2,1)S(1)}, u32[]{:S(2)}, u32[]{:S(2)}) collective-permute-start(bf16[192,768]{1,0:T(8,128)(2,1)S(1)} %get-tuple-element.125.refs_3_), channel_id=1, source_target_pairs={{0,1},{1,0},{2,3},{3,2},{4,5},{5,4},{6,7},{7,6},{8,9},{9,8},{10,11... | collective-permute-start | bytes 884744 | tf_op jit(solution)/shard_map/ppermute | solution.py:176
  91.5 9.5 %collective-permute-start.24 = (bf16[192,768]{1,0:T(8,128)(2,1)S(1)}, bf16[192,768]{1,0:T(8,128)(2,1)S(1)}, u32[]{:S(2)}, u32[]{:S(2)}) collective-permute-start(bf16[192,768]{1,0:T(8,128)(2,1)S(1)} %far.6.refs_5_), channel_id=1, source_target_pairs={{0,2},{1,3},{2,0},{3,1},{4,6},{5,7},{6,4},{7,5},{8,10},{9,11},{10,... | collective-permute-start | bytes 884744 | tf_op jit(solution)/shard_map/ppermute | solution.py:176
  101.3 8.4 %collective-permute-start.25 = (bf16[128,768]{1,0:T(8,128)(2,1)S(1)}, bf16[128,768]{1,0:T(8,128)(2,1)S(1)}, u32[]{:S(2)}, u32[]{:S(2)}) collective-permute-start(bf16[128,768]{1,0:T(8,128)(2,1)S(1)} %get-tuple-element.139.refs_1_), channel_id=1, source_target_pairs={{0,2},{1,3},{2,0},{3,1},{4,6},{5,7},{6,4},{7,5},{8,10},{9,11},{10,... | collective-permute-start | bytes 589832 | tf_op jit(solution)/shard_map/ppermute | solution.py:176
  103.7 16.9 %all-to-all-start.3 = ((bf16[8,24,768]{2,1,0:T(8,128)(2,1)}), bf16[8,24,768]{2,1,0:T(8,128)(2,1)S(1)}, u32[]{:S(2)}, u32[]{:S(2)}) async-start(bf16[8,24,768]{2,1,0:T(8,128)(2,1)} %bitcast.14), calls=%async_computation.3 | async-start | bytes 589824 | tf_op jit(solution)/shard_map/all_to_all | solution.py:180
  124.9 17.8 %collective-permute-start.29 = (bf16[128,768]{1,0:T(8,128)(2,1)S(1)}, bf16[128,768]{1,0:T(8,128)(2,1)S(1)}, u32[]{:S(2)}, u32[]{:S(2)}) collective-permute-start(bf16[128,768]{1,0:T(8,128)(2,1)S(1)} %get-tuple-element.154.refs_3_), channel_id=1, source_target_pairs={{0,1},{1,0},{2,3},{3,2},{4,5},{5,4},{6,7},{7,6},{8,9},{9,8},{10,11... | collective-permute-start | bytes 589832 | tf_op jit(solution)/shard_map/ppermute | solution.py:176
  127.2 8.0 %collective-permute-start.39 = (f32[8,16,96]{2,1,0:T(8,128)S(1)}, f32[8,16,96]{2,1,0:T(8,128)S(1)}, u32[]{:S(2)}, u32[]{:S(2)}) collective-permute-start(f32[8,16,96]{2,1,0:T(8,128)S(1)} %add.14.refs_4_.refs_0_), channel_id=1, source_target_pairs={{0,2},{1,3},{2,0},{3,1},{4,6},{5,7},{6,4},{7,5},{8,10},{9,11},{10,... | collective-permute-start | bytes 147464 | tf_op jit(solution)/shard_map/ppermute | solution.py:176
  128.6 14.0 %collective-permute-start.33 = (bf16[128,768]{1,0:T(8,128)(2,1)S(1)}, bf16[128,768]{1,0:T(8,128)(2,1)S(1)}, u32[]{:S(2)}, u32[]{:S(2)}) collective-permute-start(bf16[128,768]{1,0:T(8,128)(2,1)S(1)} %far.7.refs_3_), channel_id=1, source_target_pairs={{0,2},{1,3},{2,0},{3,1},{4,6},{5,7},{6,4},{7,5},{8,10},{9,11},{10,... | collective-permute-start | bytes 589832 | tf_op jit(solution)/shard_map/ppermute | solution.py:176
  133.1 7.3 %collective-permute-start.37 = (bf16[96,768]{1,0:T(8,128)(2,1)S(1)}, bf16[96,768]{1,0:T(8,128)(2,1)S(1)}, u32[]{:S(2)}, u32[]{:S(2)}) collective-permute-start(bf16[96,768]{1,0:T(8,128)(2,1)S(1)} %get-tuple-element.165), channel_id=1, source_target_pairs={{0,8},{8,16},{16,24},{24,28},{28,20},{20,12},{12,4},{4,0},{1,9},{9... | collective-permute-start | bytes 442376 | tf_op jit(solution)/shard_map/ppermute | solution.py:260
  135.8 11.5 %all-to-all-start.4 = ((f32[8,16,96]{2,1,0:T(8,128)}), f32[8,16,96]{2,1,0:T(8,128)S(1)}, u32[]{:S(2)}, u32[]{:S(2)}) async-start(f32[8,16,96]{2,1,0:T(8,128)} %add.15.refs_3_), calls=%async_computation.4 | async-start | bytes 131072 | tf_op jit(solution)/shard_map/all_to_all | solution.py:180
  (29 other events, 150.2 us)
